TPU v7x, 32 devices: a whole 2x2x4 slice. The times are simulated.
32 devices in a mesh: rows: 2 (over core), seq: 4 (over y, x), tensor: 4 (over z).
Axes of the slice: x: 2, y: 2, z: 4, core: 2. Of those that a mesh axis runs over, the one named last changes fastest.
Arguments:
- activations: bfloat16 [2, 1280, 2048], P('rows', 'seq'), may hold values from -6 to 6
- doc_lengths: int32 [2, 4], P('rows'), may hold values from 1 to 1276, as said below
- w_query: bfloat16 [2048, 2048], P(None, 'tensor'), may hold values from -0.125 to 0.125
- key_matrix: bfloat16 [2048, 512], P(None, 'tensor'), may hold values from -0.125 to 0.125
- value_matrix: bfloat16 [2048, 512], P(None, 'tensor'), may hold values from -0.125 to 0.125
- w_output: bfloat16 [2048, 2048], P('tensor'), may hold values from -0.75 to 0.75
- w_gate: bfloat16 [2048, 8192], P(None, 'tensor'), may hold values from -0.125 to 0.125
- w_up: bfloat16 [2048, 8192], P(None, 'tensor'), may hold values from -0.125 to 0.125
- w_down: bfloat16 [8192, 2048], P('tensor'), may hold values from -0.0625 to 0.0625
- gain_attn: float32 [2048], replicated, may hold values from 0.5 to 1.5
- gain_ffn: float32 [2048], replicated, may hold values from 0.5 to 1.5
- cotangent: bfloat16 [2, 1280, 2048], P('rows', 'seq'), may hold values from -6 to 6
Outputs:
- block_output: bfloat16 [2, 1280, 2048], P('rows', 'seq')
- grad_activations: bfloat16 [2, 1280, 2048], P('rows', 'seq')
- grad_w_query: float32 [2048, 2048], P(None, 'tensor')
- grad_w_key: float32 [2048, 512], P(None, 'tensor')
- grad_w_value: float32 [2048, 512], P(None, 'tensor')
- grad_w_output: float32 [2048, 2048], P('tensor')
- grad_w_gate: float32 [2048, 8192], P(None, 'tensor')
- grad_w_up: float32 [2048, 8192], P(None, 'tensor')
- grad_w_down: float32 [8192, 2048], P('tensor')
- grad_gain_attn: float32 [2048], replicated
- grad_gain_ffn: float32 [2048], replicated
Inputs may be any that keep to these rules, and one draw needn't show every extreme that they name: `doc_lengths`: each row's lengths sum to less than 1280; the rest of the row is padding. In every row one document starts within the first 320 places and ends within the last 320.
All inputs are finite; a program needn't handle non-finite values.
Results may differ from a plain program's by a relative error of at most 0.023.
Values may be sent and summed in bfloat16 or wider, within the bound.
No kernel may reach another device: no remote copies, remote signals or barrier semaphores. Data moves between devices by JAX's collectives and lax.ppermute only.
A program may use at most 256 MiB of HBM per device.

v0:
```python
import jax
import jax.numpy as jnp
from jax import lax
from jax.sharding import PartitionSpec as P

HEAD_SIZE = 64
DOCS = 4


EPSILON = 1e-05


def rope_tables(positions):
    half = HEAD_SIZE // 2
    expo = jnp.arange(half, dtype=jnp.float32) * 2.0 / HEAD_SIZE
    inverse = 1.0 / 500000.0**expo
    wavelength = 2.0 * jnp.pi / inverse
    smooth = (8192.0 / wavelength - 1.0) / 3.0
    middle = (1.0 - smooth) * inverse / 32.0 + smooth * inverse
    scaled = jnp.where(
        wavelength < 2048.0, inverse, jnp.where(wavelength > 8192.0, inverse / 32.0, middle)
    )
    angles = positions.astype(jnp.float32)[:, None] * scaled[None, :]
    return (jnp.cos(angles), jnp.sin(angles))


def apply_rotation(values, cosine_table, sine_table):
    half = values.shape[-1] // 2
    first = values[..., :half]
    second = values[..., half:]
    cosine_table = cosine_table[:, None, :]
    sine_table = sine_table[:, None, :]
    return jnp.concatenate(
        [first * cosine_table - second * sine_table, second * cosine_table + first * sine_table],
        axis=-1,
    )


def layout(row_lengths, places):
    ends = jnp.cumsum(row_lengths)
    starts = ends - row_lengths
    segment = jnp.sum((places[:, None] >= ends[None, :]).astype(jnp.int32), axis=1)
    labels = jnp.arange(row_lengths.shape[0], dtype=jnp.int32)
    begin = jnp.sum(jnp.where(segment[:, None] == labels[None, :], starts[None, :], 0), axis=1)
    begin = begin + jnp.where(segment == row_lengths.shape[0], ends[-1], 0)
    return (segment, places - begin)


def rms_back(grad_normed, gain, values, inverse):
    scaled = grad_normed * gain
    product = jnp.mean(scaled * values, axis=-1, keepdims=True)
    return inverse * scaled - values * inverse * inverse * inverse * product


def per_device(
    activations,
    doc_lengths,
    w_query,
    key_matrix,
    value_matrix,
    w_output,
    w_gate,
    w_up,
    w_down,
    gain_attn,
    gain_ffn,
    cotangent,
):
    span = activations.shape[1]
    whole = span * lax.axis_size("seq")
    heads_kv = key_matrix.shape[1] // HEAD_SIZE
    query_group = w_query.shape[1] // key_matrix.shape[1]
    width = heads_kv * HEAD_SIZE
    scale = HEAD_SIZE ** (-0.5)
    row_lengths = doc_lengths[0]
    places = lax.axis_index("seq") * span + jnp.arange(span, dtype=jnp.int32)
    segment, position = layout(row_lengths, places)
    key_places = jnp.arange(whole, dtype=jnp.int32)
    key_segment = layout(row_lengths, key_places)[0]
    allowed = (segment[:, None] == key_segment[None, :]) & (places[:, None] >= key_places[None, :])
    cosine_table, sine_table = rope_tables(position)
    stream = activations[0].astype(jnp.float32)
    inverse_one = lax.rsqrt(jnp.mean(stream * stream, axis=-1, keepdims=True) + EPSILON)
    first_normed = (stream * inverse_one * gain_attn).astype(jnp.bfloat16)
    query_lin = jnp.dot(first_normed, w_query, preferred_element_type=jnp.float32)
    key_lin = jnp.dot(first_normed, key_matrix, preferred_element_type=jnp.float32)
    value_lin = jnp.dot(first_normed, value_matrix, preferred_element_type=jnp.float32)
    queries = apply_rotation(
        query_lin.reshape(span, heads_kv * query_group, HEAD_SIZE), cosine_table, sine_table
    ).astype(jnp.bfloat16)
    query_four = queries.reshape(span, heads_kv, query_group, HEAD_SIZE)
    keys = apply_rotation(
        key_lin.reshape(span, heads_kv, HEAD_SIZE), cosine_table, sine_table
    ).astype(jnp.bfloat16)
    values = value_lin.astype(jnp.bfloat16)
    packed = jnp.concatenate([keys.reshape(span, width), values], axis=1)
    gathered = lax.all_gather(packed, "seq", axis=0, tiled=True)

    def score_block(key_full):
        raw = (
            jnp.einsum("chgd,whd->hgcw", query_four, key_full, preferred_element_type=jnp.float32)
            * scale
        )
        return jnp.where(allowed[None, None], raw, -1e30)

    key_full = gathered[:, :width].reshape(whole, heads_kv, HEAD_SIZE)
    value_full = gathered[:, width:].reshape(whole, heads_kv, HEAD_SIZE)
    masked = score_block(key_full)
    top = jnp.max(masked, axis=-1, keepdims=True)
    weights = jnp.exp(masked - top)
    total = jnp.sum(weights, axis=-1, keepdims=True)
    probs = (weights / total).astype(jnp.bfloat16)
    mixed = jnp.einsum("hgcw,whd->chgd", probs, value_full, preferred_element_type=jnp.float32)
    attended = mixed.reshape(span, width * query_group).astype(jnp.bfloat16)
    attn_part = jnp.dot(attended, w_output, preferred_element_type=jnp.float32)
    middle = stream + lax.psum(attn_part.astype(jnp.bfloat16), "tensor").astype(jnp.float32)
    inverse_two = lax.rsqrt(jnp.mean(middle * middle, axis=-1, keepdims=True) + EPSILON)
    normed_here = (middle * inverse_two * gain_ffn).astype(jnp.bfloat16)
    gate = jnp.dot(normed_here, w_gate, preferred_element_type=jnp.float32)
    up_proj = jnp.dot(normed_here, w_up, preferred_element_type=jnp.float32)
    sigmoid = jax.nn.sigmoid(gate)
    activated = gate * sigmoid
    hidden = (activated * up_proj).astype(jnp.bfloat16)
    down_part = jnp.dot(hidden, w_down, preferred_element_type=jnp.float32)
    block_output = (
        middle + lax.psum(down_part.astype(jnp.bfloat16), "tensor").astype(jnp.float32)
    ).astype(jnp.bfloat16)
    valid = (segment < DOCS).astype(jnp.float32)
    upstream = cotangent[0].astype(jnp.float32) * valid[:, None]
    upstream_low = upstream.astype(jnp.bfloat16)
    grad_down = jnp.einsum("cf,cd->fd", hidden, upstream_low, preferred_element_type=jnp.float32)
    grad_hidden = jnp.einsum("cd,fd->cf", upstream_low, w_down, preferred_element_type=jnp.float32)
    grad_gate = (grad_hidden * up_proj * sigmoid * (1.0 + gate * (1.0 - sigmoid))).astype(
        jnp.bfloat16
    )
    grad_up = (grad_hidden * activated).astype(jnp.bfloat16)
    grad_gate_w = jnp.einsum(
        "cd,cf->df", normed_here, grad_gate, preferred_element_type=jnp.float32
    )
    grad_up_w = jnp.einsum("cd,cf->df", normed_here, grad_up, preferred_element_type=jnp.float32)
    part_two = jnp.einsum("cf,df->cd", grad_gate, w_gate, preferred_element_type=jnp.float32)
    part_two = part_two + jnp.einsum("cf,df->cd", grad_up, w_up, preferred_element_type=jnp.float32)
    grad_normed_two = lax.psum(part_two.astype(jnp.bfloat16), "tensor").astype(jnp.float32)
    grad_gain_two = jnp.sum(grad_normed_two * middle * inverse_two, axis=0)
    grad_middle = upstream + rms_back(grad_normed_two, gain_ffn, middle, inverse_two)
    grad_middle_here = grad_middle.astype(jnp.bfloat16)
    grad_wo = jnp.einsum(
        "ce,cd->ed", attended, grad_middle_here, preferred_element_type=jnp.float32
    )
    grad_attended = jnp.einsum(
        "cd,ed->ce", grad_middle_here, w_output, preferred_element_type=jnp.float32
    )
    grad_attended = grad_attended.astype(jnp.bfloat16).reshape(
        span, heads_kv, query_group, HEAD_SIZE
    )
    renewed = jnp.exp(score_block(key_full) - top) / total
    renewed_low = renewed.astype(jnp.bfloat16)
    grad_probs = jnp.einsum(
        "chgd,whd->hgcw", grad_attended, value_full, preferred_element_type=jnp.float32
    )
    inner = jnp.sum(renewed * grad_probs, axis=-1, keepdims=True)
    grad_scores = (renewed * (grad_probs - inner)).astype(jnp.bfloat16)
    grad_query_rot = (
        jnp.einsum("hgcw,whd->chgd", grad_scores, key_full, preferred_element_type=jnp.float32)
        * scale
    )
    grad_key_term = (
        jnp.einsum("hgcw,chgd->whd", grad_scores, query_four, preferred_element_type=jnp.float32)
        * scale
    )
    grad_value_term = jnp.einsum(
        "hgcw,chgd->whd", renewed_low, grad_attended, preferred_element_type=jnp.float32
    )
    kv_term = jnp.concatenate(
        [grad_key_term.reshape(whole, width), grad_value_term.reshape(whole, width)], axis=1
    )
    kv_grad = lax.psum_scatter(
        kv_term.astype(jnp.bfloat16), "seq", scatter_dimension=0, tiled=True
    ).astype(jnp.float32)
    grad_query_lin = apply_rotation(
        grad_query_rot.reshape(span, heads_kv * query_group, HEAD_SIZE), cosine_table, -sine_table
    )
    grad_query_lin = grad_query_lin.reshape(span, width * query_group).astype(jnp.bfloat16)
    grad_key_lin = apply_rotation(
        kv_grad[:, :width].reshape(span, heads_kv, HEAD_SIZE), cosine_table, -sine_table
    )
    grad_key_lin = grad_key_lin.reshape(span, width).astype(jnp.bfloat16)
    grad_value_lin = kv_grad[:, width:].astype(jnp.bfloat16)
    grad_wq = jnp.einsum(
        "cd,ce->de", first_normed, grad_query_lin, preferred_element_type=jnp.float32
    )
    grad_wk = jnp.einsum(
        "cd,ce->de", first_normed, grad_key_lin, preferred_element_type=jnp.float32
    )
    grad_wv = jnp.einsum(
        "cd,ce->de", first_normed, grad_value_lin, preferred_element_type=jnp.float32
    )
    part_one = jnp.einsum("ce,de->cd", grad_query_lin, w_query, preferred_element_type=jnp.float32)
    part_one = part_one + jnp.einsum(
        "ce,de->cd", grad_key_lin, key_matrix, preferred_element_type=jnp.float32
    )
    part_one = part_one + jnp.einsum(
        "ce,de->cd", grad_value_lin, value_matrix, preferred_element_type=jnp.float32
    )
    grad_normed_one = lax.psum(part_one.astype(jnp.bfloat16), "tensor").astype(jnp.float32)
    grad_gain_one = jnp.sum(grad_normed_one * stream * inverse_one, axis=0)
    grad_input = (grad_middle + rms_back(grad_normed_one, gain_attn, stream, inverse_one)).astype(
        jnp.bfloat16
    )
    results = (
        lax.psum(grad_wq.astype(jnp.bfloat16), ("rows", "seq")).astype(jnp.float32),
        lax.psum(grad_wk.astype(jnp.bfloat16), ("rows", "seq")).astype(jnp.float32),
        lax.psum(grad_wv.astype(jnp.bfloat16), ("rows", "seq")).astype(jnp.float32),
        lax.psum(grad_wo.astype(jnp.bfloat16), ("rows", "seq")).astype(jnp.float32),
        lax.psum(grad_gate_w.astype(jnp.bfloat16), ("rows", "seq")).astype(jnp.float32),
        lax.psum(grad_up_w.astype(jnp.bfloat16), ("rows", "seq")).astype(jnp.float32),
        lax.psum(grad_down.astype(jnp.bfloat16), ("rows", "seq")).astype(jnp.float32),
        lax.psum(grad_gain_one.astype(jnp.bfloat16), ("rows", "seq")).astype(jnp.float32),
        lax.psum(grad_gain_two.astype(jnp.bfloat16), ("rows", "seq")).astype(jnp.float32),
    )
    gain_one_total = results[7]
    gain_two_total = results[8]
    return (
        block_output[None],
        grad_input[None],
        results[0],
        results[1],
        results[2],
        results[3],
        results[4],
        results[5],
        results[6],
        gain_one_total,
        gain_two_total,
    )


def solution(mesh):
    placed = (
        P("rows", "seq", None),
        P("rows", None),
        P(None, "tensor"),
        P(None, "tensor"),
        P(None, "tensor"),
        P("tensor", None),
        P(None, "tensor"),
        P(None, "tensor"),
        P("tensor", None),
        P(),
        P(),
        P("rows", "seq", None),
    )
    return jax.shard_map(
        per_device,
        mesh=mesh,
        in_specs=placed,
        out_specs=(
            P("rows", "seq", None),
            P("rows", "seq", None),
            P(None, "tensor"),
            P(None, "tensor"),
            P(None, "tensor"),
            P("tensor", None),
            P(None, "tensor"),
            P(None, "tensor"),
            P("tensor", None),
            P(),
            P(),
        ),
        check_vma=False,
    )
```

profile of v0, /device:TPU:0, one launch (start us, length us, event | category | flops | bytes accessed | tf_op | source)
XLA Modules:
  0.0 818.5 jit_solution(14472374198365326649)
XLA Ops:
  10.8 1.7 fusion.35
  13.0 2.0 copy.44
  16.8 2.2 fusion.58
  19.6 1.6 copy.45
  21.3 1.7 convolution_convert_fusion.10
  23.0 12.0 %all_gather.3 = bf16[1280,256]{1,0:T(8,128)(2,1)S(1)} all-gather(bf16[320,256]{1,0:T(8,128)(2,1)S(1)} %pad_maximum_fusion.2), channel_id=1, replica_groups=mesh['rows'=2,'seq'=4,'tensor'=4] {'seq'}, dimensions={0}, use_global_device_ids=true | all-gather | bytes 819200 | tf_op jit(solution)/shard_map/all_gather | solution.py:97
  35.9 1.9 copy.47
  37.8 4.1 copy.48
  41.9 3.0 fusion.56
  47.0 1.9 copy.46
  48.9 10.6 %fusion.88 = (f32[2,4,320]{2,1,0:T(4,128)S(1)}, f32[2,4,320,1280]{3,2,1,0:T(8,128)}) fusion(pred[320,1280]{1,0:T(8,128)(4,1)} %fusion.53, bf16[1280,2,64,1]{0,2,3,1:T(8,128)(2,1)} %bitcast.209, bf16[320,2,4,32]{0,3,2,1:T(8,128)(2,1)} %bitcast.217, bf16[320,2,4,32]{0,3,2,1:T(8,128)(2,1)} %bitcast.213), kind=kOutput, calls=%fused_computation.138 | convolution fusion | flops 433194240 | bytes 14182400 | tf_op jit(solution)/shard_map/sub | solution.py:110
  59.5 7.2 fusion.62
  66.7 2.9 convolution_convert_fusion.6
  70.2 59.9 %all-reduce.8.cloned.1.call-done = bf16[320,2048]{1,0:T(8,128)(2,1)} async-done(((bf16[320,2048]{1,0:T(8,128)(2,1)}), bf16[320,2048]{1,0:T(8,128)(2,1)}) %all-reduce.8.cloned.1.call-update) | async-done | bytes 1310736 | tf_op jit(solution)/shard_map/psum | solution.py:116
  130.1 1.9 multiply_reduce_fusion
  132.7 6.1 fusion.89
  138.9 4.5 fusion.90
  143.3 11.7 %multiply_convert_fusion = (bf16[320,2048]{1,0:T(8,128)(2,1)}, bf16[320,2048]{1,0:T(8,128)(2,1)}, bf16[320,2048]{1,0:T(8,128)(2,1)}) fusion(f32[320,2048]{1,0:T(8,128)S(1)} %fusion.89, f32[320,2048]{1,0:T(8,128)} %fusion.90, bf16[2048,2048]{1,0:T(8,128)(2,1)} %param.20, bf16[1,320,2048]{2,1,0:T(8,128)(2,1)S(1)} %copy-done.14, f32[320]{0:T(512)S(1)} %compare_convert_fusion), kind=kOutput, calls=%fused_computation.63 | convolution fusion | flops 2696151040 | bytes 18875648 | tf_op jit(solution)/shard_map/cd,fd->cf/dot_general | solution.py:132
  155.1 4.3 fusion.91
  159.5 7.4 fusion.22
  167.1 59.6 %all-reduce.10.cloned.1.call-done = bf16[320,2048]{1,0:T(8,128)(2,1)} async-done(((bf16[320,2048]{1,0:T(8,128)(2,1)}), bf16[320,2048]{1,0:T(8,128)(2,1)}) %all-reduce.10.cloned.1.call-update) | async-done | bytes 1310736 | tf_op jit(solution)/shard_map/psum | solution.py:143
  226.7 2.8 fusion.34
  229.6 2.7 fusion.31
  232.4 2.7 convolution_convert_fusion.9
  235.3 6.8 fusion.48
  242.1 6.4 fusion.1
  250.8 2.0 fusion.3
  256.8 7.9 convolution_convert_fusion.5
  264.7 2.2 convolution_multiply_fusion
  268.3 13.7 %reduce-scatter.4.cloned.1.call-done = bf16[320,256]{1,0:T(8,128)(2,1)} async-done(((bf16[1280,256]{1,0:T(8,128)(2,1)}), bf16[320,256]{1,0:T(8,128)(2,1)}) %reduce-scatter.4.cloned.1.call-update) | async-done | bytes 163856
  283.6 1.6 copy.56
  288.7 1.6 fusion.23
  290.9 6.8 convolution_convert_fusion.1
  297.7 6.8 convolution_convert_fusion.2
  304.5 6.9 convolution_convert_fusion
  311.5 2.8 convolution_convert_fusion.4
  314.3 4.4 convolution_convert_fusion.3
  320.3 1.6 convolution_convert_fusion.8
  321.8 73.1 %all-reduce.14.cloned.1.call-done = (bf16[320,2048]{1,0:T(8,128)(2,1)}, bf16[320,2048]{1,0:T(8,128)(2,1)}) async-done(((bf16[320,2048]{1,0:T(8,128)(2,1)}, bf16[320,2048]{1,0:T(8,128)(2,1)}), (bf16[320,2048]{1,0:T(8,128)(2,1)}, bf16[320,2048]{1,0:T(8,128)(2,1)})) %all-reduce.14.cloned.1.call-update) | async-done | bytes 2621456 | tf_op jit(solution)/shard_map/psum | solution.py:126
  395.0 2.1 fusion.38
  397.1 15.2 %all-reduce = (bf16[2048]{0:T(1024)(128)(2,1)S(1)}, bf16[2048]{0:T(1024)(128)(2,1)S(1)}) all-reduce(bf16[2048]{0:T(1024)(128)(2,1)S(1)} %get-tuple-element.13, bf16[2048]{0:T(1024)(128)(2,1)S(1)} %get-tuple-element.11), channel_id=1, replica_groups=mesh['rows'=2,'seq'=4,'tensor'=4] {'rows','seq'}, use_global_device_ids=true, to_apply=%region_24.25 | all-reduce | flops 4096 | bytes 16384 | tf_op jit(solution)/shard_map/psum | solution.py:218
  413.5 5.6 fusion.55
  419.1 350.0 %all-reduce.12.cloned.1.call-done = (bf16[2048,512]{1,0:T(8,128)(2,1)}, bf16[2048,128]{1,0:T(8,128)(2,1)}, bf16[2048,128]{1,0:T(8,128)(2,1)}, bf16[512,2048]{1,0...) async-done(((bf16[2048,512]{1,0:T(8,128)(2,1)}, bf16[2048,128]{1,0:T(8,128)(2,1)}, bf16[2048,128]{1,0:T(8,128)(2,1)}, ...) | async-done | bytes 30408720 | tf_op jit(solution)/shard_map/psum | solution.py:211
  769.2 11.7 %convert_element_type.258 = f32[2048,2048]{1,0:T(8,128)} convert(bf16[2048,2048]{1,0:T(8,128)(2,1)} %get-tuple-element.21) | non-fusion elementwise | flops 4194304 | bytes 25165824 | tf_op jit(solution)/shard_map/convert_element_type | solution.py:215
  780.8 11.7 %convert_element_type.260 = f32[2048,2048]{1,0:T(8,128)} convert(bf16[2048,2048]{1,0:T(8,128)(2,1)} %get-tuple-element.22) | non-fusion elementwise | flops 4194304 | bytes 25165824 | tf_op jit(solution)/shard_map/convert_element_type | solution.py:216
  792.5 11.8 %convert_element_type.262 = f32[2048,2048]{1,0:T(8,128)} convert(bf16[2048,2048]{1,0:T(8,128)(2,1)} %get-tuple-element.23) | non-fusion elementwise | flops 4194304 | bytes 25165824 | tf_op jit(solution)/shard_map/convert_element_type | solution.py:217
  804.3 2.6 convert_element_type.250
  807.0 2.5 convert_element_type.256
  (167 shorter events, 29.3 us)
Async XLA Ops:
  7.2 59.5 %copy-start = (bf16[512,2048]{1,0:T(8,128)(2,1)S(1)}, bf16[512,2048]{1,0:T(8,128)(2,1)}, u32[]{:S(2)}) copy-start(bf16[512,2048]{1,0:T(8,128)(2,1)} %param.17) | copy-start | bytes 6291460
  7.2 122.9 %all-reduce.8.cloned.1.call-start = ((), (), s32[]{:S(2)}) async-start(), calls=%async_computation.1 | async-start | bytes 2621440 | tf_op jit(solution)/shard_map/psum | solution.py:116
  10.8 4.4 copy-start.35
  12.4 8.8 %copy-start.3 = (bf16[1,320,2048]{2,1,0:T(8,128)(2,1)S(1)}, bf16[1,320,2048]{2,1,0:T(8,128)(2,1)}, u32[]{:S(2)}) copy-start(bf16[1,320,2048]{2,1,0:T(8,128)(2,1)} %param.12) | copy-start | bytes 3932164
  16.7 250.2 %copy-start.20 = (f32[320,32]{0,1:T(8,128)}, f32[320,32]{0,1:T(8,128)S(1)}, u32[]{:S(2)}) copy-start(f32[320,32]{0,1:T(8,128)S(1)} %get-tuple-element.43) | copy-start | bytes 122884
  16.8 250.2 %copy-start.26 = (f32[320,32]{0,1:T(8,128)}, f32[320,32]{0,1:T(8,128)S(1)}, u32[]{:S(2)}) copy-start(f32[320,32]{0,1:T(8,128)S(1)} %get-tuple-element.41) | copy-start | bytes 122884
  41.9 3.9 copy-start.36
  41.9 3.9 copy-start.38
  41.9 3.9 copy-start.41
  66.7 3.5 copy-start.37
  69.6 62.5 %copy-start.34 = (f32[2048]{0:T(1024)S(1)}, f32[2048]{0:T(1024)}, u32[]{:S(2)}) copy-start(f32[2048]{0:T(1024)} %param.22) | copy-start | bytes 24580
  69.6 157.1 %all-reduce.10.cloned.1.call-start = ((), (), s32[]{:S(2)}) async-start(), calls=%async_computation.2 | async-start | bytes 2621440 | tf_op jit(solution)/shard_map/psum | solution.py:143
  132.1 6.8 slice-start.8
  132.7 6.1 copy-start.17
  132.7 6.2 slice-start.9
  138.9 4.5 copy-start.14
  138.9 16.2 %slice-start.6 = ((s8[8388608]{0:T(1024)(128)(4,1)}), s8[4194304]{0:T(1024)(128)(4,1)S(1)}, s32[]{:S(2)}) async-start(s8[8388608]{0:T(1024)(128)(4,1)} %bitcast.233), calls=%async_computation.12 | async-start | bytes 8388608
  143.3 11.7 %slice-start.7 = ((s8[8388608]{0:T(1024)(128)(4,1)}), s8[4194304]{0:T(1024)(128)(4,1)S(1)}, s32[]{:S(2)}) async-start(s8[8388608]{0:T(1024)(128)(4,1)} %bitcast.233), calls=%async_computation.13 | async-start | bytes 8388608
  155.1 4.4 copy-start.43
  166.9 115.2 %reduce-scatter.4.cloned.1.call-start = ((), (), s32[]{:S(2)}) async-start(), calls=%async_computation.3 | async-start | bytes 819200
  226.7 2.8 copy-start.6
  226.7 2.8 copy-start.9
  226.7 2.9 copy-start.15
  232.3 2.9 copy-start.19
  232.3 2.9 copy-start.21
  232.3 2.9 copy-start.22
  235.3 6.9 copy-start.27
  242.1 6.5 slice-start.2
  242.1 7.4 slice-start.3
  242.1 8.6 %slice-start.4 = ((s8[13107200]{0:T(1024)(128)(4,1)}), s8[4194304]{0:T(1024)(128)(4,1)S(1)}, s32[]{:S(2)}) async-start(s8[13107200]{0:T(1024)(128)(4,1)} %bitcast.200), calls=%async_computation.10 | async-start | bytes 8388608
  242.1 8.7 %slice-start.5 = ((s8[13107200]{0:T(1024)(128)(4,1)}), s8[524288]{0:T(1024)(128)(4,1)S(1)}, s32[]{:S(2)}) async-start(s8[13107200]{0:T(1024)(128)(4,1)} %bitcast.200), calls=%async_computation.11 | async-start | bytes 1048576
  256.8 8.0 slice-start
  256.8 138.2 %all-reduce.14.cloned.1.call-start = ((), (), s32[]{:S(2)}) async-start(), calls=%async_computation.5 | async-start | bytes 5242880 | tf_op jit(solution)/shard_map/psum | solution.py:126
  256.8 7.9 slice-start.1
  267.1 20.5 %copy-start.12 = (bf16[2048,128]{1,0:T(8,128)(2,1)S(1)}, bf16[2048,128]{1,0:T(8,128)(2,1)}, u32[]{:S(2)}) copy-start(bf16[2048,128]{1,0:T(8,128)(2,1)} %param.15) | copy-start | bytes 1572868
  290.3 478.8 %all-reduce.12.cloned.1.call-start = ((), (), s32[]{:S(2)}) async-start(), calls=%async_computation.4 | async-start | bytes 60817408 | tf_op jit(solution)/shard_map/psum | solution.py:211
  290.9 6.8 copy-start.45
  297.7 6.8 copy-start.16
  297.7 6.8 copy-start.46
  304.5 7.0 copy-start.4
  304.5 7.0 copy-start.39
  304.5 7.0 copy-start.42
  311.5 2.8 copy-start.13
  314.3 4.4 copy-start.33
  321.8 91.7 %copy-start.7 = (bf16[320,2048]{1,0:T(8,128)(2,1)S(1)}, bf16[320,2048]{1,0:T(8,128)(2,1)}, u32[]{:S(2)}) copy-start(bf16[320,2048]{1,0:T(8,128)(2,1)} %all-reduce.8.cloned.1.call-done) | copy-start | bytes 3932164
  792.5 11.8 %copy-start.11 = (bf16[2048,512]{1,0:T(8,128)(2,1)S(1)}, bf16[2048,512]{1,0:T(8,128)(2,1)}, u32[]{:S(2)}) copy-start(bf16[2048,512]{1,0:T(8,128)(2,1)} %get-tuple-element.17) | copy-start | bytes 6291460
  806.9 3.6 copy-start.24
  806.9 4.6 copy-start.1
  (14 other events, 25.9 us)
Sparse Core Ops, SparseCore 0:
  69.7 60.3 all-reduce.7
  167.0 59.6 all-reduce.9
  256.9 25.0 reduce-scatter.3
  290.4 104.4 all-reduce.13
  401.8 367.2 all-reduce.11
where the time goes:
time: 822 us; the launch traced here: 819 us
  waiting for transfers between devices  557 us (68%)
  matrix products  123 us (15%)
  other arithmetic  73.1 us (9%)
  blocking collectives  27.2 us (3%)
  local copies, waits for them, and re-layouts  22.9 us (3%)
  between operations  14.8 us (2%)
    psum x1, waiting for transfers between devices, per_device(): lax.psum(grad_wq.astype(jnp.bfloat16), ('rows', 'seq')).astype(jnp.float32)  350 us
    psum x1, waiting for transfers between devices, per_device(): lax.psum(down_part.astype(jnp.bfloat16), 'tensor').astype(jnp.float32)  73.1 us
    psum x1, waiting for transfers between devices, per_device(): lax.psum(attn_part.astype(jnp.bfloat16), 'tensor').astype(jnp.float32)  59.9 us
    psum x1, waiting for transfers between devices, per_device(): lax.psum(part_two.astype(jnp.bfloat16), 'tensor').astype(jnp.float32)  59.6 us
  transfers between devices with their start and end apart: 5, of which 5 were waited for; matrix products, arithmetic and copies ran while one was open for 6% of the time, Pallas kernels for 0%

commit v1 on v0

v1 whole, which is shorter than its diff:
```python
import functools

import jax
import jax.numpy as jnp
from jax import lax
from jax.experimental import pallas as pl
from jax.experimental.pallas import tpu as pltpu
from jax.sharding import PartitionSpec as P

HEAD_SIZE = 64
DOCS = 4
EPSILON = 1e-05
BF = jnp.bfloat16
F32 = jnp.float32


MIB = 1 << 20


def kernel_params(dims):
    return pltpu.CompilerParams(
        vmem_limit_bytes=56 * MIB, dimension_semantics=("arbitrary",) * dims
    )


def contract(a, b, dim_a, dim_b):
    return lax.dot_general(
        a, b, (((dim_a,), (dim_b,)), ((), ())), preferred_element_type=F32
    )


def tile(limit, size):
    while size > limit and size % 2 == 0:
        size //= 2
    return size


def cost(flops, moved, exps=0):
    return pl.CostEstimate(
        flops=flops // 64, bytes_accessed=moved // 64, transcendentals=exps // 64
    )


def hidden_half_kernel(core, upstream, weight, out):
    out[...] = contract(upstream[...], weight[...], 1, 1).astype(BF)


def grad_hidden_half(core, upstream, w_down):
    tokens, depth = upstream.shape
    half = w_down.shape[0] // 2
    rows, cols = tile(640, tokens), tile(1024, half)
    steps = half // cols
    return pl.pallas_call(
        hidden_half_kernel,
        out_shape=jax.ShapeDtypeStruct((tokens, half), BF),
        grid_spec=pltpu.PrefetchScalarGridSpec(
            num_scalar_prefetch=1,
            grid=(steps, tokens // rows),
            in_specs=[
                pl.BlockSpec((rows, depth), lambda j, i, c: (i, 0)),
                pl.BlockSpec((cols, depth), lambda j, i, c: (c[0] * steps + j, 0)),
            ],
            out_specs=pl.BlockSpec((rows, cols), lambda j, i, c: (i, j)),
        ),
        compiler_params=kernel_params(2),
        cost_estimate=cost(
            2 * tokens * depth * half, 2 * (tokens * depth + half * depth + tokens * half)
        ),
        name="grad_hidden_half",
    )(core, upstream, w_down)


def swish_grads(gate, up_proj, grad_hidden):
    sigmoid = 1.0 / (1.0 + jnp.exp(-gate))
    activated = gate * sigmoid
    hidden = (activated * up_proj).astype(BF)
    grad_gate = (grad_hidden * up_proj * (sigmoid * (1.0 + gate * (1.0 - sigmoid)))).astype(BF)
    grad_up = (grad_hidden * activated).astype(BF)
    return hidden, grad_gate, grad_up


def feed_half_kernel(core, normed, gate_w, up_w, grad_hidden, hidden, grad_gate, grad_up):
    rows = normed[...]
    hidden[...], grad_gate[...], grad_up[...] = swish_grads(
        contract(rows, gate_w[...], 1, 0),
        contract(rows, up_w[...], 1, 0),
        grad_hidden[...].astype(F32),
    )


def feed_half(core, normed, w_gate, w_up, grad_hidden):
    tokens, depth = normed.shape
    half = w_gate.shape[1] // 2
    rows, cols = tile(640, tokens), tile(512, half)
    steps = half // cols
    out = jax.ShapeDtypeStruct((tokens, half), BF)
    weight = pl.BlockSpec((depth, cols), lambda j, i, c: (0, c[0] * steps + j))
    block = pl.BlockSpec((rows, cols), lambda j, i, c: (i, j))
    return pl.pallas_call(
        feed_half_kernel,
        out_shape=(out, out, out),
        grid_spec=pltpu.PrefetchScalarGridSpec(
            num_scalar_prefetch=1,
            grid=(steps, tokens // rows),
            in_specs=[
                pl.BlockSpec((rows, depth), lambda j, i, c: (i, 0)),
                weight,
                weight,
                block,
            ],
            out_specs=(block, block, block),
        ),
        compiler_params=kernel_params(2),
        cost_estimate=cost(
            4 * tokens * depth * half,
            2 * (tokens * depth + 2 * half * depth + 4 * tokens * half),
            tokens * half,
        ),
        name="feed_half",
    )(core, normed, w_gate, w_up, grad_hidden)


def feed_own_kernel(normed, gate_w, up_w, grad_hidden, hidden, part, total):
    step = pl.program_id(0)
    rows = normed[...]
    gate_now = gate_w[...]
    up_now = up_w[...]
    hidden[...], grad_gate, grad_up = swish_grads(
        contract(rows, gate_now, 1, 0),
        contract(rows, up_now, 1, 0),
        grad_hidden[...].astype(F32),
    )
    term = contract(grad_gate, gate_now, 1, 1) + contract(grad_up, up_now, 1, 1)

    @pl.when(step == 0)
    def _():
        total[...] = term

    @pl.when(step > 0)
    def _():
        total[...] += term

    @pl.when(step == pl.num_programs(0) - 1)
    def _():
        part[...] = total[...]


def feed_own(normed, w_gate, w_up, grad_hidden):
    tokens, depth = normed.shape
    units = w_gate.shape[1]
    cols = tile(512, units)
    weight = pl.BlockSpec((depth, cols), lambda j: (0, j))
    block = pl.BlockSpec((tokens, cols), lambda j: (0, j))
    rows = pl.BlockSpec((tokens, depth), lambda j: (0, 0))
    return pl.pallas_call(
        feed_own_kernel,
        out_shape=(
            jax.ShapeDtypeStruct((tokens, units), BF),
            jax.ShapeDtypeStruct((tokens, depth), F32),
        ),
        grid=(units // cols,),
        in_specs=[rows, weight, weight, block],
        out_specs=(block, rows),
        scratch_shapes=[pltpu.VMEM((tokens, depth), F32)],
        compiler_params=kernel_params(1),
        cost_estimate=cost(8 * tokens * depth * units, 4 * depth * units, tokens * units),
        name="feed_own",
    )(normed, w_gate, w_up, grad_hidden)


def weight_grad_kernel(count, core, *refs):
    lefts, rights = refs[:count], refs[count : 2 * count]
    wide, low = refs[2 * count :]
    total = contract(lefts[0][...], rights[0][...], 0, 0)
    for left, right in zip(lefts[1:], rights[1:]):
        total = total + contract(left[...], right[...], 0, 0)
    wide[...] = total
    low[...] = total.astype(BF)


def weight_grad(core, lefts, rights, dim):
    tokens, m = lefts[0].shape
    n = rights[0].shape[1]
    count = len(lefts)
    rows, cols = tile(512, m), tile(1024, n)
    down, across = m // rows, n // cols
    if dim == 0:
        full = (2 * m, n)
        place = lambda j, i, c: (c[0] * down + i, j)
    else:
        full = (m, 2 * n)
        place = lambda j, i, c: (i, c[0] * across + j)
    return pl.pallas_call(
        functools.partial(weight_grad_kernel, count),
        out_shape=(jax.ShapeDtypeStruct(full, F32), jax.ShapeDtypeStruct((m, n), BF)),
        grid_spec=pltpu.PrefetchScalarGridSpec(
            num_scalar_prefetch=1,
            grid=(across, down),
            in_specs=[pl.BlockSpec((tokens, rows), lambda j, i, c: (0, i))] * count
            + [pl.BlockSpec((tokens, cols), lambda j, i, c: (0, j))] * count,
            out_specs=(
                pl.BlockSpec((rows, cols), place),
                pl.BlockSpec((rows, cols), lambda j, i, c: (i, j)),
            ),
        ),
        compiler_params=kernel_params(2),
        cost_estimate=cost(
            2 * tokens * count * m * n, 2 * tokens * count * (m + n) + 6 * m * n
        ),
        name="weight_grad",
    )(core, *lefts, *rights)


def fill_other_kernel(core, other, held, out):
    out[...] = other[...].astype(F32)


def fill_other(core, other, held, dim):
    m, n = other.shape
    rows = tile(256, m)
    down = m // rows
    if dim == 0:
        place = lambda i, c: ((1 - c[0]) * down + i, 0)
    else:
        place = lambda i, c: (i, 1 - c[0])
    return pl.pallas_call(
        fill_other_kernel,
        out_shape=jax.ShapeDtypeStruct(held.shape, F32),
        grid_spec=pltpu.PrefetchScalarGridSpec(
            num_scalar_prefetch=1,
            grid=(down,),
            in_specs=[
                pl.BlockSpec((rows, n), lambda i, c: (i, 0)),
                pl.BlockSpec(memory_space=pl.ANY),
            ],
            out_specs=pl.BlockSpec((rows, n), place),
        ),
        input_output_aliases={2: 0},
        compiler_params=kernel_params(1),
        cost_estimate=cost(m * n, 6 * m * n),
        name="fill_other",
    )(core, other, held)


def rope_tables(positions):
    half = HEAD_SIZE // 2
    expo = jnp.arange(half, dtype=F32) * 2.0 / HEAD_SIZE
    inverse = 1.0 / 500000.0**expo
    wavelength = 2.0 * jnp.pi / inverse
    smooth = (8192.0 / wavelength - 1.0) / 3.0
    middle = (1.0 - smooth) * inverse / 32.0 + smooth * inverse
    scaled = jnp.where(
        wavelength < 2048.0, inverse, jnp.where(wavelength > 8192.0, inverse / 32.0, middle)
    )
    angles = positions.astype(F32)[:, None] * scaled[None, :]
    return (jnp.cos(angles), jnp.sin(angles))


def apply_rotation(values, cosine_table, sine_table):
    half = values.shape[-1] // 2
    first = values[..., :half]
    second = values[..., half:]
    cosine_table = cosine_table[:, None, :]
    sine_table = sine_table[:, None, :]
    return jnp.concatenate(
        [first * cosine_table - second * sine_table, second * cosine_table + first * sine_table],
        axis=-1,
    )


def layout(row_lengths, places):
    ends = jnp.cumsum(row_lengths)
    starts = ends - row_lengths
    segment = jnp.sum((places[:, None] >= ends[None, :]).astype(jnp.int32), axis=1)
    labels = jnp.arange(row_lengths.shape[0], dtype=jnp.int32)
    begin = jnp.sum(jnp.where(segment[:, None] == labels[None, :], starts[None, :], 0), axis=1)
    begin = begin + jnp.where(segment == row_lengths.shape[0], ends[-1], 0)
    return (segment, places - begin)


def rms_back(grad_normed, gain, values, inverse):
    scaled = grad_normed * gain
    product = jnp.mean(scaled * values, axis=-1, keepdims=True)
    return inverse * scaled - values * inverse * inverse * inverse * product


def dot(a, b):
    return jnp.dot(a, b, preferred_element_type=F32)


def dot_right(a, b):
    return jnp.einsum("cf,df->cd", a, b, preferred_element_type=F32)


def dot_left(a, b):
    return jnp.einsum("cd,cf->df", a, b, preferred_element_type=F32)


def flip(value, axis, mask):
    return lax.ppermute(value, axis, [(i, i ^ mask) for i in range(lax.axis_size(axis))])


def reorder(value, axis):
    n = lax.axis_size(axis)
    me = lax.axis_index(axis)
    chunk = value.shape[0] // n
    return jnp.concatenate(
        [lax.dynamic_slice_in_dim(value, (me ^ k) * chunk, chunk, 0) for k in range(n)], axis=0
    )


def scatter_sum(part, axis):
    n = lax.axis_size(axis)
    chunk = part.shape[0] // n
    total = part[:chunk]
    low = part.astype(BF)
    for k in reversed(range(1, n)):
        total = total + flip(low[k * chunk : (k + 1) * chunk], axis, k).astype(F32)
    return total


def spread(chunk, axis):
    return jnp.concatenate(
        [chunk] + [flip(chunk, axis, k) for k in range(1, lax.axis_size(axis))], axis=0
    )


def after(value, *others):
    return lax.optimization_barrier((value,) + others)[0]


def gather_halves(value):
    half = value.shape[0] // 2
    return [
        lax.all_gather(value[:half], ("rows", "seq"), axis=0, tiled=True),
        lax.all_gather(value[half:], ("seq", "rows"), axis=0, tiled=True),
    ]


def total_over(value, axes):
    for axis in axes:
        n = lax.axis_size(axis)
        for b in range(n.bit_length() - 1):
            value = value + flip(value, axis, 1 << b)
    return value


def per_device(
    activations,
    doc_lengths,
    w_query,
    key_matrix,
    value_matrix,
    w_output,
    w_gate,
    w_up,
    w_down,
    gain_attn,
    gain_ffn,
    cotangent,
):
    span = activations.shape[1]
    blocks = lax.axis_size("seq")
    whole = span * blocks
    chunk = span // lax.axis_size("tensor")
    heads_kv = key_matrix.shape[1] // HEAD_SIZE
    query_group = w_query.shape[1] // key_matrix.shape[1]
    width = heads_kv * HEAD_SIZE
    scale = HEAD_SIZE ** (-0.5)
    row_lengths = doc_lengths[0]
    block_here = lax.axis_index("seq")
    order = reorder(jnp.arange(span, dtype=jnp.int32), "tensor")
    places = block_here * span + order
    segment, position = layout(row_lengths, places)
    key_places = jnp.concatenate([(block_here ^ j) * span + order for j in range(blocks)])
    key_segment = layout(row_lengths, key_places)[0]
    allowed = (segment[:, None] == key_segment[None, :]) & (places[:, None] >= key_places[None, :])
    cosine_table, sine_table = rope_tables(position)

    stream = reorder(activations[0], "tensor").astype(F32)
    valid = (segment < DOCS).astype(F32)
    upstream_low = (reorder(cotangent[0], "tensor").astype(F32) * valid[:, None]).astype(BF)
    stream_chunk = stream[:chunk]
    upstream_chunk = upstream_low[:chunk].astype(F32)

    inverse_one = lax.rsqrt(jnp.mean(stream * stream, axis=-1, keepdims=True) + EPSILON)
    first_normed = (stream * inverse_one * gain_attn).astype(BF)
    key_lin = dot(first_normed, key_matrix)
    value_lin = dot(first_normed, value_matrix)
    keys = apply_rotation(
        key_lin.reshape(span, heads_kv, HEAD_SIZE), cosine_table, sine_table
    ).astype(BF)
    packed = jnp.concatenate([keys.reshape(span, width), value_lin.astype(BF)], axis=1)
    gathered = spread(packed, "seq")
    upstream_all = gather_halves(upstream_low)

    query_lin = dot(first_normed, w_query)
    queries = apply_rotation(
        query_lin.reshape(span, heads_kv * query_group, HEAD_SIZE), cosine_table, sine_table
    ).astype(BF)
    query_four = queries.reshape(span, heads_kv, query_group, HEAD_SIZE)

    def score_block(key_full):
        raw = (
            jnp.einsum("chgd,whd->hgcw", query_four, key_full, preferred_element_type=F32) * scale
        )
        return jnp.where(allowed[None, None], raw, -1e30)

    key_full = gathered[:, :width].reshape(whole, heads_kv, HEAD_SIZE)
    value_full = gathered[:, width:].reshape(whole, heads_kv, HEAD_SIZE)
    masked = score_block(key_full)
    top = jnp.max(masked, axis=-1, keepdims=True)
    weights = jnp.exp(masked - top)
    total = jnp.sum(weights, axis=-1, keepdims=True)
    probs = (weights / total).astype(BF)
    mixed = jnp.einsum("hgcw,whd->chgd", probs, value_full, preferred_element_type=F32)
    attended = mixed.reshape(span, width * query_group).astype(BF)

    core = lax.axis_index("rows").astype(jnp.int32).reshape(1)
    attn_part = dot(attended, w_output)
    attn_sum = scatter_sum(attn_part, "tensor")
    grad_hidden = dot_right(after(upstream_low, attn_part), w_down).astype(BF)
    attn_sum, grad_hidden = lax.optimization_barrier((attn_sum, grad_hidden))
    middle = stream_chunk + attn_sum
    inverse_two = lax.rsqrt(jnp.mean(middle * middle, axis=-1, keepdims=True) + EPSILON)
    normed_chunk = (middle * inverse_two * gain_ffn).astype(BF)
    normed_here = spread(normed_chunk, "tensor")
    grad_hidden_all = [grad_hidden_half(core, after(u, attn_sum), w_down) for u in upstream_all]
    normed_here, *grad_hidden_all = lax.optimization_barrier((normed_here, *grad_hidden_all))
    normed_all = gather_halves(normed_here)

    hidden, part_two = feed_own(normed_here, w_gate, w_up, grad_hidden)
    grad_normed_two = scatter_sum(part_two, "tensor")
    down_part = dot(after(hidden, part_two), w_down)
    grad_normed_two, down_part = lax.optimization_barrier((grad_normed_two, down_part))
    gain_two = jnp.sum(grad_normed_two * middle * inverse_two, axis=0)
    grad_middle = upstream_chunk + rms_back(grad_normed_two, gain_ffn, middle, inverse_two)
    grad_middle_here = spread(grad_middle.astype(BF), "tensor")
    first_feed = feed_half(
        core, after(normed_all[0], grad_normed_two), w_gate, w_up, grad_hidden_all[0]
    )
    grad_middle_here, *first_feed = lax.optimization_barrier((grad_middle_here, *first_feed))
    grad_wo = lax.psum(dot_left(attended, grad_middle_here).astype(BF), ("rows", "seq"))
    block_sum = scatter_sum(after(down_part, grad_middle_here), "tensor")

    grad_attended = (
        dot_right(grad_middle_here, w_output)
        .astype(BF)
        .reshape(span, heads_kv, query_group, HEAD_SIZE)
    )
    renewed = jnp.exp(score_block(key_full) - top) / total
    renewed_low = renewed.astype(BF)
    grad_probs = jnp.einsum(
        "chgd,whd->hgcw", grad_attended, value_full, preferred_element_type=F32
    )
    inner = jnp.sum(renewed * grad_probs, axis=-1, keepdims=True)
    grad_scores = (renewed * (grad_probs - inner)).astype(BF)
    grad_query_rot = (
        jnp.einsum("hgcw,whd->chgd", grad_scores, key_full, preferred_element_type=F32) * scale
    )
    grad_key_term = (
        jnp.einsum("hgcw,chgd->whd", grad_scores, query_four, preferred_element_type=F32) * scale
    )
    grad_value_term = jnp.einsum(
        "hgcw,chgd->whd", renewed_low, grad_attended, preferred_element_type=F32
    )
    kv_term = jnp.concatenate(
        [grad_key_term.reshape(whole, width), grad_value_term.reshape(whole, width)], axis=1
    )
    kv_term, block_sum = lax.optimization_barrier((kv_term, block_sum))
    kv_grad = scatter_sum(kv_term, "seq")
    second_feed = feed_half(
        core, after(normed_all[1], kv_term), w_gate, w_up, grad_hidden_all[1]
    )
    kv_grad, *second_feed = lax.optimization_barrier((kv_grad, *second_feed))
    block_chunk = middle + block_sum
    block_output = reorder(spread(block_chunk.astype(BF), "tensor"), "tensor")
    grad_query_lin = apply_rotation(
        grad_query_rot.reshape(span, heads_kv * query_group, HEAD_SIZE), cosine_table, -sine_table
    )
    grad_query_lin = grad_query_lin.reshape(span, width * query_group).astype(BF)
    grad_key_lin = apply_rotation(
        kv_grad[:, :width].reshape(span, heads_kv, HEAD_SIZE), cosine_table, -sine_table
    )
    grad_key_lin = grad_key_lin.reshape(span, width).astype(BF)
    grad_value_lin = kv_grad[:, width:].astype(BF)

    lin = jnp.concatenate([grad_query_lin, grad_key_lin, grad_value_lin], axis=1)
    lin_part = dot_left(after(first_normed, grad_wo), lin).astype(BF)
    grad_query_lin, lin_part = lax.optimization_barrier((grad_query_lin, lin_part))
    grad_lin = lax.psum(lin_part, ("rows", "seq"))
    part_one = (
        dot_right(grad_query_lin, w_query)
        + dot_right(grad_key_lin, key_matrix)
        + dot_right(grad_value_lin, value_matrix)
    )
    grad_normed_one = scatter_sum(part_one, "tensor")
    hidden_all, grad_gate_all, grad_up_all = zip(first_feed, second_feed)
    grad_down = weight_grad(
        core, [after(h, part_one) for h in hidden_all], upstream_all, 0
    )
    down_other = flip(grad_down[1], "rows", 1)
    grad_gate_w = weight_grad(
        core, [after(n, grad_down[1]) for n in normed_all], grad_gate_all, 1
    )
    gate_other = flip(grad_gate_w[1], "rows", 1)
    grad_normed_one, wide, down_other = lax.optimization_barrier(
        (grad_normed_one, grad_gate_w[0], down_other)
    )
    grad_gate_w = (wide, grad_gate_w[1])
    inverse_chunk = inverse_one[:chunk]
    gain_one = jnp.sum(grad_normed_one * stream_chunk * inverse_chunk, axis=0)
    grad_input = grad_middle + rms_back(grad_normed_one, gain_attn, stream_chunk, inverse_chunk)
    grad_input = spread(grad_input.astype(BF), "tensor")
    grad_up_w = weight_grad(
        core, [after(n, grad_normed_one) for n in normed_all], grad_up_all, 1
    )
    up_other = flip(grad_up_w[1], "rows", 1)
    grad_down = fill_other(core, after(down_other, grad_up_w[1]), grad_down[0], 0)
    grad_gate_w = fill_other(core, after(gate_other, grad_down), grad_gate_w[0], 1)
    grad_up_w = fill_other(core, up_other, grad_up_w[0], 1)
    grad_input = reorder(grad_input, "tensor")
    grad_wq = grad_lin[:, : width * query_group].astype(F32)
    grad_wkv = grad_lin[:, width * query_group :].astype(F32)
    gains = total_over(jnp.stack([gain_one, gain_two]), ("rows", "seq", "tensor"))
    return (
        block_output[None],
        grad_input[None],
        grad_wq,
        grad_wkv[:, :width],
        grad_wkv[:, width:],
        grad_wo.astype(F32),
        grad_gate_w,
        grad_up_w,
        grad_down,
        gains[0],
        gains[1],
    )


def solution(mesh):
    placed = (
        P("rows", "seq", None),
        P("rows", None),
        P(None, "tensor"),
        P(None, "tensor"),
        P(None, "tensor"),
        P("tensor", None),
        P(None, "tensor"),
        P(None, "tensor"),
        P("tensor", None),
        P(),
        P(),
        P("rows", "seq", None),
    )
    return jax.shard_map(
        per_device,
        mesh=mesh,
        in_specs=placed,
        out_specs=(
            P("rows", "seq", None),
            P("rows", "seq", None),
            P(None, "tensor"),
            P(None, "tensor"),
            P(None, "tensor"),
            P("tensor", None),
            P(None, "tensor"),
            P(None, "tensor"),
            P("tensor", None),
            P(),
            P(),
        ),
        check_vma=False,
    )
```

time: 822 us -> 549 us (0.67)
  waiting for transfers between devices: 557 us -> 185 us
  Pallas kernels: 0 us -> 148 us
  matrix products: 123 us -> 69.9 us
  starting transfers between devices: 1.05 us -> 51.2 us
  blocking collectives: 27.2 us -> 0 us
  other arithmetic: 73.1 us -> 54.6 us
    psum x4 -> x2, waiting for transfers between devices: 543 us -> 56.5 us  [the longest x1 38.3 us: per_device(): lax.psum(dot_left(attended, grad_middle_here).astype(BF), ('rows', 'seq'))]
    pallas_call x0 -> x11, Pallas kernels: none -> 148 us  [the longest x3 53.3 us: weight_grad(): pl.pallas_call(functools.partial(weight_grad_kernel, count), out_shape=(j...]
    ppermute x0 -> x38, waiting for transfers between devices: none -> 128 us  [flip(): lax.ppermute(value, axis, [(i, i ^ mask) for i in range(lax.axis_size(axi...]
    dot_general x22 -> x13, matrix products: 95.6 us -> 38.9 us  [the longest x5 14 us: dot_right(): return jnp.einsum('cf,df->cd', a, b, preferred_element_type=F32)]
    ppermute x0 -> x38, starting transfers between devices: none -> 51 us  [flip(): lax.ppermute(value, axis, [(i, i ^ mask) for i in range(lax.axis_size(axi...]
    convert_element_type x15 -> x16, other arithmetic: 46.9 us -> 27.6 us  [the longest x1 6.14 us: per_device(): grad_scores = (renewed * (grad_probs - inner)).astype(BF)]
    psum x1 -> x0, blocking collectives: 15.2 us -> none  [per_device(): lax.psum(grad_gain_one.astype(jnp.bfloat16), ('rows', 'seq'))]
    unnamed x6, waiting for transfers between devices: 13.8 us -> 0.78 us
  transfers between devices with their start and end apart: 5 -> 44, of which waited for: 5 -> 20; matrix products, arithmetic and copies ran while one was open for 6% -> 23% of each run, Pallas kernels for 0% -> 19%
where the time goes in v1:
time: 549 us; the launch traced here: 542 us
  waiting for transfers between devices  185 us (34%)
  Pallas kernels  148 us (27%)
  matrix products  69.9 us (13%)
  other arithmetic  54.6 us (10%)
  starting transfers between devices  51.2 us (9%)
  local copies, waits for them, and re-layouts  17.8 us (3%)
  between operations  15.5 us (3%)
    ppermute x38, waiting for transfers between devices, flip(): lax.ppermute(value, axis, [(i, i ^ mask) for i in range(lax.axis_size(axi...  128 us
    pallas_call x3, Pallas kernels, weight_grad(): pl.pallas_call(functools.partial(weight_grad_kernel, count), out_shape=(j...  53.3 us
    ppermute x38, starting transfers between devices, flip(): lax.ppermute(value, axis, [(i, i ^ mask) for i in range(lax.axis_size(axi...  51 us
    psum x1, waiting for transfers between devices, per_device(): lax.psum(dot_left(attended, grad_middle_here).astype(BF), ('rows', 'seq'))  38.3 us
    pallas_call x2, Pallas kernels, feed_half(): pl.pallas_call(feed_half_kernel, out_shape=(out, out, out), grid_spec=plt...  36 us
    pallas_call x3, Pallas kernels, fill_other(): pl.pallas_call(fill_other_kernel, out_shape=jax.ShapeDtypeStruct(held.sha...  20.6 us
    pallas_call x2, Pallas kernels, grad_hidden_half(): pl.pallas_call(hidden_half_kernel, out_shape=jax.ShapeDtypeStruct((tokens...  20.3 us
    pallas_call x1, Pallas kernels, feed_own(): pl.pallas_call(feed_own_kernel, out_shape=(jax.ShapeDtypeStruct((tokens,...  18.2 us
  transfers between devices with their start and end apart: 44, of which 20 were waited for; matrix products, arithmetic and copies ran while one was open for 23% of the time, Pallas kernels for 19%

profile of v1, /device:TPU:0, one launch (start us, length us, event | category | flops | bytes accessed | tf_op | source)
XLA Modules:
  0.0 542.5 jit_solution(14103774685568367534)
XLA Ops:
  24.3 3.9 collective-permute-start.2
  31.8 3.0 maximum_convert_fusion
  38.1 2.8 collective-permute-done.1
  43.4 8.9 %fusion.49 = (f32[2,4,320]{2,1,0:T(4,128)S(1)}, f32[2,4,320,1280]{3,2,1,0:T(8,128)}) fusion(pred[320,1280]{1,0:T(8,128)(4,1)} %compare_and_fusion, bf16[1280,2,64,1]{0,2,3,1:T(8,128)(2,1)S(1)} %bitcast.135, bf16[320,2,4,32]{0,3,2,1:T(8,128)(2,1)S(1)} %bitcast.145, bf16[320,2,4,32]{0,3,2,1:T(8,128)(2,1)S(1)} %bitcast.141), kind=kOutput, calls=%fused_computation.140 | convolution fusion | flops 433194240 | bytes 14182400 | tf_op jit(solution)/shard_map/sub | solution.py:413
  52.3 6.2 %fusion.15 = bf16[2,64,4,320]{3,1,2,0:T(8,128)(2,1)S(1)} fusion(bf16[1280,2,64,1]{0,2,3,1:T(8,128)(2,1)} %bitcast.158, f32[2,4,320]{2,1,0:T(4,128)S(1)} %get-tuple-element.178, pred[320,1280]{1,0:T(8,128)(4,1)} %compare_and_fusion, bf16[1280,2,64,1]{0,2,3,1:T(8,128)(2,1)S(1)} %bitcast.136, bf16[320,2,4,32]{0,3,2,1:T(8,128)(2,1)S(1)} %bitcast.146, ...), kind=kOutput, calls=%fused_computation.39 | convolution fusion | flops 856067840 | bytes 1730560 | tf_op jit(solution)/shard_map/hgcw,whd->chgd/dot_general | solution.py:416
  59.5 3.6 collective-permute-start.3
  63.9 7.3 %convolution_convert_fusion.2.grad_hidden = bf16[320,2048]{1,0:T(8,128)(2,1)} fusion(bf16[320,2048]{1,0:T(8,128)(2,1)S(1)} %copy-done.7, bf16[2048,2048]{1,0:T(8,128)(2,1)} %weight.3), kind=kOutput, calls=%fused_computation.21 | convolution fusion | flops 2685009920 | bytes 11010048 | tf_op jit(solution)/shard_map/cf,df->cd/dot_general | solution.py:292
  72.0 6.7 %collective-permute-done.5 = bf16[80,2048]{1,0:T(8,128)(2,1)S(1)} collective-permute-done((bf16[80,2048]{1,0:T(8,128)(2,1)S(1)}, bf16[80,2048]{1,0:T(8,128)(2,1)S(1)}, u32[]{:S(2)}, u32[]{:S(2)}) %collective-permute-start.5) | collective-permute-done | bytes 327712 | tf_op jit(solution)/shard_map/ppermute | solution.py:300
  78.7 12.1 %collective-permute-done.4 = bf16[80,2048]{1,0:T(8,128)(2,1)S(1)} collective-permute-done((bf16[80,2048]{1,0:T(8,128)(2,1)S(1)}, bf16[80,2048]{1,0:T(8,128)(2,1)S(1)}, u32[]{:S(2)}, u32[]{:S(2)}) %collective-permute-start.4) | collective-permute-done | bytes 327712 | tf_op jit(solution)/shard_map/ppermute | solution.py:300
  92.4 2.6 collective-permute-start.8
  96.9 8.2 %collective-permute-done.8 = bf16[80,2048]{1,0:T(8,128)(2,1)S(1)} collective-permute-done((bf16[80,2048]{1,0:T(8,128)(2,1)S(1)}, bf16[80,2048]{1,0:T(8,128)(2,1)S(1)}, u32[]{:S(2)}, u32[]{:S(2)}) %collective-permute-start.8) | collective-permute-done | bytes 327712 | tf_op jit(solution)/shard_map/ppermute | solution.py:300
  105.1 15.9 %collective-permute-done.7 = bf16[80,2048]{1,0:T(8,128)(2,1)} collective-permute-done((bf16[80,2048]{1,0:T(8,128)(2,1)S(1)}, bf16[80,2048]{1,0:T(8,128)(2,1)}, u32[]{:S(2)}, u32[]{:S(2)}) %collective-permute-start.7) | collective-permute-done | bytes 327712 | tf_op jit(solution)/shard_map/ppermute | solution.py:300
  123.2 10.3 %grad_hidden_half.2.grad_hidden = bf16[1280,1024]{1,0:T(8,128)(2,1)} custom-call(s32[1]{0:T(128)} %bitcast.29.core, bf16[1280,2048]{1,0:T(8,128)(2,1)} %all-gather.5.cloned.1.call-done.upstream.refs_2_, bf16[2048,2048]{1,0:T(8,128)(2,1)} %weight.3), custom_call_target="tpu_custom_call" | custom-call | flops 83886080 | bytes 188416 | tf_op jit(solution)/shard_map/grad_hidden_half/pallas_call | solution.py:53
  133.6 10.0 %grad_hidden_half.3.grad_hidden = bf16[1280,1024]{1,0:T(8,128)(2,1)} custom-call(s32[1]{0:T(128)} %bitcast.29.core, bf16[1280,2048]{1,0:T(8,128)(2,1)} %all-gather.7.cloned.1.call-done.upstream.refs_3_, bf16[2048,2048]{1,0:T(8,128)(2,1)} %weight.3), custom_call_target="tpu_custom_call" | custom-call | flops 83886080 | bytes 188416 | tf_op jit(solution)/shard_map/grad_hidden_half/pallas_call | solution.py:53
  144.8 18.2 %feed_own.1 = (bf16[320,2048]{1,0:T(8,128)(2,1)}, f32[320,2048]{1,0:T(8,128)}) custom-call(bf16[320,2048]{1,0:T(8,128)(2,1)} %pad_maximum_fusion.normed, bf16[2048,2048]{1,0:T(8,128)(2,1)} %gate_w.5, bf16[2048,2048]{1,0:T(8,128)(2,1)} %up_w.5, bf16[320,2048]{1,0:T(8,128)(2,1)} %convolution_convert_fusion.2.grad_hidden), custom_call_target="tpu_custom_call" | custom-call | flops 167772160 | bytes 262144 | tf_op jit(solution)/shard_map/feed_own/pallas_call | solution.py:155
  167.8 2.5 collective-permute-start.10
  170.4 8.3 %fusion.55 = f32[320,2048]{1,0:T(8,128)} fusion(bf16[320,2048]{1,0:T(8,128)(2,1)} %get-tuple-element.70, bf16[2048,2048]{1,0:T(8,128)(2,1)} %weight.3), kind=kOutput, calls=%fused_computation.146 | convolution fusion | flops 2684354560 | bytes 12320768 | tf_op jit(solution)/shard_map/dot_general | solution.py:288
  178.7 6.8 %collective-permute-done.11 = bf16[80,2048]{1,0:T(8,128)(2,1)S(1)} collective-permute-done((bf16[80,2048]{1,0:T(8,128)(2,1)}, bf16[80,2048]{1,0:T(8,128)(2,1)S(1)}, u32[]{:S(2)}, u32[]{:S(2)}) %collective-permute-start.11) | collective-permute-done | bytes 327712 | tf_op jit(solution)/shard_map/ppermute | solution.py:300
  185.4 8.0 %collective-permute-done.10 = bf16[80,2048]{1,0:T(8,128)(2,1)} collective-permute-done((bf16[80,2048]{1,0:T(8,128)(2,1)}, bf16[80,2048]{1,0:T(8,128)(2,1)}, u32[]{:S(2)}, u32[]{:S(2)}) %collective-permute-start.10) | collective-permute-done | bytes 327712 | tf_op jit(solution)/shard_map/ppermute | solution.py:300
  198.7 3.0 collective-permute-start.12
  201.7 8.1 %collective-permute-done.14 = bf16[80,2048]{1,0:T(8,128)(2,1)S(1)} collective-permute-done((bf16[80,2048]{1,0:T(8,128)(2,1)S(1)}, bf16[80,2048]{1,0:T(8,128)(2,1)S(1)}, u32[]{:S(2)}, u32[]{:S(2)}) %collective-permute-start.14) | collective-permute-done | bytes 327712 | tf_op jit(solution)/shard_map/ppermute | solution.py:300
  209.7 13.2 %collective-permute-done.13 = bf16[80,2048]{1,0:T(8,128)(2,1)S(1)} collective-permute-done((bf16[80,2048]{1,0:T(8,128)(2,1)S(1)}, bf16[80,2048]{1,0:T(8,128)(2,1)S(1)}, u32[]{:S(2)}, u32[]{:S(2)}) %collective-permute-start.13) | collective-permute-done | bytes 327712 | tf_op jit(solution)/shard_map/ppermute | solution.py:300
  224.0 17.8 %feed_half.2 = (bf16[1280,1024]{1,0:T(8,128)(2,1)}, bf16[1280,1024]{1,0:T(8,128)(2,1)}, bf16[1280,1024]{1,0:T(8,128)(2,1)}) custom-call(s32[1]{0:T(128)} %bitcast.29.core, bf16[1280,2048]{1,0:T(8,128)(2,1)} %all-gather.9.cloned.1.call-done.normed.refs_0_, bf16[2048,2048]{1,0:T(8,128)(2,1)} %gate_w.5, bf16[2048,2048]{1,0:T(8,128)(2,1)} %up_w.5, ...), custom_call_target="tpu_custom_call" | custom-call | flops 167772160 | bytes 376832 | tf_op jit(solution)/shard_map/feed_half/pallas_call | solution.py:99
  246.0 2.7 collective-permute-start.15
  250.4 2.6 convolution_convert_fusion.1
  253.0 12.0 %fusion.1 = (f32[2,4,320]{2,1,0:T(4,128)S(1)}, f32[2,1280,320,4]{1,2,3,0:T(8,128)}) fusion(f32[2,4,320,1280]{3,2,1,0:T(8,128)} %get-tuple-element.179, f32[2,4,320]{2,1,0:T(4,128)S(1)} %get-tuple-element.178, bf16[1280,2,64,1]{0,2,3,1:T(8,128)(2,1)S(1)} %bitcast.159, bf16[320,2,4,64]{0,3,2,1:T(8,128)(2,1)S(1)} %bitcast.154), kind=kOutput, calls=%fused_computation.3 | convolution fusion | flops 429258240 | bytes 26890240 | tf_op jit(solution)/shard_map/chgd,whd->hgcw/dot_general | solution.py:453
  265.9 6.1 %fusion.3 = bf16[2,4,320,1280]{3,2,1,0:T(8,128)(2,1)S(1)} fusion(f32[2,1280,320,4]{1,2,3,0:T(8,128)} %get-tuple-element.183, f32[2,4,320]{2,1,0:T(4,128)S(1)} %get-tuple-element.182, f32[2,4,320,1280]{3,2,1,0:T(8,128)S(1)} %bitcast.130, f32[2,4,320]{2,1,0:T(4,128)S(1)} %get-tuple-element.178), kind=kLoop, calls=%fused_computation.5 | loop fusion | flops 13107200 | bytes 32788480 | tf_op jit(solution)/shard_map/convert_element_type | solution.py:457
  275.6 6.8 %fusion.8 = f32[2,64,1280,1]{2,1,3,0:T(8,128)} fusion(bf16[320,2,4,64]{0,3,2,1:T(8,128)(2,1)S(1)} %bitcast.155, f32[2,4,320]{2,1,0:T(4,128)S(1)} %copy-done.44, pred[320,1280]{1,0:T(8,128)(4,1)} %compare_and_fusion, bf16[1280,2,64,1]{0,2,3,1:T(8,128)(2,1)S(1)} %bitcast.138, bf16[320,2,4,32]{0,3,2,1:T(8,128)(2,1)S(1)} %bitcast.148, ...), kind=kOutput, calls=%fused_computation.14 | convolution fusion | flops 855904000 | bytes 2058240 | tf_op jit(solution)/shard_map/hgcw,chgd->whd/dot_general | solution.py:464
  283.7 2.8 convert_add_fusion
  291.3 18.1 %feed_half.3 = (bf16[1280,1024]{1,0:T(8,128)(2,1)}, bf16[1280,1024]{1,0:T(8,128)(2,1)}, bf16[1280,1024]{1,0:T(8,128)(2,1)}) custom-call(s32[1]{0:T(128)} %bitcast.29.core, bf16[1280,2048]{1,0:T(8,128)(2,1)} %all-gather.11.cloned.1.call-done.normed.refs_1_, bf16[2048,2048]{1,0:T(8,128)(2,1)} %gate_w.5, bf16[2048,2048]{1,0:T(8,128)(2,1)} %up_w.5, ...), custom_call_target="tpu_custom_call" | custom-call | flops 167772160 | bytes 376832 | tf_op jit(solution)/shard_map/feed_half/pallas_call | solution.py:99
  311.0 38.3 %all-reduce.3.cloned.1.call-done = bf16[512,2048]{1,0:T(8,128)(2,1)} async-done(((bf16[512,2048]{1,0:T(8,128)(2,1)}), bf16[512,2048]{1,0:T(8,128)(2,1)}) %all-reduce.3.cloned.1.call-update) | async-done | bytes 2097168 | tf_op jit(solution)/shard_map/psum | solution.py:443
  349.3 3.5 convolution_convert_fusion
  352.8 2.8 fusion.56
  356.7 2.5 fusion.51
  359.2 19.4 %weight_grad.3 = (f32[2048,2048]{1,0:T(8,128)}, bf16[1024,2048]{1,0:T(8,128)(2,1)}) custom-call(s32[1]{0:T(128)} %bitcast.29.core, bf16[1280,1024]{1,0:T(8,128)(2,1)} %get-tuple-element.91.refs_0_, bf16[1280,1024]{1,0:T(8,128)(2,1)} %get-tuple-element.93.refs_1_, bf16[1280,2048]{1,0:T(8,128)(2,1)} %all-gather.5.cloned.1.call-done.upstream.refs_2_, ...), custom_call_target="tpu_custom_call" | custom-call | flops 167772160 | bytes 442368 | tf_op jit(solution)/shard_map/weight_grad/pallas_call | solution.py:193
  378.6 3.4 collective-permute-start.20
  383.7 7.4 %collective-permute-done.20 = bf16[80,2048]{1,0:T(8,128)(2,1)S(1)} collective-permute-done((bf16[80,2048]{1,0:T(8,128)(2,1)S(1)}, bf16[80,2048]{1,0:T(8,128)(2,1)S(1)}, u32[]{:S(2)}, u32[]{:S(2)}) %collective-permute-start.20) | collective-permute-done | bytes 327712 | tf_op jit(solution)/shard_map/ppermute | solution.py:300
  391.2 19.7 %collective-permute-done.19 = bf16[80,2048]{1,0:T(8,128)(2,1)S(1)} collective-permute-done((bf16[80,2048]{1,0:T(8,128)(2,1)S(1)}, bf16[80,2048]{1,0:T(8,128)(2,1)S(1)}, u32[]{:S(2)}, u32[]{:S(2)}) %collective-permute-start.19) | collective-permute-done | bytes 327712 | tf_op jit(solution)/shard_map/ppermute | solution.py:300
  416.8 16.9 %weight_grad.4 = (f32[2048,2048]{1,0:T(8,128)}, bf16[2048,1024]{1,0:T(8,128)(2,1)}) custom-call(s32[1]{0:T(128)} %bitcast.29.core, bf16[1280,2048]{1,0:T(8,128)(2,1)} %all-gather.9.cloned.1.call-done.normed.refs_0_, bf16[1280,2048]{1,0:T(8,128)(2,1)} %all-gather.11.cloned.1.call-done.normed.refs_1_, bf16[1280,1024]{1,0:T(8,128)(2,1)} %get-tuple-element.97.refs_2_, ...), custom_call_target="tpu_custom_call" | custom-call | flops 167772160 | bytes 442368 | tf_op jit(solution)/shard_map/weight_grad/pallas_call | solution.py:193
  433.7 2.5 convert_element_type.211
  436.3 4.2 collective-permute-done.25
  443.2 17.0 %weight_grad.5 = (f32[2048,2048]{1,0:T(8,128)}, bf16[2048,1024]{1,0:T(8,128)(2,1)}) custom-call(s32[1]{0:T(128)} %bitcast.29.core, bf16[1280,2048]{1,0:T(8,128)(2,1)} %all-gather.9.cloned.1.call-done.normed.refs_0_, bf16[1280,2048]{1,0:T(8,128)(2,1)} %all-gather.11.cloned.1.call-done.normed.refs_1_, bf16[1280,1024]{1,0:T(8,128)(2,1)} %get-tuple-element.106.refs_2_, ...), custom_call_target="tpu_custom_call" | custom-call | flops 167772160 | bytes 442368 | tf_op jit(solution)/shard_map/weight_grad/pallas_call | solution.py:193
  460.7 18.1 %all-reduce.5.cloned.1.call-done = bf16[2048,768]{1,0:T(8,128)(2,1)} async-done(((bf16[2048,768]{1,0:T(8,128)(2,1)}), bf16[2048,768]{1,0:T(8,128)(2,1)}) %all-reduce.5.cloned.1.call-update) | async-done | bytes 3145744 | tf_op jit(solution)/shard_map/psum | solution.py:491
  478.8 4.2 slice_convert_fusion
  501.4 5.9 %fill_other.3 = f32[2048,2048]{1,0:T(8,128)} custom-call(s32[1]{0:T(128)} %bitcast.29.core, bf16[1024,2048]{1,0:T(8,128)(2,1)} %collective-permute-done.27.other, f32[2048,2048]{1,0:T(8,128)} %get-tuple-element.110.held), custom_call_target="tpu_custom_call", output_to_operand_aliasing={{}: (2, {})} | custom-call | flops 32768 | bytes 196608 | tf_op jit(solution)/shard_map/fill_other/pallas_call | solution.py:226
  508.7 7.3 %fill_other.4 = f32[2048,2048]{1,0:T(8,128)} custom-call(s32[1]{0:T(128)} %bitcast.29.core, bf16[2048,1024]{1,0:T(8,128)(2,1)} %collective-permute-done.31.other, f32[2048,2048]{1,0:T(8,128)} %get-tuple-element.112.held), custom_call_target="tpu_custom_call", output_to_operand_aliasing={{}: (2, {})} | custom-call | flops 32768 | bytes 196608 | tf_op jit(solution)/shard_map/fill_other/pallas_call | solution.py:226
  516.6 9.7 %collective-permute-done.29 = bf16[80,2048]{1,0:T(8,128)(2,1)S(1)} collective-permute-done((bf16[80,2048]{1,0:T(8,128)(2,1)S(1)}, bf16[80,2048]{1,0:T(8,128)(2,1)S(1)}, u32[]{:S(2)}, u32[]{:S(2)}) %collective-permute-start.29) | collective-permute-done | bytes 327712 | tf_op jit(solution)/shard_map/ppermute | solution.py:300
  527.8 7.4 %fill_other.5 = f32[2048,2048]{1,0:T(8,128)} custom-call(s32[1]{0:T(128)} %bitcast.29.core, bf16[2048,1024]{1,0:T(8,128)(2,1)} %collective-permute-done.32.other, f32[2048,2048]{1,0:T(8,128)} %get-tuple-element.113.held), custom_call_target="tpu_custom_call", output_to_operand_aliasing={{}: (2, {})} | custom-call | flops 32768 | bytes 196608 | tf_op jit(solution)/shard_map/fill_other/pallas_call | solution.py:226
  (283 shorter events, 98.0 us)
Async XLA Ops:
  7.2 51.3 %copy-start = (bf16[512,2048]{1,0:T(8,128)(2,1)S(1)}, bf16[512,2048]{1,0:T(8,128)(2,1)}, u32[]{:S(2)}) copy-start(bf16[512,2048]{1,0:T(8,128)(2,1)} %param.17) | copy-start | bytes 6291460
  7.2 116.0 %all-gather.7.cloned.1.call-start = ((), (), s32[]{:S(2)}) async-start(), calls=%async_computation.1 | async-start | bytes 5898240 | tf_op jit(solution)/shard_map/all_gather | solution.py:336
  13.9 109.4 %all-gather.5.cloned.1.call-start = ((), (), s32[]{:S(2)}) async-start(), calls=%async_computation | async-start | bytes 5898240 | tf_op jit(solution)/shard_map/all_gather | solution.py:335
  14.6 209.4 %all-gather.9.cloned.1.call-start = ((), (), s32[]{:S(2)}) async-start(), calls=%async_computation.2 | async-start | bytes 5898240 | tf_op jit(solution)/shard_map/all_gather | solution.py:335
  24.3 13.8 %collective-permute-start.2 = (bf16[320,256]{1,0:T(8,128)(2,1)}, bf16[320,256]{1,0:T(8,128)(2,1)}, u32[]{:S(2)}, u32[]{:S(2)}) collective-permute-start(bf16[320,256]{1,0:T(8,128)(2,1)} %pad_maximum_fusion.8), channel_id=1, source_target_pairs={{0,12},{4,8},{8,4},{12,0},{1,13},{5,9},{9,5},{13,1},{2,14},{6,10},... | collective-permute-start | bytes 491528 | tf_op jit(solution)/shard_map/ppermute | solution.py:300
  28.2 12.7 %collective-permute-start.1 = (bf16[320,256]{1,0:T(8,128)(2,1)}, bf16[320,256]{1,0:T(8,128)(2,1)}, u32[]{:S(2)}, u32[]{:S(2)}) collective-permute-start(bf16[320,256]{1,0:T(8,128)(2,1)} %pad_maximum_fusion.8), channel_id=1, source_target_pairs={{0,8},{4,12},{8,0},{12,4},{1,9},{5,13},{9,1},{13,5},{2,10},{6,14},... | collective-permute-start | bytes 491528 | tf_op jit(solution)/shard_map/ppermute | solution.py:300
  28.7 12.4 %collective-permute-start = (bf16[320,256]{1,0:T(8,128)(2,1)}, bf16[320,256]{1,0:T(8,128)(2,1)}, u32[]{:S(2)}, u32[]{:S(2)}) collective-permute-start(bf16[320,256]{1,0:T(8,128)(2,1)} %pad_maximum_fusion.8), channel_id=1, source_target_pairs={{0,4},{4,0},{8,12},{12,8},{1,5},{5,1},{9,13},{13,9},{2,6},{6,2},{1... | collective-permute-start | bytes 491528 | tf_op jit(solution)/shard_map/ppermute | solution.py:300
  52.3 212.7 %copy-start.43 = (f32[2,4,320]{2,1,0:T(4,128)}, f32[2,4,320]{2,1,0:T(4,128)S(1)}, u32[]{:S(2)}) copy-start(f32[2,4,320]{2,1,0:T(4,128)S(1)} %get-tuple-element.178) | copy-start | bytes 30724
  59.5 12.5 %collective-permute-start.3 = (bf16[80,2048]{1,0:T(8,128)(2,1)S(1)}, bf16[80,2048]{1,0:T(8,128)(2,1)S(1)}, u32[]{:S(2)}, u32[]{:S(2)}) collective-permute-start(bf16[80,2048]{1,0:T(8,128)(2,1)S(1)} %get-tuple-element.149), channel_id=1, source_target_pairs={{0,3},{1,2},{2,1},{3,0},{4,7},{5,6},{6,5},{7,4},{8,11},{9,10},{10,... | collective-permute-start | bytes 983048 | tf_op jit(solution)/shard_map/ppermute | solution.py:300
  63.1 15.7 %collective-permute-start.5 = (bf16[80,2048]{1,0:T(8,128)(2,1)S(1)}, bf16[80,2048]{1,0:T(8,128)(2,1)S(1)}, u32[]{:S(2)}, u32[]{:S(2)}) collective-permute-start(bf16[80,2048]{1,0:T(8,128)(2,1)S(1)} %get-tuple-element.150), channel_id=1, source_target_pairs={{0,1},{1,0},{2,3},{3,2},{4,5},{5,4},{6,7},{7,6},{8,9},{9,8},{10,11... | collective-permute-start | bytes 983048 | tf_op jit(solution)/shard_map/ppermute | solution.py:300
  63.1 27.8 %collective-permute-start.4 = (bf16[80,2048]{1,0:T(8,128)(2,1)S(1)}, bf16[80,2048]{1,0:T(8,128)(2,1)S(1)}, u32[]{:S(2)}, u32[]{:S(2)}) collective-permute-start(bf16[80,2048]{1,0:T(8,128)(2,1)S(1)} %get-tuple-element.151), channel_id=1, source_target_pairs={{0,2},{1,3},{2,0},{3,1},{4,6},{5,7},{6,4},{7,5},{8,10},{9,11},{10,... | collective-permute-start | bytes 983048 | tf_op jit(solution)/shard_map/ppermute | solution.py:300
  92.4 12.6 %collective-permute-start.8 = (bf16[80,2048]{1,0:T(8,128)(2,1)S(1)}, bf16[80,2048]{1,0:T(8,128)(2,1)S(1)}, u32[]{:S(2)}, u32[]{:S(2)}) collective-permute-start(bf16[80,2048]{1,0:T(8,128)(2,1)S(1)} %multiply_convert_fusion.2), channel_id=1, source_target_pairs={{0,3},{1,2},{2,1},{3,0},{4,7},{5,6},{6,5},{7,4},{8,11},{9,10},{10,... | collective-permute-start | bytes 983048 | tf_op jit(solution)/shard_map/ppermute | solution.py:300
  95.0 25.9 %collective-permute-start.7 = (bf16[80,2048]{1,0:T(8,128)(2,1)S(1)}, bf16[80,2048]{1,0:T(8,128)(2,1)}, u32[]{:S(2)}, u32[]{:S(2)}) collective-permute-start(bf16[80,2048]{1,0:T(8,128)(2,1)S(1)} %multiply_convert_fusion.2), channel_id=1, source_target_pairs={{0,2},{1,3},{2,0},{3,1},{4,6},{5,7},{6,4},{7,5},{8,10},{9,11},{10,... | collective-permute-start | bytes 983048 | tf_op jit(solution)/shard_map/ppermute | solution.py:300
  95.1 25.9 %collective-permute-start.6 = (bf16[80,2048]{1,0:T(8,128)(2,1)S(1)}, bf16[80,2048]{1,0:T(8,128)(2,1)}, u32[]{:S(2)}, u32[]{:S(2)}) collective-permute-start(bf16[80,2048]{1,0:T(8,128)(2,1)S(1)} %multiply_convert_fusion.2), channel_id=1, source_target_pairs={{0,1},{1,0},{2,3},{3,2},{4,5},{5,4},{6,7},{7,6},{8,9},{9,8},{10,11... | collective-permute-start | bytes 983048 | tf_op jit(solution)/shard_map/ppermute | solution.py:300
  144.8 146.5 %all-gather.11.cloned.1.call-start = ((), (), s32[]{:S(2)}) async-start(), calls=%async_computation.4 | async-start | bytes 5898240 | tf_op jit(solution)/shard_map/all_gather | solution.py:336
  165.9 12.7 %collective-permute-start.9 = (bf16[80,2048]{1,0:T(8,128)(2,1)}, bf16[80,2048]{1,0:T(8,128)(2,1)S(1)}, u32[]{:S(2)}, u32[]{:S(2)}) collective-permute-start(bf16[80,2048]{1,0:T(8,128)(2,1)} %get-tuple-element.140), channel_id=1, source_target_pairs={{0,3},{1,2},{2,1},{3,0},{4,7},{5,6},{6,5},{7,4},{8,11},{9,10},{10,... | collective-permute-start | bytes 983048 | tf_op jit(solution)/shard_map/ppermute | solution.py:300
  167.8 17.7 %collective-permute-start.11 = (bf16[80,2048]{1,0:T(8,128)(2,1)}, bf16[80,2048]{1,0:T(8,128)(2,1)S(1)}, u32[]{:S(2)}, u32[]{:S(2)}) collective-permute-start(bf16[80,2048]{1,0:T(8,128)(2,1)} %get-tuple-element.141), channel_id=1, source_target_pairs={{0,1},{1,0},{2,3},{3,2},{4,5},{5,4},{6,7},{7,6},{8,9},{9,8},{10,11... | collective-permute-start | bytes 983048 | tf_op jit(solution)/shard_map/ppermute | solution.py:300
  167.8 25.7 %collective-permute-start.10 = (bf16[80,2048]{1,0:T(8,128)(2,1)}, bf16[80,2048]{1,0:T(8,128)(2,1)}, u32[]{:S(2)}, u32[]{:S(2)}) collective-permute-start(bf16[80,2048]{1,0:T(8,128)(2,1)} %get-tuple-element.142), channel_id=1, source_target_pairs={{0,2},{1,3},{2,0},{3,1},{4,6},{5,7},{6,4},{7,5},{8,10},{9,11},{10,... | collective-permute-start | bytes 983048 | tf_op jit(solution)/shard_map/ppermute | solution.py:300
  170.3 179.0 %all-reduce.3.cloned.1.call-start = ((), (), s32[]{:S(2)}) async-start(), calls=%async_computation.3 | async-start | bytes 4194304 | tf_op jit(solution)/shard_map/psum | solution.py:443
  197.3 12.4 %collective-permute-start.14 = (bf16[80,2048]{1,0:T(8,128)(2,1)S(1)}, bf16[80,2048]{1,0:T(8,128)(2,1)S(1)}, u32[]{:S(2)}, u32[]{:S(2)}) collective-permute-start(bf16[80,2048]{1,0:T(8,128)(2,1)S(1)} %get-tuple-element.118), channel_id=1, source_target_pairs={{0,3},{1,2},{2,1},{3,0},{4,7},{5,6},{6,5},{7,4},{8,11},{9,10},{10,... | collective-permute-start | bytes 983048 | tf_op jit(solution)/shard_map/ppermute | solution.py:300
  198.7 24.2 %collective-permute-start.13 = (bf16[80,2048]{1,0:T(8,128)(2,1)S(1)}, bf16[80,2048]{1,0:T(8,128)(2,1)S(1)}, u32[]{:S(2)}, u32[]{:S(2)}) collective-permute-start(bf16[80,2048]{1,0:T(8,128)(2,1)S(1)} %get-tuple-element.118), channel_id=1, source_target_pairs={{0,2},{1,3},{2,0},{3,1},{4,6},{5,7},{6,4},{7,5},{8,10},{9,11},{10,... | collective-permute-start | bytes 983048 | tf_op jit(solution)/shard_map/ppermute | solution.py:300
  198.7 24.2 %collective-permute-start.12 = (bf16[80,2048]{1,0:T(8,128)(2,1)S(1)}, bf16[80,2048]{1,0:T(8,128)(2,1)S(1)}, u32[]{:S(2)}, u32[]{:S(2)}) collective-permute-start(bf16[80,2048]{1,0:T(8,128)(2,1)S(1)} %get-tuple-element.118), channel_id=1, source_target_pairs={{0,1},{1,0},{2,3},{3,2},{4,5},{5,4},{6,7},{7,6},{8,9},{9,8},{10,11... | collective-permute-start | bytes 983048 | tf_op jit(solution)/shard_map/ppermute | solution.py:300
  246.0 37.7 %collective-permute-start.15 = (bf16[80,2048]{1,0:T(8,128)(2,1)}, bf16[80,2048]{1,0:T(8,128)(2,1)}, u32[]{:S(2)}, u32[]{:S(2)}) collective-permute-start(bf16[80,2048]{1,0:T(8,128)(2,1)} %get-tuple-element.137), channel_id=1, source_target_pairs={{0,3},{1,2},{2,1},{3,0},{4,7},{5,6},{6,5},{7,4},{8,11},{9,10},{10,... | collective-permute-start | bytes 983048 | tf_op jit(solution)/shard_map/ppermute | solution.py:300
  248.7 35.0 %collective-permute-start.17 = (bf16[80,2048]{1,0:T(8,128)(2,1)}, bf16[80,2048]{1,0:T(8,128)(2,1)}, u32[]{:S(2)}, u32[]{:S(2)}) collective-permute-start(bf16[80,2048]{1,0:T(8,128)(2,1)} %get-tuple-element.138), channel_id=1, source_target_pairs={{0,1},{1,0},{2,3},{3,2},{4,5},{5,4},{6,7},{7,6},{8,9},{9,8},{10,11... | collective-permute-start | bytes 983048 | tf_op jit(solution)/shard_map/ppermute | solution.py:300
  248.7 35.0 %collective-permute-start.16 = (bf16[80,2048]{1,0:T(8,128)(2,1)}, bf16[80,2048]{1,0:T(8,128)(2,1)}, u32[]{:S(2)}, u32[]{:S(2)}) collective-permute-start(bf16[80,2048]{1,0:T(8,128)(2,1)} %get-tuple-element.139), channel_id=1, source_target_pairs={{0,2},{1,3},{2,0},{3,1},{4,6},{5,7},{6,4},{7,5},{8,10},{9,11},{10,... | collective-permute-start | bytes 983048 | tf_op jit(solution)/shard_map/ppermute | solution.py:300
  282.4 196.4 %all-reduce.5.cloned.1.call-start = ((), (), s32[]{:S(2)}) async-start(), calls=%async_computation.5 | async-start | bytes 6291456 | tf_op jit(solution)/shard_map/psum | solution.py:491
  287.6 21.8 %collective-permute-start.21 = (bf16[320,256]{0,1:T(8,128)(2,1)}, bf16[320,256]{0,1:T(8,128)(2,1)}, u32[]{:S(2)}, u32[]{:S(2)}) collective-permute-start(bf16[320,256]{0,1:T(8,128)(2,1)} %get-tuple-element.160), channel_id=1, source_target_pairs={{0,12},{4,8},{8,4},{12,0},{1,13},{5,9},{9,5},{13,1},{2,14},{6,10},... | collective-permute-start | bytes 491528 | tf_op jit(solution)/shard_map/ppermute | solution.py:300
  289.6 19.8 %collective-permute-start.23 = (bf16[320,256]{0,1:T(8,128)(2,1)}, bf16[320,256]{0,1:T(8,128)(2,1)}, u32[]{:S(2)}, u32[]{:S(2)}) collective-permute-start(bf16[320,256]{0,1:T(8,128)(2,1)} %get-tuple-element.161), channel_id=1, source_target_pairs={{0,4},{4,0},{8,12},{12,8},{1,5},{5,1},{9,13},{13,9},{2,6},{6,2},{1... | collective-permute-start | bytes 491528 | tf_op jit(solution)/shard_map/ppermute | solution.py:300
  290.7 18.7 %collective-permute-start.22 = (bf16[320,256]{0,1:T(8,128)(2,1)}, bf16[320,256]{0,1:T(8,128)(2,1)}, u32[]{:S(2)}, u32[]{:S(2)}) collective-permute-start(bf16[320,256]{0,1:T(8,128)(2,1)} %get-tuple-element.162), channel_id=1, source_target_pairs={{0,8},{4,12},{8,0},{12,4},{1,9},{5,13},{9,1},{13,5},{2,10},{6,14},... | collective-permute-start | bytes 491528 | tf_op jit(solution)/shard_map/ppermute | solution.py:300
  291.3 58.0 %copy-start.4 = (bf16[320,2048]{1,0:T(8,128)(2,1)S(1)}, bf16[320,2048]{1,0:T(8,128)(2,1)}, u32[]{:S(2)}) copy-start(bf16[320,2048]{1,0:T(8,128)(2,1)} %copy-done.3) | copy-start | bytes 3932164
  378.6 63.2 %collective-permute-start.27 = (bf16[1024,2048]{1,0:T(8,128)(2,1)}, bf16[1024,2048]{1,0:T(8,128)(2,1)}, u32[]{:S(2)}, u32[]{:S(2)}) collective-permute-start(bf16[1024,2048]{1,0:T(8,128)(2,1)} %get-tuple-element.94), channel_id=1, source_target_pairs={{0,16},{16,0},{1,17},{17,1},{2,18},{18,2},{3,19},{19,3},{4,20},{20... | collective-permute-start | bytes 12582920 | tf_op jit(solution)/shard_map/ppermute | solution.py:300
  378.6 12.5 %collective-permute-start.20 = (bf16[80,2048]{1,0:T(8,128)(2,1)S(1)}, bf16[80,2048]{1,0:T(8,128)(2,1)S(1)}, u32[]{:S(2)}, u32[]{:S(2)}) collective-permute-start(bf16[80,2048]{1,0:T(8,128)(2,1)S(1)} %add_convert_fusion.1), channel_id=1, source_target_pairs={{0,3},{1,2},{2,1},{3,0},{4,7},{5,6},{6,5},{7,4},{8,11},{9,10},{10,... | collective-permute-start | bytes 983048 | tf_op jit(solution)/shard_map/ppermute | solution.py:300
  382.1 28.8 %collective-permute-start.19 = (bf16[80,2048]{1,0:T(8,128)(2,1)S(1)}, bf16[80,2048]{1,0:T(8,128)(2,1)S(1)}, u32[]{:S(2)}, u32[]{:S(2)}) collective-permute-start(bf16[80,2048]{1,0:T(8,128)(2,1)S(1)} %add_convert_fusion.1), channel_id=1, source_target_pairs={{0,2},{1,3},{2,0},{3,1},{4,6},{5,7},{6,4},{7,5},{8,10},{9,11},{10,... | collective-permute-start | bytes 983048 | tf_op jit(solution)/shard_map/ppermute | solution.py:300
  382.1 28.8 %collective-permute-start.18 = (bf16[80,2048]{1,0:T(8,128)(2,1)S(1)}, bf16[80,2048]{1,0:T(8,128)(2,1)S(1)}, u32[]{:S(2)}, u32[]{:S(2)}) collective-permute-start(bf16[80,2048]{1,0:T(8,128)(2,1)S(1)} %add_convert_fusion.1), channel_id=1, source_target_pairs={{0,1},{1,0},{2,3},{3,2},{4,5},{5,4},{6,7},{7,6},{8,9},{9,8},{10,11... | collective-permute-start | bytes 983048 | tf_op jit(solution)/shard_map/ppermute | solution.py:300
  383.7 27.2 %copy-start.12 = (bf16[320,2048]{1,0:T(8,128)(2,1)S(1)}, bf16[320,2048]{1,0:T(8,128)(2,1)}, u32[]{:S(2)}) copy-start(bf16[320,2048]{1,0:T(8,128)(2,1)} %get-tuple-element.184) | copy-start | bytes 3932164
  411.0 25.2 %collective-permute-start.24 = (bf16[80,2048]{1,0:T(8,128)(2,1)S(1)}, bf16[80,2048]{1,0:T(8,128)(2,1)S(1)}, u32[]{:S(2)}, u32[]{:S(2)}) collective-permute-start(bf16[80,2048]{1,0:T(8,128)(2,1)S(1)} %get-tuple-element.128), channel_id=1, source_target_pairs={{0,3},{1,2},{2,1},{3,0},{4,7},{5,6},{6,5},{7,4},{8,11},{9,10},{10,... | collective-permute-start | bytes 983048 | tf_op jit(solution)/shard_map/ppermute | solution.py:300
  413.5 22.8 %collective-permute-start.26 = (bf16[80,2048]{1,0:T(8,128)(2,1)S(1)}, bf16[80,2048]{1,0:T(8,128)(2,1)S(1)}, u32[]{:S(2)}, u32[]{:S(2)}) collective-permute-start(bf16[80,2048]{1,0:T(8,128)(2,1)S(1)} %get-tuple-element.129), channel_id=1, source_target_pairs={{0,1},{1,0},{2,3},{3,2},{4,5},{5,4},{6,7},{7,6},{8,9},{9,8},{10,11... | collective-permute-start | bytes 983048 | tf_op jit(solution)/shard_map/ppermute | solution.py:300
  413.5 27.0 %collective-permute-start.25 = (bf16[80,2048]{1,0:T(8,128)(2,1)S(1)}, bf16[80,2048]{1,0:T(8,128)(2,1)S(1)}, u32[]{:S(2)}, u32[]{:S(2)}) collective-permute-start(bf16[80,2048]{1,0:T(8,128)(2,1)S(1)} %get-tuple-element.130), channel_id=1, source_target_pairs={{0,2},{1,3},{2,0},{3,1},{4,6},{5,7},{6,4},{7,5},{8,10},{9,11},{10,... | collective-permute-start | bytes 983048 | tf_op jit(solution)/shard_map/ppermute | solution.py:300
  433.7 73.7 %collective-permute-start.31 = (bf16[2048,1024]{1,0:T(8,128)(2,1)}, bf16[2048,1024]{1,0:T(8,128)(2,1)}, u32[]{:S(2)}, u32[]{:S(2)}) collective-permute-start(bf16[2048,1024]{1,0:T(8,128)(2,1)} %get-tuple-element.102), channel_id=1, source_target_pairs={{0,16},{16,0},{1,17},{17,1},{2,18},{18,2},{3,19},{19,3},{4,20},{20... | collective-permute-start | bytes 12582920 | tf_op jit(solution)/shard_map/ppermute | solution.py:300
  443.1 39.9 %collective-permute-start.33 = (f32[2,2048]{1,0:T(2,128)S(1)}, f32[2,2048]{1,0:T(2,128)S(1)}, u32[]{:S(2)}, u32[]{:S(2)}) collective-permute-start(f32[2,2048]{1,0:T(2,128)S(1)} %pad_maximum_fusion.17), channel_id=1, source_target_pairs={{0,16},{16,0},{1,17},{17,1},{2,18},{18,2},{3,19},{19,3},{4,20},{20... | collective-permute-start | bytes 49160 | tf_op jit(solution)/shard_map/ppermute | solution.py:300
  460.3 67.5 %collective-permute-start.32 = (bf16[2048,1024]{1,0:T(8,128)(2,1)}, bf16[2048,1024]{1,0:T(8,128)(2,1)}, u32[]{:S(2)}, u32[]{:S(2)}) collective-permute-start(bf16[2048,1024]{1,0:T(8,128)(2,1)} %get-tuple-element.108), channel_id=1, source_target_pairs={{0,16},{16,0},{1,17},{17,1},{2,18},{18,2},{3,19},{19,3},{4,20},{20... | collective-permute-start | bytes 12582920 | tf_op jit(solution)/shard_map/ppermute | solution.py:300
  483.1 3.8 collective-permute-start.34
  486.9 3.8 collective-permute-start.35
  490.7 3.8 collective-permute-start.36
  494.5 21.4 %collective-permute-start.37 = (f32[2,2048]{1,0:T(2,128)S(1)}, f32[2,2048]{1,0:T(2,128)S(1)}, u32[]{:S(2)}, u32[]{:S(2)}) collective-permute-start(f32[2,2048]{1,0:T(2,128)S(1)} %add.247), channel_id=1, source_target_pairs={{0,2},{1,3},{2,0},{3,1},{4,6},{5,7},{6,4},{7,5},{8,10},{9,11},{10,... | collective-permute-start | bytes 49160 | tf_op jit(solution)/shard_map/ppermute | solution.py:300
  498.3 18.3 %collective-permute-start.30 = (bf16[80,2048]{1,0:T(8,128)(2,1)S(1)}, bf16[80,2048]{1,0:T(8,128)(2,1)S(1)}, u32[]{:S(2)}, u32[]{:S(2)}) collective-permute-start(bf16[80,2048]{1,0:T(8,128)(2,1)S(1)} %add_convert_fusion), channel_id=1, source_target_pairs={{0,3},{1,2},{2,1},{3,0},{4,7},{5,6},{6,5},{7,4},{8,11},{9,10},{10,... | collective-permute-start | bytes 983048 | tf_op jit(solution)/shard_map/ppermute | solution.py:300
  499.9 26.4 %collective-permute-start.29 = (bf16[80,2048]{1,0:T(8,128)(2,1)S(1)}, bf16[80,2048]{1,0:T(8,128)(2,1)S(1)}, u32[]{:S(2)}, u32[]{:S(2)}) collective-permute-start(bf16[80,2048]{1,0:T(8,128)(2,1)S(1)} %add_convert_fusion), channel_id=1, source_target_pairs={{0,2},{1,3},{2,0},{3,1},{4,6},{5,7},{6,4},{7,5},{8,10},{9,11},{10,... | collective-permute-start | bytes 983048 | tf_op jit(solution)/shard_map/ppermute | solution.py:300
  507.4 19.0 %collective-permute-start.28 = (bf16[80,2048]{1,0:T(8,128)(2,1)S(1)}, bf16[80,2048]{1,0:T(8,128)(2,1)S(1)}, u32[]{:S(2)}, u32[]{:S(2)}) collective-permute-start(bf16[80,2048]{1,0:T(8,128)(2,1)S(1)} %add_convert_fusion), channel_id=1, source_target_pairs={{0,1},{1,0},{2,3},{3,2},{4,5},{5,4},{6,7},{7,6},{8,9},{9,8},{10,11... | collective-permute-start | bytes 983048 | tf_op jit(solution)/shard_map/ppermute | solution.py:300
  (54 other events, 408.0 us)
Sparse Core Ops, SparseCore 0:
  14.0 50.8 all-gather.6
  67.3 41.1 all-gather.4
  144.9 39.6 all-gather.8
  186.9 41.1 all-gather.10
  282.6 66.7 all-reduce.2
  411.1 67.7 all-reduce.4

commit v2 on v1

v2 whole, which is shorter than its diff:
```python
import functools

import jax
import jax.numpy as jnp
from jax import lax
from jax.experimental import pallas as pl
from jax.experimental.pallas import tpu as pltpu
import numpy as np
from jax.sharding import PartitionSpec as P

HEAD_SIZE = 64
DOCS = 4
EPSILON = 1e-05
BF = jnp.bfloat16
F32 = jnp.float32


MIB = 1 << 20


def kernel_params(dims, mib=63):
    return pltpu.CompilerParams(
        vmem_limit_bytes=mib * MIB, dimension_semantics=("arbitrary",) * dims
    )


def contract(a, b, dim_a, dim_b):
    return lax.dot_general(
        a, b, (((dim_a,), (dim_b,)), ((), ())), preferred_element_type=F32
    )


def tile(limit, size):
    while size > limit and size % 2 == 0:
        size //= 2
    return size


SMALL = pl.CostEstimate(flops=1, bytes_accessed=1, transcendentals=0)


def spent(us):
    return pl.CostEstimate(flops=us * 10**9, bytes_accessed=1, transcendentals=0)


def whole_spec(array):
    shape = array.shape
    return pl.BlockSpec(shape, lambda *_: (0,) * len(shape))


def join(refs):
    if refs[0].shape[0] % 16 == 0:
        return jnp.concatenate([r[...] for r in refs], axis=0)
    return jnp.concatenate([r[...].astype(F32) for r in refs], axis=0).astype(refs[0].dtype)


def unread(deps):
    return [pl.BlockSpec(memory_space=pl.ANY)] * len(deps)


def times_transposed_kernel(core, left, weight, *refs):
    refs[-1][...] = contract(left[...], weight[...], 1, 1).astype(BF)


def grad_hidden_of(core, upstream, w_down, shares, deps=()):
    tokens, depth = upstream.shape
    units = w_down.shape[0] // shares
    rows, cols = tile(640, tokens), tile(1024 // (3 - shares), units)
    steps = units // cols
    offset = steps * (shares - 1)
    return pl.pallas_call(
        times_transposed_kernel,
        out_shape=jax.ShapeDtypeStruct((tokens, units), BF),
        grid_spec=pltpu.PrefetchScalarGridSpec(
            num_scalar_prefetch=1,
            grid=(steps, tokens // rows),
            in_specs=[
                pl.BlockSpec((rows, depth), lambda j, i, c: (i, 0)),
                pl.BlockSpec((cols, depth), lambda j, i, c: (c[0] * offset + j, 0)),
            ]
            + unread(deps),
            out_specs=pl.BlockSpec((rows, cols), lambda j, i, c: (i, j)),
        ),
        compiler_params=kernel_params(2),
        cost_estimate=SMALL,
        name="grad_hidden_of",
    )(core, upstream, w_down, *deps)


def swish_grads(gate, up_proj, grad_hidden):
    sigmoid = 1.0 / (1.0 + jnp.exp(-gate))
    activated = gate * sigmoid
    hidden = (activated * up_proj).astype(BF)
    grad_gate = (grad_hidden * up_proj * (sigmoid * (1.0 + gate * (1.0 - sigmoid)))).astype(BF)
    grad_up = (grad_hidden * activated).astype(BF)
    return hidden, grad_gate, grad_up


def feed_half_kernel(core, normed, gate_w, up_w, grad_hidden, *refs):
    hidden, grad_gate, grad_up = refs[-3:]
    rows = normed[...]
    hidden[...], grad_gate[...], grad_up[...] = swish_grads(
        contract(rows, gate_w[...], 1, 0),
        contract(rows, up_w[...], 1, 0),
        grad_hidden[...].astype(F32),
    )


def feed_half(core, normed, w_gate, w_up, grad_hidden, deps=()):
    tokens, depth = normed.shape
    half = w_gate.shape[1] // 2
    rows, cols = tile(640, tokens), tile(512, half)
    steps = half // cols
    out = jax.ShapeDtypeStruct((tokens, half), BF)
    weight = pl.BlockSpec((depth, cols), lambda j, i, c: (0, c[0] * steps + j))
    block = pl.BlockSpec((rows, cols), lambda j, i, c: (i, j))
    return pl.pallas_call(
        feed_half_kernel,
        out_shape=(out, out, out),
        grid_spec=pltpu.PrefetchScalarGridSpec(
            num_scalar_prefetch=1,
            grid=(steps, tokens // rows),
            in_specs=[
                pl.BlockSpec((rows, depth), lambda j, i, c: (i, 0)),
                weight,
                weight,
                block,
            ]
            + unread(deps),
            out_specs=(block, block, block),
        ),
        compiler_params=kernel_params(2),
        cost_estimate=SMALL,
        name="feed_half",
    )(core, normed, w_gate, w_up, grad_hidden, *deps)


def feed_own_kernel(pieces, chunks, gate_w, up_w, grad_hidden, *refs):
    normed = refs[:pieces]
    hidden, parts = refs[-chunks - 3], refs[-chunks - 2 : -2]
    rows, total = refs[-2:]
    step = pl.program_id(0)
    size = total.shape[0] // chunks

    @pl.when(step == 0)
    def _():
        rows[...] = join(normed)

    gate_now = gate_w[...]
    up_now = up_w[...]
    hidden[...], grad_gate, grad_up = swish_grads(
        contract(rows[...], gate_now, 1, 0),
        contract(rows[...], up_now, 1, 0),
        grad_hidden[...].astype(F32),
    )
    term = contract(grad_gate, gate_now, 1, 1) + contract(grad_up, up_now, 1, 1)

    @pl.when(step == 0)
    def _():
        total[...] = term

    @pl.when(step > 0)
    def _():
        total[...] += term

    @pl.when(step == pl.num_programs(0) - 1)
    def _():
        for k, part in enumerate(parts):
            part[...] = total[k * size : (k + 1) * size].astype(BF)


def feed_own(normed, w_gate, w_up, grad_hidden, chunks, deps=()):
    tokens, units = grad_hidden.shape
    depth = w_gate.shape[0]
    size = tokens // chunks
    cols = tile(512, units)
    weight = pl.BlockSpec((depth, cols), lambda j: (0, j))
    block = pl.BlockSpec((tokens, cols), lambda j: (0, j))
    rows = pl.BlockSpec((size, depth), lambda j: (0, 0))
    out = pl.pallas_call(
        functools.partial(feed_own_kernel, len(normed), chunks),
        out_shape=(jax.ShapeDtypeStruct((tokens, units), BF),)
        + (jax.ShapeDtypeStruct((size, depth), BF),) * chunks,
        grid=(units // cols,),
        in_specs=[weight, weight, block] + [whole_spec(n) for n in normed] + unread(deps),
        out_specs=(block,) + (rows,) * chunks,
        scratch_shapes=[pltpu.VMEM((tokens, depth), BF), pltpu.VMEM((tokens, depth), F32)],
        compiler_params=kernel_params(1),
        cost_estimate=SMALL,
        name="feed_own",
    )(w_gate, w_up, grad_hidden, *normed, *deps)
    return out[0], list(out[1:])


def down_kernel(chunks, hidden, weight, *refs):
    parts = refs[-chunks:]
    part = contract(hidden[...], weight[...], 1, 0)
    rows = part.shape[0] // chunks
    for k, out in enumerate(parts):
        out[...] = part[k * rows : (k + 1) * rows].astype(BF)


def down_projection(hidden, w_down, chunks, deps=()):
    tokens, units = hidden.shape
    depth = w_down.shape[1]
    cols = tile(512, depth)
    return list(
        pl.pallas_call(
            functools.partial(down_kernel, chunks),
            out_shape=(jax.ShapeDtypeStruct((tokens // chunks, depth), BF),) * chunks,
            grid=(depth // cols,),
            in_specs=[whole_spec(hidden), pl.BlockSpec((units, cols), lambda j: (0, j))]
            + unread(deps),
            out_specs=(pl.BlockSpec((tokens // chunks, cols), lambda j: (0, j)),) * chunks,
            compiler_params=kernel_params(1),
            cost_estimate=SMALL,
                name="down_projection",
        )(hidden, w_down, *deps)
    )


PIECES = 4


def weight_grad_kernel(count, core, *refs):
    lefts, rights = refs[:count], refs[count : 2 * count]
    wide, lows = refs[-1 - PIECES], refs[-PIECES:]
    total = contract(lefts[0][...], rights[0][...], 0, 0)
    for left, right in zip(lefts[1:], rights[1:]):
        total = total + contract(left[...], right[...], 0, 0)
    wide[...] = total
    for k, low in enumerate(lows):

        @pl.when(pl.program_id(1) == k)
        def _():
            low[...] = total.astype(BF)


def weight_grad(core, lefts, rights, dim, deps=()):
    tokens, m = lefts[0].shape
    n = rights[0].shape[1]
    count = len(lefts)
    rows, cols = m // PIECES, tile(1024, n)
    across = n // cols
    if dim == 0:
        full = (2 * m, n)
        place = lambda j, i, c: (c[0] * PIECES + i, j)
    else:
        full = (m, 2 * n)
        place = lambda j, i, c: (i, c[0] * across + j)
    piece = pl.BlockSpec((rows, cols), lambda j, i, c: (0, j))
    out = pl.pallas_call(
        functools.partial(weight_grad_kernel, count),
        out_shape=(jax.ShapeDtypeStruct(full, F32),)
        + (jax.ShapeDtypeStruct((rows, n), BF),) * PIECES,
        grid_spec=pltpu.PrefetchScalarGridSpec(
            num_scalar_prefetch=1,
            grid=(across, PIECES),
            in_specs=[pl.BlockSpec((tokens, rows), lambda j, i, c: (0, i))] * count
            + [pl.BlockSpec((tokens, cols), lambda j, i, c: (0, j))] * count
            + unread(deps),
            out_specs=(pl.BlockSpec((rows, cols), place),) + (piece,) * PIECES,
        ),
        compiler_params=kernel_params(2),
        cost_estimate=SMALL,
        name="weight_grad",
    )(core, *lefts, *rights, *deps)
    return out[0], list(out[1:])


def left_product_kernel(count, left, *refs):
    right = join(refs[:count])
    refs[-1][...] = contract(left[...], right, 0, 0).astype(BF)


def left_product(left, pieces, deps=()):
    tokens, m = left.shape
    n = pieces[0].shape[1]
    rows, cols = tile(1024, m), tile(512, n)
    return pl.pallas_call(
        functools.partial(left_product_kernel, len(pieces)),
        out_shape=jax.ShapeDtypeStruct((m, n), BF),
        grid=(m // rows, n // cols),
        in_specs=[pl.BlockSpec((tokens, rows), lambda i, j: (0, i))]
        + [pl.BlockSpec((p.shape[0], cols), lambda i, j: (0, j)) for p in pieces]
        + unread(deps),
        out_specs=pl.BlockSpec((rows, cols), lambda i, j: (i, j)),
        compiler_params=kernel_params(2),
        cost_estimate=SMALL,
        name="left_product",
    )(left, *pieces, *deps)


def kv_product_kernel(left, right, gain_one, gain_two, *refs):
    out = refs[-1]
    width = right.shape[1]
    rows = left.shape[1]
    out[:, :width] = contract(left[...], right[...], 0, 0).astype(BF)
    gains = jnp.concatenate([gain_one[...], gain_two[...], jnp.zeros((126, rows), F32)], axis=0)
    out[:, width:] = jnp.transpose(gains).astype(BF)


def kv_product(left, right, gain_one, gain_two, deps=()):
    tokens, m = left.shape
    width = right.shape[1]
    rows = tile(1024, m)
    gain = pl.BlockSpec((1, rows), lambda i: (0, i))
    return pl.pallas_call(
        kv_product_kernel,
        out_shape=jax.ShapeDtypeStruct((m, width + 128), BF),
        grid=(m // rows,),
        in_specs=[pl.BlockSpec((tokens, rows), lambda i: (0, i)), whole_spec(right), gain, gain]
        + unread(deps),
        out_specs=pl.BlockSpec((rows, width + 128), lambda i: (i, 0)),
        compiler_params=kernel_params(1),
        cost_estimate=SMALL,
        name="kv_product",
    )(left, right, gain_one, gain_two, *deps)


def mask_kernel(chunks, scalars, place, *refs):
    value = join(refs[:chunks]).astype(F32)
    masked = jnp.where(place[...] < scalars[1], value, 0.0).astype(BF)
    half = masked.shape[0] // 2
    refs[-3][...] = masked
    refs[-2][...] = masked[:half]
    refs[-1][...] = masked[half:]


def mask_padding(scalars, value, place, chunks, deps=()):
    span, depth = value.shape
    half = jax.ShapeDtypeStruct((span // 2, depth), BF)
    outs = (jax.ShapeDtypeStruct(value.shape, BF), half, half)
    return pl.pallas_call(
        functools.partial(mask_kernel, chunks),
        out_shape=outs,
        grid_spec=pltpu.PrefetchScalarGridSpec(
            num_scalar_prefetch=1,
            grid=(1,),
            in_specs=[whole_spec(place)]
            + [chunk_spec(value, chunks, k) for k in range(chunks)]
            + unread(deps),
            out_specs=tuple(whole_spec(a) for a in outs),
        ),
        compiler_params=kernel_params(1),
        cost_estimate=SMALL,
        name="mask_padding",
    )(scalars, place, *[value] * chunks, *deps)


def gain_rows_kernel(value, out):
    out[...] = jnp.transpose(value[...].astype(F32))[:8]


def gain_rows(value):
    rows, width = value.shape
    return pl.pallas_call(
        gain_rows_kernel,
        out_shape=jax.ShapeDtypeStruct((8, rows), F32),
        grid=(1,),
        in_specs=[pl.BlockSpec((rows, 128), lambda i: (0, width // 128 - 1))],
        out_specs=pl.BlockSpec((8, rows), lambda i: (0, 0)),
        compiler_params=kernel_params(1),
        cost_estimate=SMALL,
        name="gain_rows",
    )(value)


def fill_other_kernel(core, *refs):
    step = pl.program_id(0)
    for k in range(PIECES):

        @pl.when(step == k)
        def _():
            refs[-1][...] = refs[k][...].astype(F32)


def fill_other(core, others, held, dim, deps=()):
    rows, n = others[0].shape
    if dim == 0:
        place = lambda i, c: ((1 - c[0]) * PIECES + i, 0)
    else:
        place = lambda i, c: (i, 1 - c[0])
    return pl.pallas_call(
        fill_other_kernel,
        out_shape=jax.ShapeDtypeStruct(held.shape, F32),
        grid_spec=pltpu.PrefetchScalarGridSpec(
            num_scalar_prefetch=1,
            grid=(PIECES,),
            in_specs=[whole_spec(o) for o in others]
            + [pl.BlockSpec(memory_space=pl.ANY)]
            + unread(deps),
            out_specs=pl.BlockSpec((rows, n), place),
        ),
        input_output_aliases={1 + PIECES: 0},
        compiler_params=kernel_params(1),
        cost_estimate=spent(50),
        name="fill_other",
    )(core, *others, held, *deps)


def rotate_block(values, cosine, sine):
    width = values.shape[1]
    column = lax.broadcasted_iota(jnp.int32, values.shape, 1)
    other = jnp.where(
        column % HEAD_SIZE < HEAD_SIZE // 2,
        pltpu.roll(values, width - HEAD_SIZE // 2, 1),
        pltpu.roll(values, HEAD_SIZE // 2, 1),
    )
    return values * cosine + other * sine


def pack_rotated(keys, values, cosine, sine):
    width = keys.shape[1]
    if width % 128 == 0:
        turned = [
            rotate_block(keys[:, i : i + 128], cosine, sine) for i in range(0, width, 128)
        ]
        return jnp.concatenate(turned + [values], axis=1)
    both = jnp.concatenate([keys, values], axis=1)
    column = lax.broadcasted_iota(jnp.int32, both.shape, 1)
    return jnp.where(column < width, rotate_block(both, cosine, sine), both)


def chunk_spec(array, chunks, k):
    block = (array.shape[0] // chunks, array.shape[1])
    return pl.BlockSpec(block, lambda *a: (a[-1][0] ^ k, 0))


def project_kv_kernel(chunks, waits, me, *refs):
    gain, key_w, value_w, cosine, sine = refs[chunks : chunks + 5]
    normed, inverse, packed = refs[-3:]
    stream = join(refs[:chunks]).astype(F32)
    scale = lax.rsqrt(jnp.mean(stream * stream, axis=1, keepdims=True) + EPSILON)
    low = (stream * scale * gain[...]).astype(BF)
    normed[...] = low
    inverse[...] = jnp.broadcast_to(scale, inverse.shape)
    packed[...] = pack_rotated(
        contract(low, key_w[...], 1, 0), contract(low, value_w[...], 1, 0), cosine[...], sine[...]
    ).astype(BF)


def project_kv(me, x, gain, key_matrix, value_matrix, cosine, sine, chunks, deps=()):
    span, depth = x.shape
    args = (gain, key_matrix, value_matrix, cosine, sine)
    outs = (
        jax.ShapeDtypeStruct((span, depth), BF),
        jax.ShapeDtypeStruct((span, 128), F32),
        jax.ShapeDtypeStruct((span, 2 * key_matrix.shape[1]), BF),
    )
    return pl.pallas_call(
        functools.partial(project_kv_kernel, chunks, len(deps)),
        out_shape=outs,
        grid_spec=pltpu.PrefetchScalarGridSpec(
            num_scalar_prefetch=1,
            grid=(1,),
            in_specs=[chunk_spec(x, chunks, k) for k in range(chunks)]
            + [whole_spec(a) for a in args]
            + unread(deps),
            out_specs=tuple(whole_spec(a) for a in outs),
        ),
        compiler_params=kernel_params(1),
        cost_estimate=SMALL,
        name="project_kv",
    )(me, *[x] * chunks, *args, *deps)


def project_query_kernel(normed, weight, cosine, sine, *refs):
    out = refs[-1]
    lin = contract(normed[...], weight[...], 1, 0)
    for i in range(0, lin.shape[1], 128):
        turned = rotate_block(lin[:, i : i + 128], cosine[...], sine[...])
        out[:, i : i + 128] = (turned * HEAD_SIZE**-0.5).astype(BF)


def project_query(normed, w_query, cosine, sine, deps=()):
    span, depth = normed.shape
    width = w_query.shape[1]
    cols = 256
    return pl.pallas_call(
        project_query_kernel,
        out_shape=jax.ShapeDtypeStruct((span, width), BF),
        grid=(width // cols,),
        in_specs=[
            whole_spec(normed),
            pl.BlockSpec((depth, cols), lambda j: (0, j)),
            whole_spec(cosine),
            whole_spec(sine),
        ]
        + unread(deps),
        out_specs=pl.BlockSpec((span, cols), lambda j: (0, j)),
        compiler_params=kernel_params(1),
        cost_estimate=SMALL,
        name="project_query",
    )(normed, w_query, cosine, sine, *deps)


def head_columns(array, index):
    return array[:, index * HEAD_SIZE : (index + 1) * HEAD_SIZE]


def stack_heads(array, heads):
    return jnp.concatenate([head_columns(array, h) for h in heads], axis=0)


def store_heads(out, turned, first, span, finish):
    for i in range(0, turned.shape[1] // span, 2):
        pair = jnp.concatenate(
            [turned[:, (i + e) * span : (i + e + 1) * span] for e in range(2)], axis=0
        )
        at = (first + i) * HEAD_SIZE
        out[:, at : at + 128] = finish(jnp.transpose(pair)).astype(BF)


def attend_kernel(blocks, chunks, shift, query, place, place_row, begin_row, w_output, *refs):
    packed = refs[:blocks]
    attended, stats, *parts = refs[-2 - chunks :]
    span, width = query.shape
    heads_kv = packed[0].shape[1] // (2 * HEAD_SIZE)
    group = width // HEAD_SIZE // heads_kv
    last = jnp.concatenate([place_row[...]] * group, axis=1)
    first = jnp.concatenate([begin_row[...]] * group, axis=1)
    for g in range(heads_kv):
        q = stack_heads(query, range(g * group, (g + 1) * group))
        top = total = mixed = None
        for j in range(blocks):
            keys = head_columns(packed[j], g)
            values = head_columns(packed[j], heads_kv + g)
            key_place = place[...] + shift[j]
            allowed = (key_place >= first) & (key_place <= last)
            masked = jnp.where(allowed, contract(keys, q, 1, 1), -1e30)
            peak = jnp.max(masked, axis=0, keepdims=True)
            peak = peak if j == 0 else jnp.maximum(top, peak)
            terms = jnp.exp(masked - peak)
            amount = jnp.sum(terms, axis=0, keepdims=True)
            term = contract(values, terms.astype(BF), 0, 0)
            if j == 0:
                total, mixed = amount, term
            else:
                fade = jnp.exp(top - peak)
                total, mixed = total * fade + amount, mixed * fade + term
            top = peak
        stats[g : g + 1, :] = top + jnp.log(total)
        store_heads(attended, mixed * (1.0 / total), g * group, span, lambda v: v)
    part = contract(attended[...], w_output[...], 1, 0)
    chunk = span // len(parts)
    for k, out in enumerate(parts):
        out[...] = part[k * chunk : (k + 1) * chunk].astype(BF)


def attend(shift, query, packed, places, w_output, chunks, deps=()):
    span, width = query.shape
    depth = w_output.shape[1]
    blocks = len(packed)
    heads_kv = packed[0].shape[1] // (2 * HEAD_SIZE)
    args = (
        query,
        *places,
        w_output,
        *packed,
    )
    outs = (
        jax.ShapeDtypeStruct((span, width), BF),
        jax.ShapeDtypeStruct((heads_kv, width // HEAD_SIZE // heads_kv * span), F32),
    )
    outs += (jax.ShapeDtypeStruct((span // chunks, depth), BF),) * chunks
    out = pl.pallas_call(
        functools.partial(attend_kernel, blocks, chunks),
        out_shape=outs,
        grid_spec=pltpu.PrefetchScalarGridSpec(
            num_scalar_prefetch=1,
            grid=(1,),
            in_specs=[whole_spec(a) for a in args] + unread(deps),
            out_specs=tuple(whole_spec(a) for a in outs),
        ),
        compiler_params=kernel_params(1),
        cost_estimate=spent(87),
        name="attend",
    )(shift, *args, *deps)
    return out[0], out[1], list(out[2:])


def sum_chunks(refs):
    total = refs[0][...].astype(F32)
    for ref in refs[1:]:
        total = total + ref[...].astype(F32)
    return total


def middle_kernel(count, me, x, gain, *refs):
    chunks, (middle, inverse, normed) = refs[:count], refs[-3:]
    stream = x[...].astype(F32) + sum_chunks(chunks)
    scale = lax.rsqrt(jnp.mean(stream * stream, axis=1, keepdims=True) + EPSILON)
    middle[...] = stream
    inverse[...] = jnp.broadcast_to(scale, inverse.shape)
    normed[...] = (stream * scale * gain[...]).astype(BF)


def middle_norm(me, x, gain, chunks, deps=()):
    rows, depth = chunks[0].shape
    outs = (
        jax.ShapeDtypeStruct((rows, depth), F32),
        jax.ShapeDtypeStruct((rows, 128), F32),
        jax.ShapeDtypeStruct((rows, depth), BF),
    )
    return pl.pallas_call(
        functools.partial(middle_kernel, len(chunks)),
        out_shape=outs,
        grid_spec=pltpu.PrefetchScalarGridSpec(
            num_scalar_prefetch=1,
            grid=(1,),
            in_specs=[chunk_spec(x, len(chunks), 0)]
            + [whole_spec(a) for a in (gain, *chunks)]
            + unread(deps),
            out_specs=tuple(whole_spec(a) for a in outs),
        ),
        compiler_params=kernel_params(1),
        cost_estimate=SMALL,
        name="middle_norm",
    )(me, x, gain, *chunks, *deps)


def halves_kernel(count, *refs):
    half = count // 2
    refs[-2][...] = join(refs[:half])
    refs[-1][...] = join(refs[half:count])


def join_halves(chunks, deps=()):
    rows, depth = chunks[0].shape
    outs = (jax.ShapeDtypeStruct((rows * len(chunks) // 2, depth), BF),) * 2
    return pl.pallas_call(
        functools.partial(halves_kernel, len(chunks)),
        out_shape=outs,
        grid=(1,),
        in_specs=[whole_spec(a) for a in chunks] + unread(deps),
        out_specs=tuple(whole_spec(a) for a in outs),
        compiler_params=kernel_params(1),
        cost_estimate=SMALL,
        name="join_halves",
    )(*chunks, *deps)


def norm_gradient(grad, rows, scale, gain):
    scaled = grad * gain
    product = jnp.mean(scaled * rows, axis=1, keepdims=True)
    gain_grad = jnp.sum(grad * rows * scale, axis=0, keepdims=True)
    return scale * scaled - rows * (scale * scale * scale * product), gain_grad


def norm_back_kernel(count, upstream, middle, inverse, gain, *refs):
    chunks, (wide, low, gain_grad) = refs[:count], refs[-3:]
    grad, gain_grad[...] = norm_gradient(
        sum_chunks(chunks), middle[...], inverse[:, :1], gain[...]
    )
    total = upstream[...].astype(F32) + grad
    wide[...] = total
    low[...] = total.astype(BF)


def norm_back(upstream, middle, inverse, gain, chunks, deps=()):
    rows, depth = middle.shape
    args = (middle, inverse, gain, *chunks)
    outs = (
        jax.ShapeDtypeStruct((rows, depth), F32),
        jax.ShapeDtypeStruct((rows, depth), BF),
        jax.ShapeDtypeStruct((1, depth), F32),
    )
    return pl.pallas_call(
        functools.partial(norm_back_kernel, len(chunks)),
        out_shape=outs,
        grid=(1,),
        in_specs=[pl.BlockSpec((rows, depth), lambda i: (0, 0))]
        + [whole_spec(a) for a in args]
        + unread(deps),
        out_specs=tuple(whole_spec(a) for a in outs),
        compiler_params=kernel_params(1),
        cost_estimate=SMALL,
        name="norm_back",
    )(upstream, *args, *deps)


def finish_kernel(count, me, x, inverse, gain, grad_middle, *refs):
    grad, _ = norm_gradient(
        sum_chunks(refs[:count]), x[...].astype(F32), inverse[:, :1], gain[...]
    )
    refs[-1][...] = (grad_middle[...] + grad).astype(BF)


def finish(me, x, inverse, gain, grad_middle, chunks, deps=()):
    rows, depth = grad_middle.shape
    args = (gain, grad_middle, *chunks)
    outs = jax.ShapeDtypeStruct((rows, depth), BF)
    return pl.pallas_call(
        functools.partial(finish_kernel, len(chunks)),
        out_shape=outs,
        grid_spec=pltpu.PrefetchScalarGridSpec(
            num_scalar_prefetch=1,
            grid=(1,),
            in_specs=[
                chunk_spec(x, len(chunks), 0),
                pl.BlockSpec((rows, 128), lambda i, c: (0, 0)),
            ]
            + [whole_spec(a) for a in args]
            + unread(deps),
            out_specs=whole_spec(outs),
        ),
        compiler_params=kernel_params(1),
        cost_estimate=SMALL,
        name="finish",
    )(me, x, inverse, *args, *deps)


def add_kernel(count, *refs):
    refs[-1][...] = sum_chunks(refs[:count]).astype(refs[-1].dtype)


def add_up(arrays, dtype, deps=()):
    out = jax.ShapeDtypeStruct(arrays[0].shape, dtype)
    return pl.pallas_call(
        functools.partial(add_kernel, len(arrays)),
        out_shape=out,
        grid=(1,),
        in_specs=[whole_spec(a) for a in arrays] + unread(deps),
        out_specs=whole_spec(out),
        compiler_params=kernel_params(1),
        cost_estimate=SMALL,
        name="add_up",
    )(*arrays, *deps)


def restore_kernel(count, me, *refs):
    step = pl.program_id(0)
    for k in range(count):

        @pl.when(step == k)
        def _():
            refs[-1][...] = refs[k][...]


def restore(me, pieces, cost, deps=()):
    count = len(pieces)
    rows, depth = pieces[0].shape
    if rows % 16:
        return reorder(jnp.concatenate(pieces, axis=0), "tensor")
    return pl.pallas_call(
        functools.partial(restore_kernel, count),
        out_shape=jax.ShapeDtypeStruct((count * rows, depth), BF),
        grid_spec=pltpu.PrefetchScalarGridSpec(
            num_scalar_prefetch=1,
            grid=(count,),
            in_specs=[whole_spec(p) for p in pieces] + unread(deps),
            out_specs=pl.BlockSpec((rows, depth), lambda i, c: (c[0] ^ i, 0)),
        ),
        compiler_params=kernel_params(1),
        cost_estimate=cost,
        name="restore",
    )(me, *pieces, *deps)


def attend_back_kernel(blocks, count, shift, query, attended, stats, place, place_row, begin_row,
                       cosine, sine, w_output, *refs):
    packed = refs[:blocks]
    chunks = refs[blocks : blocks + count]
    grad_query = refs[-1 - blocks]
    terms = refs[-blocks:]
    span, width = query.shape
    heads_kv = packed[0].shape[1] // (2 * HEAD_SIZE)
    group = width // HEAD_SIZE // heads_kv
    grad_middle = join(chunks)
    grad_attended = contract(grad_middle, w_output[...], 1, 1).astype(BF)
    last = jnp.concatenate([place_row[...]] * group, axis=1)
    first = jnp.concatenate([begin_row[...]] * group, axis=1)
    key_terms = [[] for _ in range(blocks)]
    value_terms = [[] for _ in range(blocks)]
    for g in range(heads_kv):
        mine = range(g * group, (g + 1) * group)
        q = stack_heads(query, mine)
        grad = stack_heads(grad_attended, mine)
        norm = stats[g : g + 1, :]
        inner = lax.dot_general(
            jnp.ones((8, HEAD_SIZE), F32),
            grad.astype(F32) * stack_heads(attended, mine).astype(F32),
            (((1,), (1,)), ((), ())),
            preferred_element_type=F32,
            precision=lax.Precision.HIGHEST,
        )[:1]
        total = None
        for j in range(blocks):
            keys = head_columns(packed[j], g)
            values = head_columns(packed[j], heads_kv + g)
            key_place = place[...] + shift[j]
            allowed = (key_place >= first) & (key_place <= last)
            scores = contract(keys, q, 1, 1)
            probs = jnp.exp(jnp.where(allowed, scores - norm, -1e30))
            grad_scores = (probs * (contract(values, grad, 1, 1) - inner)).astype(BF)
            value_terms[j].append(contract(probs.astype(BF), grad, 1, 0))
            key_terms[j].append(contract(grad_scores, q, 1, 0))
            term = contract(keys, grad_scores, 0, 0)
            total = term if total is None else total + term
        store_heads(
            grad_query,
            total,
            g * group,
            span,
            lambda v: rotate_block(v * HEAD_SIZE**-0.5, cosine[...], -sine[...]),
        )
    for j in range(blocks):
        terms[j][...] = jnp.concatenate(key_terms[j] + value_terms[j], axis=1).astype(BF)


def attend_back(shift, query, attended, stats, packed, places, cosine, sine, w_output, chunks,
                deps=()):
    span, width = query.shape
    blocks = len(packed)
    args = (
        query,
        attended,
        stats,
        *places,
        cosine,
        sine,
        w_output,
        *packed,
        *chunks,
    )
    outs = (jax.ShapeDtypeStruct((span, width), BF),)
    outs += (jax.ShapeDtypeStruct(packed[0].shape, BF),) * blocks
    out = pl.pallas_call(
        functools.partial(attend_back_kernel, blocks, len(chunks)),
        out_shape=outs,
        grid_spec=pltpu.PrefetchScalarGridSpec(
            num_scalar_prefetch=1,
            grid=(1,),
            in_specs=[whole_spec(a) for a in args] + unread(deps),
            out_specs=tuple(whole_spec(a) for a in outs),
        ),
        compiler_params=kernel_params(1),
        cost_estimate=SMALL,
        name="attend_back",
    )(shift, *args, *deps)
    return out[0], list(out[1:])


def input_back_kernel(
    count, chunks, me, grad_query, w_query, key_w, value_w, cosine, sine, inverse, *refs
):
    terms, rows = refs[:count], refs[count : count + chunks]
    lin, gain_grad, *parts = refs[-2 - chunks :]
    normed = join(rows).astype(F32) * inverse[:, :1]
    width = key_w.shape[1]
    total = sum_chunks(terms)
    low = pack_rotated(total[:, :width], total[:, width:], cosine[...], -sine[...]).astype(BF)
    lin[...] = low
    part = contract(grad_query[...], w_query[...], 1, 1)
    part = part + contract(low[:, :width], key_w[...], 1, 1)
    part = part + contract(low[:, width:], value_w[...], 1, 1)
    rows = part.shape[0] // chunks
    for k, out in enumerate(parts):
        out[...] = part[k * rows : (k + 1) * rows].astype(BF)
    gain_grad[...] = jnp.sum(part * normed, axis=0, keepdims=True)


def input_back(
    me, grad_query, w_query, key_matrix, value_matrix, cosine, sine, inverse, x, terms, chunks, deps=()
):
    span = grad_query.shape[0]
    depth = w_query.shape[0]
    args = (grad_query, w_query, key_matrix, value_matrix, cosine, sine, inverse, *terms)
    outs = (
        jax.ShapeDtypeStruct(terms[0].shape, BF),
        jax.ShapeDtypeStruct((1, depth), F32),
    )
    outs += (jax.ShapeDtypeStruct((span // chunks, depth), BF),) * chunks
    out = pl.pallas_call(
        functools.partial(input_back_kernel, len(terms), chunks),
        out_shape=outs,
        grid_spec=pltpu.PrefetchScalarGridSpec(
            num_scalar_prefetch=1,
            grid=(1,),
            in_specs=[whole_spec(a) for a in args]
            + [chunk_spec(x, chunks, k) for k in range(chunks)]
            + unread(deps),
            out_specs=tuple(whole_spec(a) for a in outs),
        ),
        compiler_params=kernel_params(1),
        cost_estimate=SMALL,
        name="input_back",
    )(me, *args, *[x] * chunks, *deps)
    return out[0], out[1], list(out[2:])


def rope_tables(positions):
    expo = np.arange(HEAD_SIZE // 2, dtype=np.float64) * 2.0 / HEAD_SIZE
    inverse = 1.0 / 500000.0**expo
    wavelength = 2.0 * np.pi / inverse
    smooth = (8192.0 / wavelength - 1.0) / 3.0
    middle = (1.0 - smooth) * inverse / 32.0 + smooth * inverse
    scaled = np.where(
        wavelength < 2048.0, inverse, np.where(wavelength > 8192.0, inverse / 32.0, middle)
    )
    scaled = jnp.asarray(np.tile(scaled, 4)[None, :].astype(np.float32))
    sign = jnp.asarray(np.tile(np.repeat([-1.0, 1.0], HEAD_SIZE // 2), 2)[None, :].astype(np.float32))
    angles = positions.astype(F32)[:, None] * scaled
    return jnp.cos(angles), jnp.sin(angles) * sign


def flip(value, axis, mask):
    return lax.ppermute(value, axis, [(i, i ^ mask) for i in range(lax.axis_size(axis))])


def reorder(value, axis):
    n = lax.axis_size(axis)
    me = lax.axis_index(axis)
    chunk = value.shape[0] // n
    return jnp.concatenate(
        [lax.dynamic_slice_in_dim(value, (me ^ k) * chunk, chunk, 0) for k in range(n)], axis=0
    )


def exchange(chunks, axis):
    return chunks[:1] + [flip(chunks[k], axis, k) for k in reversed(range(1, len(chunks)))]


def spread(chunk, axis):
    return [chunk] + [flip(chunk, axis, k) for k in range(1, lax.axis_size(axis))]


def gather_halves(first, second):
    return [
        lax.all_gather(first, ("rows", "seq"), axis=0, tiled=True),
        lax.all_gather(second, ("seq", "rows"), axis=0, tiled=True),
    ]


def per_device(
    activations,
    doc_lengths,
    w_query,
    key_matrix,
    value_matrix,
    w_output,
    w_gate,
    w_up,
    w_down,
    gain_attn,
    gain_ffn,
    cotangent,
):
    span = activations.shape[1]
    blocks = lax.axis_size("seq")
    chunks = lax.axis_size("tensor")
    chunk = span // chunks
    core = lax.axis_index("rows").astype(jnp.int32).reshape(1)
    block_here = lax.axis_index("seq")
    gain_attn = gain_attn.reshape(1, -1)
    gain_ffn = gain_ffn.reshape(1, -1)
    stream, cotangent = activations[0], cotangent[0]
    me = lax.axis_index("tensor").astype(jnp.int32)
    token = jnp.arange(span, dtype=jnp.int32)
    place = block_here * span + (me ^ (token // chunk)) * chunk + token % chunk
    if chunk % 16:
        stream, cotangent = reorder(stream, "tensor"), reorder(cotangent, "tensor")
        me = jnp.zeros_like(me)
    ends = [doc_lengths[0, 0]]
    for d in range(1, DOCS):
        ends.append(ends[-1] + doc_lengths[0, d])
    begin = jnp.zeros_like(place)
    for end in ends:
        begin = jnp.where(place >= end, end, begin)
    cosine, sine = rope_tables(place - begin)
    shift = jnp.stack([((block_here ^ j) - block_here) * span for j in range(blocks)])
    shift = shift.astype(jnp.int32)
    scalars = jnp.stack([me, ends[-1].astype(jnp.int32)])
    places = (place.reshape(span, 1), place.reshape(1, span), begin.reshape(1, span))

    normed_one, inverse_one, packed = project_kv(
        scalars, stream, gain_attn, key_matrix, value_matrix, cosine, sine, chunks, (shift, *places)
    )
    packed = spread(packed, "seq")
    query = project_query(normed_one, w_query, cosine, sine)
    attended, stats, parts = attend(shift, query, packed, places, w_output, chunks)

    upstream, *upstream_halves = mask_padding(scalars, cotangent, places[0], chunks, (parts[0],))
    upstream_all = gather_halves(*upstream_halves)
    sent = exchange(parts, "tensor")
    grad_hidden = grad_hidden_of(core, upstream, w_down, 1, (parts[0],))
    middle, inverse_two, normed = middle_norm(scalars, stream, gain_ffn, sent, (grad_hidden,))

    grad_hidden_first = grad_hidden_of(core, upstream_all[0], w_down, 2, (middle,))
    normed = join_halves(spread(normed, "tensor"), (grad_hidden_first,))
    normed_all = gather_halves(*normed)
    hidden, parts = feed_own(normed, w_gate, w_up, grad_hidden, chunks)

    sent = exchange(parts, "tensor")
    grad_hidden_second = grad_hidden_of(core, upstream_all[1], w_down, 2, (parts[0],))
    grad_middle, grad_middle_low, gain_two = norm_back(
        upstream, middle, inverse_two, gain_ffn, sent, (grad_hidden_second,)
    )
    grad_middle_all = spread(grad_middle_low, "tensor")
    feed_first = feed_half(
        core, normed_all[0], w_gate, w_up, grad_hidden_first, (grad_middle,)
    )
    down_parts = down_projection(hidden, w_down, chunks, (feed_first[0],))
    grad_query, kv_terms = attend_back(
        shift,
        query,
        attended,
        stats,
        packed,
        places,
        cosine,
        sine,
        w_output,
        grad_middle_all,
        (down_parts[0],),
    )
    block_sent = exchange(down_parts, "tensor")

    kv_sent = exchange(kv_terms, "seq")
    wo_part = left_product(attended, grad_middle_all, (grad_query,))
    wq_part = left_product(normed_one, [grad_query], (wo_part,))
    grad_kv, gain_one, parts = input_back(
        scalars,
        grad_query,
        w_query,
        key_matrix,
        value_matrix,
        cosine,
        sine,
        inverse_one,
        stream,
        kv_sent,
        chunks,
        (wq_part, normed_all[1]),
    )

    sent = exchange(parts, "tensor")
    wkv_part = kv_product(normed_one, grad_kv, gain_one, gain_two, (parts[0],))
    grad_wo, grad_wq, grad_wkv = lax.psum((wo_part, wq_part, wkv_part), ("rows", "seq"))
    feed_second = feed_half(
        core, normed_all[1], w_gate, w_up, grad_hidden_second, (wkv_part,)
    )
    block_chunk = add_up([middle, *block_sent], BF, (feed_second[0],))
    block_all = spread(block_chunk, "tensor")
    hidden_all, grad_gate_all, grad_up_all = zip(feed_first, feed_second)
    grad_down, low = weight_grad(core, hidden_all, upstream_all, 0, (block_chunk,))
    down_other = [flip(v, "rows", 1) for v in low]
    grad_input = finish(
        scalars, stream, inverse_one, gain_attn, grad_middle, sent, (grad_down,)
    )
    grad_input_all = spread(grad_input, "tensor")
    grad_gate_w, low = weight_grad(core, normed_all, grad_gate_all, 1, (grad_input,))
    gate_other = [flip(v, "rows", 1) for v in low]
    block_output = restore(scalars, block_all, SMALL, (grad_gate_w,))
    grad_up_w, low = weight_grad(core, normed_all, grad_up_all, 1, (block_output,))
    up_other = [flip(v, "rows", 1) for v in low]
    grad_input = restore(scalars, grad_input_all, spent(25), (grad_up_w,))
    width_kv = key_matrix.shape[1]
    gains_sent = spread(gain_rows(grad_wkv), "tensor")
    grad_down = fill_other(core, down_other, grad_down, 0, (grad_input,))
    grad_gate_w = fill_other(core, gate_other, grad_gate_w, 1, (grad_down,))
    gains = add_up(gains_sent, F32, (grad_gate_w,))
    grad_up_w = fill_other(core, up_other, grad_up_w, 1, (gains,))
    return (
        block_output[None],
        grad_input[None],
        grad_wq.astype(F32),
        grad_wkv[:, :width_kv].astype(F32),
        grad_wkv[:, width_kv : 2 * width_kv].astype(F32),
        grad_wo.astype(F32),
        grad_gate_w,
        grad_up_w,
        grad_down,
        gains[0],
        gains[1],
    )


def solution(mesh):
    placed = (
        P("rows", "seq", None),
        P("rows", None),
        P(None, "tensor"),
        P(None, "tensor"),
        P(None, "tensor"),
        P("tensor", None),
        P(None, "tensor"),
        P(None, "tensor"),
        P("tensor", None),
        P(),
        P(),
        P("rows", "seq", None),
    )
    return jax.shard_map(
        per_device,
        mesh=mesh,
        in_specs=placed,
        out_specs=(
            P("rows", "seq", None),
            P("rows", "seq", None),
            P(None, "tensor"),
            P(None, "tensor"),
            P(None, "tensor"),
            P("tensor", None),
            P(None, "tensor"),
            P(None, "tensor"),
            P("tensor", None),
            P(),
            P(),
        ),
        check_vma=False,
    )
```

time: 549 us -> 424 us (0.77)
  waiting for transfers between devices: 185 us -> 72.3 us
  Pallas kernels: 148 us -> 246 us
  matrix products: 69.9 us -> 0 us
  other arithmetic: 54.6 us -> 13.7 us
  local copies, waits for them, and re-layouts: 17.8 us -> 9.8 us
  starting transfers between devices: 51.2 us -> 57.1 us
    pallas_call x3 -> x23, Pallas kernels: 38.5 us -> 134 us  [the longest x3 27.1 us: grad_hidden_of(): pl.pallas_call(times_transposed_kernel, out_shape=jax.ShapeDtypeStruct((t...]
    ppermute x38 -> x45, waiting for transfers between devices: 128 us -> 43.8 us  [flip(): lax.ppermute(value, axis, [(i, i ^ mask) for i in range(lax.axis_size(axi...]
    dot_general x17 -> x0, matrix products: 61.1 us -> none  [the longest x5 14 us: dot_right(): return jnp.einsum('cf,df->cd', a, b, preferred_element_type=F32)]
    psum x2 -> x1, waiting for transfers between devices: 56.5 us -> 19.5 us  [per_device(): lax.psum((wo_part, wq_part, wkv_part), ('rows', 'seq'))]
    convert_element_type x15 -> x3, other arithmetic: 25.1 us -> 5.92 us  [the longest x1 2.65 us: per_device(): grad_wkv[:, width_kv:2 * width_kv].astype(F32)]
    sub x1 -> x0, matrix products: 8.85 us -> none  [per_device(): weights = jnp.exp(masked - top)]
    add x12 -> x1, other arithmetic: 9.05 us -> 0.76 us  [per_device(): place = block_here * span + (me ^ token // chunk) * chunk + token % chunk]
    slice x15 -> x1, local copies, waits for them, and re-layouts: 9.26 us -> 1.4 us  [per_device(): ends.append(ends[-1] + doc_lengths[0, d])]
  transfers between devices with their start and end apart: 44 -> 50, of which waited for: 20 -> 10; matrix products, arithmetic and copies ran while one was open for 23% -> 2% of each run, Pallas kernels for 19% -> 53%
where the time goes in v2:
time: 424 us; the launch traced here: 416 us
  Pallas kernels  246 us (58%)
  waiting for transfers between devices  72.3 us (17%)
  starting transfers between devices  57.1 us (13%)
  between operations  16.9 us (4%)
  other arithmetic  13.7 us (3%)
  local copies, waits for them, and re-layouts  9.8 us (2%)
    pallas_call x3, Pallas kernels, weight_grad(): pl.pallas_call(functools.partial(weight_grad_kernel, count), out_shape=(j...  58.8 us
    ppermute x45, starting transfers between devices, flip(): lax.ppermute(value, axis, [(i, i ^ mask) for i in range(lax.axis_size(axi...  56.7 us
    ppermute x45, waiting for transfers between devices, flip(): lax.ppermute(value, axis, [(i, i ^ mask) for i in range(lax.axis_size(axi...  43.8 us
    pallas_call x2, Pallas kernels, feed_half(): pl.pallas_call(feed_half_kernel, out_shape=(out, out, out), grid_spec=plt...  36.3 us
    pallas_call x3, Pallas kernels, grad_hidden_of(): pl.pallas_call(times_transposed_kernel, out_shape=jax.ShapeDtypeStruct((t...  27.1 us
    psum x1, waiting for transfers between devices, per_device(): lax.psum((wo_part, wq_part, wkv_part), ('rows', 'seq'))  19.5 us
    pallas_call x1, Pallas kernels, feed_own(): pl.pallas_call(functools.partial(feed_own_kernel, len(normed), chunks), o...  18.7 us
    pallas_call x3, Pallas kernels, fill_other(): pl.pallas_call(fill_other_kernel, out_shape=jax.ShapeDtypeStruct(held.sha...  17.4 us
  transfers between devices with their start and end apart: 50, of which 10 were waited for; matrix products, arithmetic and copies ran while one was open for 2% of the time, Pallas kernels for 53%

profile of v2, /device:TPU:0, one launch (start us, length us, event | category | flops | bytes accessed | tf_op | source)
XLA Modules:
  0.0 416.1 jit_solution(12374460657787127538)
XLA Ops:
  17.1 4.2 %project_kv.1 = (bf16[320,2048]{1,0:T(8,128)(2,1)}, f32[320,128]{1,0:T(8,128)}, bf16[320,256]{1,0:T(8,128)(2,1)}) custom-call(s32[2]{0:T(128)} %pad_add_fusion.me.scalars, bf16[320,2048]{1,0:T(8,128)(2,1)} %bitcast.18, bf16[320,2048]{1,0:T(8,128)(2,1)} %bitcast.19, bf16[320,2048]{1,0:T(8,128)(2,1)} %bitcast.20, bf16[320,2048]{1,0:T(8,128)(2,1)} %bitcast.21, ...), custom_call_target="tpu_custom_call" | custom-call | flops 1 | bytes 1 | tf_op jit(solution)/shard_map/project_kv/pallas_call | solution.py:451
  21.4 2.9 collective-permute-start
  25.8 3.7 project_query.1.query
  29.5 4.1 collective-permute-done.1.refs_2_
  35.0 10.7 %attend.1 = (bf16[320,512]{1,0:T(8,128)(2,1)}, f32[2,1280]{1,0:T(2,128)}, bf16[80,2048]{1,0:T(8,128)(2,1)}, bf16[80,2048]{1,0:T(8,128)(2,1)}, bf16[80,2048]{1,0:T(8,128)(2,1)}, /*index=5*/bf16[80,2048]{1,0:T(8,128)(2,1)}) custom-call(s32[4]{0:T(128)} %pad_add_fusion.1.refs_9_.shift, bf16[320,512]{1,0:T(8,128)(2,1)} %project_query.1.query, ...), custom_call_target="tpu_custom_call" | custom-call | flops 86999998464 | bytes 1 | tf_op jit(solution)/shard_map/attend/pallas_call | solution.py:567
  45.7 3.7 mask_padding.1
  50.4 3.7 collective-permute-start.3
  54.9 7.3 %grad_hidden_of.3.refs_4_.grad_hidden = bf16[320,2048]{1,0:T(8,128)(2,1)} custom-call(s32[1]{0:T(128)} %bitcast.12.core, bf16[320,2048]{1,0:T(8,128)(2,1)} %get-tuple-element.78.left.upstream, bf16[2048,2048]{1,0:T(8,128)(2,1)} %weight.9, bf16[80,2048]{1,0:T(8,128)(2,1)} %get-tuple-element.74.refs_4_.refs_0_), custom_call_target="tpu_custom_call" | custom-call | flops 1 | bytes 1 | tf_op jit(solution)/shard_map/grad_hidden_of/pallas_call | solution.py:71
  63.2 17.3 %collective-permute-done.4.refs_2_ = bf16[80,2048]{1,0:T(8,128)(2,1)S(1)} collective-permute-done((bf16[80,2048]{1,0:T(8,128)(2,1)}, bf16[80,2048]{1,0:T(8,128)(2,1)S(1)}, u32[]{:S(2)}, u32[]{:S(2)}) %collective-permute-start.4) | collective-permute-done | bytes 327712 | tf_op jit(solution)/shard_map/ppermute | solution.py:909
  81.4 3.2 middle_norm.1
  84.6 3.0 collective-permute-start.7
  91.0 9.9 %grad_hidden_of.4.refs_4_.grad_hidden = bf16[1280,1024]{1,0:T(8,128)(2,1)} custom-call(s32[1]{0:T(128)} %bitcast.12.core, bf16[1280,2048]{1,0:T(8,128)(2,1)} %all-gather.5.cloned.1.call-done.left.refs_2_, bf16[2048,2048]{1,0:T(8,128)(2,1)} %weight.9, f32[80,2048]{1,0:T(8,128)} %get-tuple-element.79.refs_0_.middle), custom_call_target="tpu_custom_call" | custom-call | flops 1 | bytes 1 | tf_op jit(solution)/shard_map/grad_hidden_of/pallas_call | solution.py:71
  100.9 9.7 %collective-permute-done.7.refs_2_ = bf16[80,2048]{1,0:T(8,128)(2,1)S(1)} collective-permute-done((bf16[80,2048]{1,0:T(8,128)(2,1)}, bf16[80,2048]{1,0:T(8,128)(2,1)S(1)}, u32[]{:S(2)}, u32[]{:S(2)}) %collective-permute-start.7) | collective-permute-done | bytes 327712 | tf_op jit(solution)/shard_map/ppermute | solution.py:909
  115.0 18.7 %feed_own.1 = (bf16[320,2048]{1,0:T(8,128)(2,1)}, bf16[80,2048]{1,0:T(8,128)(2,1)}, bf16[80,2048]{1,0:T(8,128)(2,1)}, bf16[80,2048]{1,0:T(8,128)(2,1)}, bf16[80,2048]{1,0:T(8,128)(2,1)}) custom-call(bf16[2048,2048]{1,0:T(8,128)(2,1)} %gate_w.5, bf16[2048,2048]{1,0:T(8,128)(2,1)} %up_w.5, bf16[320,2048]{1,0:T(8,128)(2,1)} %grad_hidden_of.3.refs_4_.grad_hidden, ...), custom_call_target="tpu_custom_call" | custom-call | flops 1 | bytes 1 | tf_op jit(solution)/shard_map/feed_own/pallas_call | solution.py:180
  133.7 4.0 collective-permute-start.10
  140.1 9.9 %grad_hidden_of.5.refs_4_.grad_hidden = bf16[1280,1024]{1,0:T(8,128)(2,1)} custom-call(s32[1]{0:T(128)} %bitcast.12.core, bf16[1280,2048]{1,0:T(8,128)(2,1)} %all-gather.9.cloned.1.call-done.left.refs_3_, bf16[2048,2048]{1,0:T(8,128)(2,1)} %weight.9, bf16[80,2048]{1,0:T(8,128)(2,1)} %get-tuple-element.86.refs_0_), custom_call_target="tpu_custom_call" | custom-call | flops 1 | bytes 1 | tf_op jit(solution)/shard_map/grad_hidden_of/pallas_call | solution.py:71
  149.9 5.4 %collective-permute-done.10.refs_2_ = bf16[80,2048]{1,0:T(8,128)(2,1)S(1)} collective-permute-done((bf16[80,2048]{1,0:T(8,128)(2,1)}, bf16[80,2048]{1,0:T(8,128)(2,1)S(1)}, u32[]{:S(2)}, u32[]{:S(2)}) %collective-permute-start.10) | collective-permute-done | bytes 327712 | tf_op jit(solution)/shard_map/ppermute | solution.py:909
  155.3 5.7 %collective-permute-done.9.refs_1_ = bf16[80,2048]{1,0:T(8,128)(2,1)S(1)} collective-permute-done((bf16[80,2048]{1,0:T(8,128)(2,1)}, bf16[80,2048]{1,0:T(8,128)(2,1)S(1)}, u32[]{:S(2)}, u32[]{:S(2)}) %collective-permute-start.9) | collective-permute-done | bytes 327712 | tf_op jit(solution)/shard_map/ppermute | solution.py:909
  161.7 3.0 norm_back.1
  164.7 4.6 %collective-permute-start.15 = (bf16[80,2048]{1,0:T(8,128)(2,1)}, bf16[80,2048]{1,0:T(8,128)(2,1)S(1)}, u32[]{:S(2)}, u32[]{:S(2)}) collective-permute-start(bf16[80,2048]{1,0:T(8,128)(2,1)} %get-tuple-element.99.refs_4_.refs_0_), channel_id=1, source_target_pairs={{0,1},{1,0},{2,3},{3,2},{4,5},{5,4},{6,7},{7,6},{8,9},{9,8},{10,11... | collective-permute-start | bytes 983048 | tf_op jit(solution)/shard_map/ppermute | solution.py:909
  172.5 5.7 %all-gather.7.cloned.1.call-done.normed.refs_0_ = bf16[1280,2048]{1,0:T(8,128)(2,1)} async-done(((bf16[160,2048]{1,0:T(8,128)(2,1)}), bf16[1280,2048]{1,0:T(8,128)(2,1)}) %all-gather.7.cloned.1.call-update) | async-done | bytes 5242896 | tf_op jit(solution)/shard_map/all_gather | solution.py:931
  178.2 18.7 %feed_half.2 = (bf16[1280,1024]{1,0:T(8,128)(2,1)}, bf16[1280,1024]{1,0:T(8,128)(2,1)}, bf16[1280,1024]{1,0:T(8,128)(2,1)}) custom-call(s32[1]{0:T(128)} %bitcast.12.core, bf16[1280,2048]{1,0:T(8,128)(2,1)} %all-gather.7.cloned.1.call-done.normed.refs_0_, bf16[2048,2048]{1,0:T(8,128)(2,1)} %gate_w.5, bf16[2048,2048]{1,0:T(8,128)(2,1)} %up_w.5, ...), custom_call_target="tpu_custom_call" | custom-call | flops 1 | bytes 1 | tf_op jit(solution)/shard_map/feed_half/pallas_call | solution.py:117
  197.0 7.4 %down_projection.1 = (bf16[80,2048]{1,0:T(8,128)(2,1)}, bf16[80,2048]{1,0:T(8,128)(2,1)}, bf16[80,2048]{1,0:T(8,128)(2,1)}, bf16[80,2048]{1,0:T(8,128)(2,1)}) custom-call(bf16[320,2048]{1,0:T(8,128)(2,1)} %get-tuple-element.84.hidden, bf16[2048,2048]{1,0:T(8,128)(2,1)} %weight.9, bf16[1280,1024]{1,0:T(8,128)(2,1)} %get-tuple-element.92.refs_0_), custom_call_target="tpu_custom_call" | custom-call | flops 1 | bytes 1 | tf_op jit(solution)/shard_map/down_projection/pallas_call | solution.py:208
  205.3 15.4 %attend_back.1 = (bf16[320,512]{1,0:T(8,128)(2,1)}, bf16[320,256]{1,0:T(8,128)(2,1)}, bf16[320,256]{1,0:T(8,128)(2,1)}, bf16[320,256]{1,0:T(8,128)(2,1)}, bf16[320,256]{1,0:T(8,128)(2,1)}) custom-call(s32[4]{0:T(128)} %pad_add_fusion.1.refs_9_.shift, bf16[320,512]{1,0:T(8,128)(2,1)} %project_query.1.query, bf16[320,512]{1,0:T(8,128)(2,1)} %get-tuple-element.97.attended.left, ...), custom_call_target="tpu_custom_call" | custom-call | flops 1 | bytes 1 | tf_op jit(solution)/shard_map/attend_back/pallas_call | solution.py:829
  221.1 3.3 collective-permute-start.12
  229.6 4.9 %left_product.2.refs_1_ = bf16[512,2048]{1,0:T(8,128)(2,1)} custom-call(bf16[320,512]{1,0:T(8,128)(2,1)} %get-tuple-element.97.attended.left, bf16[80,2048]{1,0:T(8,128)(2,1)} %get-tuple-element.99.refs_4_.refs_0_, bf16[80,2048]{1,0:T(8,128)(2,1)} %copy-done.3, bf16[80,2048]{1,0:T(8,128)(2,1)} %copy-done.4, bf16[80,2048]{1,0:T(8,128)(2,1)} %copy-done.5, ...), custom_call_target="tpu_custom_call" | custom-call | flops 1 | bytes 1 | tf_op jit(solution)/shard_map/left_product/pallas_call | solution.py:280
  234.5 3.8 left_product.3.refs_8_
  238.4 6.0 %input_back.1 = (bf16[320,256]{1,0:T(8,128)(2,1)}, f32[1,2048]{1,0:T(1,128)}, bf16[80,2048]{1,0:T(8,128)(2,1)}, bf16[80,2048]{1,0:T(8,128)(2,1)}, bf16[80,2048]{1,0:T(8,128)(2,1)}, /*index=5*/bf16[80,2048]{1,0:T(8,128)(2,1)}) custom-call(s32[2]{0:T(128)} %pad_add_fusion.me.scalars, bf16[320,512]{1,0:T(8,128)(2,1)} %get-tuple-element.100.refs_4_.refs_0_.grad_query, ...), custom_call_target="tpu_custom_call" | custom-call | flops 1 | bytes 1 | tf_op jit(solution)/shard_map/input_back/pallas_call | solution.py:875
  244.4 3.4 collective-permute-start.24
  248.8 3.3 kv_product.1.refs_0_
  252.1 17.6 %feed_half.3 = (bf16[1280,1024]{1,0:T(8,128)(2,1)}, bf16[1280,1024]{1,0:T(8,128)(2,1)}, bf16[1280,1024]{1,0:T(8,128)(2,1)}) custom-call(s32[1]{0:T(128)} %bitcast.12.core, bf16[1280,2048]{1,0:T(8,128)(2,1)} %all-gather.11.cloned.1.call-done.refs_9_.normed.refs_1_, bf16[2048,2048]{1,0:T(8,128)(2,1)} %gate_w.5, bf16[2048,2048]{1,0:T(8,128)(2,1)} %up_w.5, ...), custom_call_target="tpu_custom_call" | custom-call | flops 1 | bytes 1 | tf_op jit(solution)/shard_map/feed_half/pallas_call | solution.py:117
  270.6 2.4 add_up.2.refs_4_.refs_0_
  274.0 2.9 collective-permute-start.22
  277.4 22.0 %weight_grad.3 = (f32[2048,2048]{1,0:T(8,128)}, bf16[256,2048]{1,0:T(8,128)(2,1)}, bf16[256,2048]{1,0:T(8,128)(2,1)}, bf16[256,2048]{1,0:T(8,128)(2,1)}, bf16[256,2048]{1,0:T(8,128)(2,1)}) custom-call(s32[1]{0:T(128)} %bitcast.12.core, bf16[1280,1024]{1,0:T(8,128)(2,1)} %get-tuple-element.92.refs_0_, bf16[1280,1024]{1,0:T(8,128)(2,1)} %get-tuple-element.110.refs_5_.refs_1_, ...), custom_call_target="tpu_custom_call" | custom-call | flops 1 | bytes 1 | tf_op jit(solution)/shard_map/weight_grad/pallas_call | solution.py:252
  299.4 3.4 finish.1.refs_4_.refs_0_
  302.9 3.9 collective-permute-start.28
  307.3 18.2 %weight_grad.4 = (f32[2048,2048]{1,0:T(8,128)}, bf16[512,1024]{1,0:T(8,128)(2,1)}, bf16[512,1024]{1,0:T(8,128)(2,1)}, bf16[512,1024]{1,0:T(8,128)(2,1)}, bf16[512,1024]{1,0:T(8,128)(2,1)}) custom-call(s32[1]{0:T(128)} %bitcast.12.core, bf16[1280,2048]{1,0:T(8,128)(2,1)} %all-gather.7.cloned.1.call-done.normed.refs_0_, ...), custom_call_target="tpu_custom_call" | custom-call | flops 1 | bytes 1 | tf_op jit(solution)/shard_map/weight_grad/pallas_call | solution.py:252
  326.2 3.6 restore.2.refs_4_
  329.9 18.6 %weight_grad.5 = (f32[2048,2048]{1,0:T(8,128)}, bf16[512,1024]{1,0:T(8,128)(2,1)}, bf16[512,1024]{1,0:T(8,128)(2,1)}, bf16[512,1024]{1,0:T(8,128)(2,1)}, bf16[512,1024]{1,0:T(8,128)(2,1)}) custom-call(s32[1]{0:T(128)} %bitcast.12.core, bf16[1280,2048]{1,0:T(8,128)(2,1)} %all-gather.7.cloned.1.call-done.normed.refs_0_, ...), custom_call_target="tpu_custom_call" | custom-call | flops 1 | bytes 1 | tf_op jit(solution)/shard_map/weight_grad/pallas_call | solution.py:252
  349.2 3.6 restore.3.refs_5_
  352.7 19.5 %all-reduce.3.cloned.1.call-done = (bf16[2048,512]{1,0:T(8,128)(2,1)}, bf16[2048,384]{1,0:T(8,128)(2,1)}, bf16[512,2048]{1,0:T(8,128)(2,1)}) async-done(((bf16[2048,512]{1,0:T(8,128)(2,1)}, bf16[2048,384]{1,0:T(8,128)(2,1)}, bf16[512,2048]{1,0:T(8,128)(2,1)}), (bf16[2048,512]{1,0:T(8,128)(2,1)}, bf16[2048,384]{1,0:T(8,128)(2,1)}, bf16[512,2048]{1,0:T(8,128)(2,1)})) %all-reduce.3.cloned.1.call-update) | async-done | bytes 5767184 | tf_op jit(solution)/shard_map/psum | solution.py:1040
  376.1 5.8 %fill_other.3.refs_5_ = f32[2048,2048]{1,0:T(8,128)} custom-call(s32[1]{0:T(128)} %bitcast.12.core, bf16[256,2048]{1,0:T(8,128)(2,1)} %collective-permute-done.34.refs_0_, bf16[256,2048]{1,0:T(8,128)(2,1)} %collective-permute-done.35.refs_1_, bf16[256,2048]{1,0:T(8,128)(2,1)} %collective-permute-done.36.refs_2_, ...), custom_call_target="tpu_custom_call", output_to_operand_aliasing={{}: (5, {})} | custom-call | flops 49999998976 | bytes 1 | tf_op jit(solution)/shard_map/fill_other/pallas_call | solution.py:384
  383.0 2.5 collective-permute-start.43
  385.4 5.8 %fill_other.4.refs_4_ = f32[2048,2048]{1,0:T(8,128)} custom-call(s32[1]{0:T(128)} %bitcast.12.core, bf16[512,1024]{1,0:T(8,128)(2,1)} %collective-permute-done.30.refs_0_, bf16[512,1024]{1,0:T(8,128)(2,1)} %collective-permute-done.31.refs_1_, bf16[512,1024]{1,0:T(8,128)(2,1)} %collective-permute-done.32.refs_2_, ...), custom_call_target="tpu_custom_call", output_to_operand_aliasing={{}: (5, {})} | custom-call | flops 49999998976 | bytes 1 | tf_op jit(solution)/shard_map/fill_other/pallas_call | solution.py:384
  392.0 2.7 slice_convert_fusion
  394.7 2.6 convert_element_type.20
  397.3 2.5 convert_element_type.23
  403.6 5.8 %fill_other.5 = f32[2048,2048]{1,0:T(8,128)} custom-call(s32[1]{0:T(128)} %bitcast.12.core, bf16[512,1024]{1,0:T(8,128)(2,1)} %collective-permute-done.38.refs_0_, bf16[512,1024]{1,0:T(8,128)(2,1)} %collective-permute-done.39.refs_1_, bf16[512,1024]{1,0:T(8,128)(2,1)} %collective-permute-done.40.refs_2_, ...), custom_call_target="tpu_custom_call", output_to_operand_aliasing={{}: (5, {})} | custom-call | flops 49999998976 | bytes 1 | tf_op jit(solution)/shard_map/fill_other/pallas_call | solution.py:384
  (153 shorter events, 49.3 us)
Async XLA Ops:
  7.2 83.8 %all-gather.5.cloned.1.call-start = ((), (), s32[]{:S(2)}) async-start(), calls=%async_computation | async-start | bytes 5898240 | tf_op jit(solution)/shard_map/all_gather | solution.py:931
  21.4 8.2 %collective-permute-start = (bf16[320,256]{1,0:T(8,128)(2,1)}, bf16[320,256]{1,0:T(8,128)(2,1)S(1)}, u32[]{:S(2)}, u32[]{:S(2)}) collective-permute-start(bf16[320,256]{1,0:T(8,128)(2,1)} %get-tuple-element.73.refs_0_), channel_id=1, source_target_pairs={{0,4},{4,0},{8,12},{12,8},{1,5},{5,1},{9,13},{13,9},{2,6},{6,2},{1... | collective-permute-start | bytes 491528 | tf_op jit(solution)/shard_map/ppermute | solution.py:909
  24.3 9.4 %collective-permute-start.1 = (bf16[320,256]{1,0:T(8,128)(2,1)}, bf16[320,256]{1,0:T(8,128)(2,1)S(1)}, u32[]{:S(2)}, u32[]{:S(2)}) collective-permute-start(bf16[320,256]{1,0:T(8,128)(2,1)} %get-tuple-element.73.refs_0_), channel_id=1, source_target_pairs={{0,8},{4,12},{8,0},{12,4},{1,9},{5,13},{9,1},{13,5},{2,10},{6,14},... | collective-permute-start | bytes 491528 | tf_op jit(solution)/shard_map/ppermute | solution.py:909
  49.4 90.6 %all-gather.9.cloned.1.call-start = ((), (), s32[]{:S(2)}) async-start(), calls=%async_computation.2 | async-start | bytes 5898240 | tf_op jit(solution)/shard_map/all_gather | solution.py:932
  50.2 128.1 %all-gather.7.cloned.1.call-start = ((), (), s32[]{:S(2)}) async-start(), calls=%async_computation.1 | async-start | bytes 5898240 | tf_op jit(solution)/shard_map/all_gather | solution.py:931
  50.4 12.8 %collective-permute-start.3 = (bf16[80,2048]{1,0:T(8,128)(2,1)}, bf16[80,2048]{1,0:T(8,128)(2,1)S(1)}, u32[]{:S(2)}, u32[]{:S(2)}) collective-permute-start(bf16[80,2048]{1,0:T(8,128)(2,1)} %get-tuple-element.75), channel_id=1, source_target_pairs={{0,3},{1,2},{2,1},{3,0},{4,7},{5,6},{6,5},{7,4},{8,11},{9,10},{10,... | collective-permute-start | bytes 983048 | tf_op jit(solution)/shard_map/ppermute | solution.py:909
  54.1 26.5 %collective-permute-start.4 = (bf16[80,2048]{1,0:T(8,128)(2,1)}, bf16[80,2048]{1,0:T(8,128)(2,1)S(1)}, u32[]{:S(2)}, u32[]{:S(2)}) collective-permute-start(bf16[80,2048]{1,0:T(8,128)(2,1)} %get-tuple-element.76), channel_id=1, source_target_pairs={{0,2},{1,3},{2,0},{3,1},{4,6},{5,7},{6,4},{7,5},{8,10},{9,11},{10,... | collective-permute-start | bytes 983048 | tf_op jit(solution)/shard_map/ppermute | solution.py:909
  54.1 26.5 %collective-permute-start.5 = (bf16[80,2048]{1,0:T(8,128)(2,1)}, bf16[80,2048]{1,0:T(8,128)(2,1)S(1)}, u32[]{:S(2)}, u32[]{:S(2)}) collective-permute-start(bf16[80,2048]{1,0:T(8,128)(2,1)} %get-tuple-element.77), channel_id=1, source_target_pairs={{0,1},{1,0},{2,3},{3,2},{4,5},{5,4},{6,7},{7,6},{8,9},{9,8},{10,11... | collective-permute-start | bytes 983048 | tf_op jit(solution)/shard_map/ppermute | solution.py:909
  84.6 16.3 %collective-permute-start.6 = (bf16[80,2048]{1,0:T(8,128)(2,1)}, bf16[80,2048]{1,0:T(8,128)(2,1)S(1)}, u32[]{:S(2)}, u32[]{:S(2)}) collective-permute-start(bf16[80,2048]{1,0:T(8,128)(2,1)} %get-tuple-element.80.refs_0_), channel_id=1, source_target_pairs={{0,1},{1,0},{2,3},{3,2},{4,5},{5,4},{6,7},{7,6},{8,9},{9,8},{10,11... | collective-permute-start | bytes 983048 | tf_op jit(solution)/shard_map/ppermute | solution.py:909
  84.6 26.0 %collective-permute-start.7 = (bf16[80,2048]{1,0:T(8,128)(2,1)}, bf16[80,2048]{1,0:T(8,128)(2,1)S(1)}, u32[]{:S(2)}, u32[]{:S(2)}) collective-permute-start(bf16[80,2048]{1,0:T(8,128)(2,1)} %get-tuple-element.80.refs_0_), channel_id=1, source_target_pairs={{0,2},{1,3},{2,0},{3,1},{4,6},{5,7},{6,4},{7,5},{8,10},{9,11},{10,... | collective-permute-start | bytes 983048 | tf_op jit(solution)/shard_map/ppermute | solution.py:909
  87.6 22.9 %collective-permute-start.8 = (bf16[80,2048]{1,0:T(8,128)(2,1)}, bf16[80,2048]{1,0:T(8,128)(2,1)S(1)}, u32[]{:S(2)}, u32[]{:S(2)}) collective-permute-start(bf16[80,2048]{1,0:T(8,128)(2,1)} %get-tuple-element.80.refs_0_), channel_id=1, source_target_pairs={{0,3},{1,2},{2,1},{3,0},{4,7},{5,6},{6,5},{7,4},{8,11},{9,10},{10,... | collective-permute-start | bytes 983048 | tf_op jit(solution)/shard_map/ppermute | solution.py:909
  114.4 123.9 %all-gather.11.cloned.1.call-start = ((), (), s32[]{:S(2)}) async-start(), calls=%async_computation.3 | async-start | bytes 5898240 | tf_op jit(solution)/shard_map/all_gather | solution.py:932
  133.7 21.6 %collective-permute-start.10 = (bf16[80,2048]{1,0:T(8,128)(2,1)}, bf16[80,2048]{1,0:T(8,128)(2,1)S(1)}, u32[]{:S(2)}, u32[]{:S(2)}) collective-permute-start(bf16[80,2048]{1,0:T(8,128)(2,1)} %get-tuple-element.88), channel_id=1, source_target_pairs={{0,2},{1,3},{2,0},{3,1},{4,6},{5,7},{6,4},{7,5},{8,10},{9,11},{10,... | collective-permute-start | bytes 983048 | tf_op jit(solution)/shard_map/ppermute | solution.py:909
  137.7 17.6 %collective-permute-start.11 = (bf16[80,2048]{1,0:T(8,128)(2,1)}, bf16[80,2048]{1,0:T(8,128)(2,1)S(1)}, u32[]{:S(2)}, u32[]{:S(2)}) collective-permute-start(bf16[80,2048]{1,0:T(8,128)(2,1)} %get-tuple-element.89), channel_id=1, source_target_pairs={{0,1},{1,0},{2,3},{3,2},{4,5},{5,4},{6,7},{7,6},{8,9},{9,8},{10,11... | collective-permute-start | bytes 983048 | tf_op jit(solution)/shard_map/ppermute | solution.py:909
  137.8 23.2 %collective-permute-start.9 = (bf16[80,2048]{1,0:T(8,128)(2,1)}, bf16[80,2048]{1,0:T(8,128)(2,1)S(1)}, u32[]{:S(2)}, u32[]{:S(2)}) collective-permute-start(bf16[80,2048]{1,0:T(8,128)(2,1)} %get-tuple-element.87), channel_id=1, source_target_pairs={{0,3},{1,2},{2,1},{3,0},{4,7},{5,6},{6,5},{7,4},{8,11},{9,10},{10,... | collective-permute-start | bytes 983048 | tf_op jit(solution)/shard_map/ppermute | solution.py:909
  164.7 39.6 %collective-permute-start.15 = (bf16[80,2048]{1,0:T(8,128)(2,1)}, bf16[80,2048]{1,0:T(8,128)(2,1)S(1)}, u32[]{:S(2)}, u32[]{:S(2)}) collective-permute-start(bf16[80,2048]{1,0:T(8,128)(2,1)} %get-tuple-element.99.refs_4_.refs_0_), channel_id=1, source_target_pairs={{0,1},{1,0},{2,3},{3,2},{4,5},{5,4},{6,7},{7,6},{8,9},{9,8},{10,11... | collective-permute-start | bytes 983048 | tf_op jit(solution)/shard_map/ppermute | solution.py:909
  169.3 35.0 %collective-permute-start.16 = (bf16[80,2048]{1,0:T(8,128)(2,1)}, bf16[80,2048]{1,0:T(8,128)(2,1)S(1)}, u32[]{:S(2)}, u32[]{:S(2)}) collective-permute-start(bf16[80,2048]{1,0:T(8,128)(2,1)} %get-tuple-element.99.refs_4_.refs_0_), channel_id=1, source_target_pairs={{0,2},{1,3},{2,0},{3,1},{4,6},{5,7},{6,4},{7,5},{8,10},{9,11},{10,... | collective-permute-start | bytes 983048 | tf_op jit(solution)/shard_map/ppermute | solution.py:909
  171.1 33.3 %collective-permute-start.17 = (bf16[80,2048]{1,0:T(8,128)(2,1)}, bf16[80,2048]{1,0:T(8,128)(2,1)S(1)}, u32[]{:S(2)}, u32[]{:S(2)}) collective-permute-start(bf16[80,2048]{1,0:T(8,128)(2,1)} %get-tuple-element.99.refs_4_.refs_0_), channel_id=1, source_target_pairs={{0,3},{1,2},{2,1},{3,0},{4,7},{5,6},{6,5},{7,4},{8,11},{9,10},{10,... | collective-permute-start | bytes 983048 | tf_op jit(solution)/shard_map/ppermute | solution.py:909
  221.1 26.7 %collective-permute-start.12 = (bf16[80,2048]{1,0:T(8,128)(2,1)}, bf16[80,2048]{1,0:T(8,128)(2,1)S(1)}, u32[]{:S(2)}, u32[]{:S(2)}) collective-permute-start(bf16[80,2048]{1,0:T(8,128)(2,1)} %get-tuple-element.94), channel_id=1, source_target_pairs={{0,3},{1,2},{2,1},{3,0},{4,7},{5,6},{6,5},{7,4},{8,11},{9,10},{10,... | collective-permute-start | bytes 983048 | tf_op jit(solution)/shard_map/ppermute | solution.py:909
  224.5 45.3 %collective-permute-start.13 = (bf16[80,2048]{1,0:T(8,128)(2,1)}, bf16[80,2048]{1,0:T(8,128)(2,1)S(1)}, u32[]{:S(2)}, u32[]{:S(2)}) collective-permute-start(bf16[80,2048]{1,0:T(8,128)(2,1)} %get-tuple-element.95), channel_id=1, source_target_pairs={{0,2},{1,3},{2,0},{3,1},{4,6},{5,7},{6,4},{7,5},{8,10},{9,11},{10,... | collective-permute-start | bytes 983048 | tf_op jit(solution)/shard_map/ppermute | solution.py:909
  224.5 45.3 %collective-permute-start.14 = (bf16[80,2048]{1,0:T(8,128)(2,1)}, bf16[80,2048]{1,0:T(8,128)(2,1)S(1)}, u32[]{:S(2)}, u32[]{:S(2)}) collective-permute-start(bf16[80,2048]{1,0:T(8,128)(2,1)} %get-tuple-element.96), channel_id=1, source_target_pairs={{0,1},{1,0},{2,3},{3,2},{4,5},{5,4},{6,7},{7,6},{8,9},{9,8},{10,11... | collective-permute-start | bytes 983048 | tf_op jit(solution)/shard_map/ppermute | solution.py:909
  225.5 12.8 %collective-permute-start.19 = (bf16[320,256]{1,0:T(8,128)(2,1)}, bf16[320,256]{1,0:T(8,128)(2,1)}, u32[]{:S(2)}, u32[]{:S(2)}) collective-permute-start(bf16[320,256]{1,0:T(8,128)(2,1)} %get-tuple-element.104), channel_id=1, source_target_pairs={{0,8},{4,12},{8,0},{12,4},{1,9},{5,13},{9,1},{13,5},{2,10},{6,14},... | collective-permute-start | bytes 491528 | tf_op jit(solution)/shard_map/ppermute | solution.py:909
  228.3 10.1 %collective-permute-start.20 = (bf16[320,256]{1,0:T(8,128)(2,1)}, bf16[320,256]{1,0:T(8,128)(2,1)}, u32[]{:S(2)}, u32[]{:S(2)}) collective-permute-start(bf16[320,256]{1,0:T(8,128)(2,1)} %get-tuple-element.105), channel_id=1, source_target_pairs={{0,4},{4,0},{8,12},{12,8},{1,5},{5,1},{9,13},{13,9},{2,6},{6,2},{1... | collective-permute-start | bytes 491528 | tf_op jit(solution)/shard_map/ppermute | solution.py:909
  244.4 32.5 %collective-permute-start.24 = (bf16[80,2048]{1,0:T(8,128)(2,1)}, bf16[80,2048]{1,0:T(8,128)(2,1)}, u32[]{:S(2)}, u32[]{:S(2)}) collective-permute-start(bf16[80,2048]{1,0:T(8,128)(2,1)} %get-tuple-element.113), channel_id=1, source_target_pairs={{0,3},{1,2},{2,1},{3,0},{4,7},{5,6},{6,5},{7,4},{8,11},{9,10},{10,... | collective-permute-start | bytes 983048 | tf_op jit(solution)/shard_map/ppermute | solution.py:909
  247.8 51.6 %collective-permute-start.25 = (bf16[80,2048]{1,0:T(8,128)(2,1)}, bf16[80,2048]{1,0:T(8,128)(2,1)}, u32[]{:S(2)}, u32[]{:S(2)}) collective-permute-start(bf16[80,2048]{1,0:T(8,128)(2,1)} %get-tuple-element.114), channel_id=1, source_target_pairs={{0,2},{1,3},{2,0},{3,1},{4,6},{5,7},{6,4},{7,5},{8,10},{9,11},{10,... | collective-permute-start | bytes 983048 | tf_op jit(solution)/shard_map/ppermute | solution.py:909
  247.8 51.6 %collective-permute-start.26 = (bf16[80,2048]{1,0:T(8,128)(2,1)}, bf16[80,2048]{1,0:T(8,128)(2,1)}, u32[]{:S(2)}, u32[]{:S(2)}) collective-permute-start(bf16[80,2048]{1,0:T(8,128)(2,1)} %get-tuple-element.115), channel_id=1, source_target_pairs={{0,1},{1,0},{2,3},{3,2},{4,5},{5,4},{6,7},{7,6},{8,9},{9,8},{10,11... | collective-permute-start | bytes 983048 | tf_op jit(solution)/shard_map/ppermute | solution.py:909
  269.7 102.6 %all-reduce.3.cloned.1.call-start = ((), (), s32[]{:S(2)}) async-start(), calls=%async_computation.4 | async-start | bytes 11534336 | tf_op jit(solution)/shard_map/psum | solution.py:1040
  272.9 33.8 %collective-permute-start.21 = (bf16[80,2048]{1,0:T(8,128)(2,1)}, bf16[80,2048]{1,0:T(8,128)(2,1)S(1)}, u32[]{:S(2)}, u32[]{:S(2)}) collective-permute-start(bf16[80,2048]{1,0:T(8,128)(2,1)} %add_up.2.refs_4_.refs_0_), channel_id=1, source_target_pairs={{0,1},{1,0},{2,3},{3,2},{4,5},{5,4},{6,7},{7,6},{8,9},{9,8},{10,11... | collective-permute-start | bytes 983048 | tf_op jit(solution)/shard_map/ppermute | solution.py:909
  274.0 51.5 %collective-permute-start.22 = (bf16[80,2048]{1,0:T(8,128)(2,1)S(1)}, bf16[80,2048]{1,0:T(8,128)(2,1)S(1)}, u32[]{:S(2)}, u32[]{:S(2)}) collective-permute-start(bf16[80,2048]{1,0:T(8,128)(2,1)S(1)} %copy-done), channel_id=1, source_target_pairs={{0,2},{1,3},{2,0},{3,1},{4,6},{5,7},{6,4},{7,5},{8,10},{9,11},{10,... | collective-permute-start | bytes 983048 | tf_op jit(solution)/shard_map/ppermute | solution.py:909
  276.9 48.7 %collective-permute-start.23 = (bf16[80,2048]{1,0:T(8,128)(2,1)S(1)}, bf16[80,2048]{1,0:T(8,128)(2,1)}, u32[]{:S(2)}, u32[]{:S(2)}) collective-permute-start(bf16[80,2048]{1,0:T(8,128)(2,1)S(1)} %copy-done), channel_id=1, source_target_pairs={{0,3},{1,2},{2,1},{3,0},{4,7},{5,6},{6,5},{7,4},{8,11},{9,10},{10,... | collective-permute-start | bytes 983048 | tf_op jit(solution)/shard_map/ppermute | solution.py:909
  302.9 45.6 %collective-permute-start.27 = (bf16[80,2048]{1,0:T(8,128)(2,1)}, bf16[80,2048]{1,0:T(8,128)(2,1)}, u32[]{:S(2)}, u32[]{:S(2)}) collective-permute-start(bf16[80,2048]{1,0:T(8,128)(2,1)} %finish.1.refs_4_.refs_0_), channel_id=1, source_target_pairs={{0,1},{1,0},{2,3},{3,2},{4,5},{5,4},{6,7},{7,6},{8,9},{9,8},{10,11... | collective-permute-start | bytes 983048 | tf_op jit(solution)/shard_map/ppermute | solution.py:909
  302.9 45.8 %collective-permute-start.28 = (bf16[80,2048]{1,0:T(8,128)(2,1)}, bf16[80,2048]{1,0:T(8,128)(2,1)}, u32[]{:S(2)}, u32[]{:S(2)}) collective-permute-start(bf16[80,2048]{1,0:T(8,128)(2,1)} %finish.1.refs_4_.refs_0_), channel_id=1, source_target_pairs={{0,2},{1,3},{2,0},{3,1},{4,6},{5,7},{6,4},{7,5},{8,10},{9,11},{10,... | collective-permute-start | bytes 983048 | tf_op jit(solution)/shard_map/ppermute | solution.py:909
  306.8 42.3 %collective-permute-start.29 = (bf16[80,2048]{1,0:T(8,128)(2,1)}, bf16[80,2048]{1,0:T(8,128)(2,1)}, u32[]{:S(2)}, u32[]{:S(2)}) collective-permute-start(bf16[80,2048]{1,0:T(8,128)(2,1)} %finish.1.refs_4_.refs_0_), channel_id=1, source_target_pairs={{0,3},{1,2},{2,1},{3,0},{4,7},{5,6},{6,5},{7,4},{8,11},{9,10},{10,... | collective-permute-start | bytes 983048 | tf_op jit(solution)/shard_map/ppermute | solution.py:909
  325.5 48.5 %collective-permute-start.34 = (bf16[256,2048]{1,0:T(8,128)(2,1)}, bf16[256,2048]{1,0:T(8,128)(2,1)}, u32[]{:S(2)}, u32[]{:S(2)}) collective-permute-start(bf16[256,2048]{1,0:T(8,128)(2,1)} %get-tuple-element.125), channel_id=1, source_target_pairs={{0,16},{16,0},{1,17},{17,1},{2,18},{18,2},{3,19},{19,3},{4,20},{20... | collective-permute-start | bytes 3145736 | tf_op jit(solution)/shard_map/ppermute | solution.py:909
  325.6 48.5 %collective-permute-start.35 = (bf16[256,2048]{1,0:T(8,128)(2,1)}, bf16[256,2048]{1,0:T(8,128)(2,1)}, u32[]{:S(2)}, u32[]{:S(2)}) collective-permute-start(bf16[256,2048]{1,0:T(8,128)(2,1)} %get-tuple-element.126), channel_id=1, source_target_pairs={{0,16},{16,0},{1,17},{17,1},{2,18},{18,2},{3,19},{19,3},{4,20},{20... | collective-permute-start | bytes 3145736 | tf_op jit(solution)/shard_map/ppermute | solution.py:909
  348.5 26.1 %collective-permute-start.36 = (bf16[256,2048]{1,0:T(8,128)(2,1)}, bf16[256,2048]{1,0:T(8,128)(2,1)}, u32[]{:S(2)}, u32[]{:S(2)}) collective-permute-start(bf16[256,2048]{1,0:T(8,128)(2,1)} %get-tuple-element.127), channel_id=1, source_target_pairs={{0,16},{16,0},{1,17},{17,1},{2,18},{18,2},{3,19},{19,3},{4,20},{20... | collective-permute-start | bytes 3145736 | tf_op jit(solution)/shard_map/ppermute | solution.py:909
  348.6 26.0 %collective-permute-start.37 = (bf16[256,2048]{1,0:T(8,128)(2,1)}, bf16[256,2048]{1,0:T(8,128)(2,1)}, u32[]{:S(2)}, u32[]{:S(2)}) collective-permute-start(bf16[256,2048]{1,0:T(8,128)(2,1)} %get-tuple-element.128), channel_id=1, source_target_pairs={{0,16},{16,0},{1,17},{17,1},{2,18},{18,2},{3,19},{19,3},{4,20},{20... | collective-permute-start | bytes 3145736 | tf_op jit(solution)/shard_map/ppermute | solution.py:909
  349.1 32.9 %collective-permute-start.30 = (bf16[512,1024]{1,0:T(8,128)(2,1)}, bf16[512,1024]{1,0:T(8,128)(2,1)}, u32[]{:S(2)}, u32[]{:S(2)}) collective-permute-start(bf16[512,1024]{1,0:T(8,128)(2,1)} %get-tuple-element.121), channel_id=1, source_target_pairs={{0,16},{16,0},{1,17},{17,1},{2,18},{18,2},{3,19},{19,3},{4,20},{20... | collective-permute-start | bytes 3145736 | tf_op jit(solution)/shard_map/ppermute | solution.py:909
  374.1 8.0 %collective-permute-start.31 = (bf16[512,1024]{1,0:T(8,128)(2,1)}, bf16[512,1024]{1,0:T(8,128)(2,1)}, u32[]{:S(2)}, u32[]{:S(2)}) collective-permute-start(bf16[512,1024]{1,0:T(8,128)(2,1)} %get-tuple-element.122), channel_id=1, source_target_pairs={{0,16},{16,0},{1,17},{17,1},{2,18},{18,2},{3,19},{19,3},{4,20},{20... | collective-permute-start | bytes 3145736 | tf_op jit(solution)/shard_map/ppermute | solution.py:909
  374.1 8.4 %collective-permute-start.32 = (bf16[512,1024]{1,0:T(8,128)(2,1)}, bf16[512,1024]{1,0:T(8,128)(2,1)}, u32[]{:S(2)}, u32[]{:S(2)}) collective-permute-start(bf16[512,1024]{1,0:T(8,128)(2,1)} %get-tuple-element.123), channel_id=1, source_target_pairs={{0,16},{16,0},{1,17},{17,1},{2,18},{18,2},{3,19},{19,3},{4,20},{20... | collective-permute-start | bytes 3145736 | tf_op jit(solution)/shard_map/ppermute | solution.py:909
  374.6 8.0 %collective-permute-start.33 = (bf16[512,1024]{1,0:T(8,128)(2,1)}, bf16[512,1024]{1,0:T(8,128)(2,1)}, u32[]{:S(2)}, u32[]{:S(2)}) collective-permute-start(bf16[512,1024]{1,0:T(8,128)(2,1)} %get-tuple-element.124), channel_id=1, source_target_pairs={{0,16},{16,0},{1,17},{17,1},{2,18},{18,2},{3,19},{19,3},{4,20},{20... | collective-permute-start | bytes 3145736 | tf_op jit(solution)/shard_map/ppermute | solution.py:909
  374.7 8.3 %collective-permute-start.42 = (f32[8,2048]{1,0:T(8,128)}, f32[8,2048]{1,0:T(8,128)S(1)}, u32[]{:S(2)}, u32[]{:S(2)}) collective-permute-start(f32[8,2048]{1,0:T(8,128)} %gain_rows.1.refs_0_), channel_id=1, source_target_pairs={{0,1},{1,0},{2,3},{3,2},{4,5},{5,4},{6,7},{7,6},{8,9},{9,8},{10,11... | collective-permute-start | bytes 196616 | tf_op jit(solution)/shard_map/ppermute | solution.py:909
  381.9 21.6 %collective-permute-start.38 = (bf16[512,1024]{1,0:T(8,128)(2,1)}, bf16[512,1024]{1,0:T(8,128)(2,1)}, u32[]{:S(2)}, u32[]{:S(2)}) collective-permute-start(bf16[512,1024]{1,0:T(8,128)(2,1)} %get-tuple-element.129), channel_id=1, source_target_pairs={{0,16},{16,0},{1,17},{17,1},{2,18},{18,2},{3,19},{19,3},{4,20},{20... | collective-permute-start | bytes 3145736 | tf_op jit(solution)/shard_map/ppermute | solution.py:909
  382.1 21.4 %collective-permute-start.39 = (bf16[512,1024]{1,0:T(8,128)(2,1)}, bf16[512,1024]{1,0:T(8,128)(2,1)}, u32[]{:S(2)}, u32[]{:S(2)}) collective-permute-start(bf16[512,1024]{1,0:T(8,128)(2,1)} %get-tuple-element.130), channel_id=1, source_target_pairs={{0,16},{16,0},{1,17},{17,1},{2,18},{18,2},{3,19},{19,3},{4,20},{20... | collective-permute-start | bytes 3145736 | tf_op jit(solution)/shard_map/ppermute | solution.py:909
  382.5 21.1 %collective-permute-start.40 = (bf16[512,1024]{1,0:T(8,128)(2,1)}, bf16[512,1024]{1,0:T(8,128)(2,1)}, u32[]{:S(2)}, u32[]{:S(2)}) collective-permute-start(bf16[512,1024]{1,0:T(8,128)(2,1)} %get-tuple-element.131), channel_id=1, source_target_pairs={{0,16},{16,0},{1,17},{17,1},{2,18},{18,2},{3,19},{19,3},{4,20},{20... | collective-permute-start | bytes 3145736 | tf_op jit(solution)/shard_map/ppermute | solution.py:909
  382.6 20.9 %collective-permute-start.41 = (bf16[512,1024]{1,0:T(8,128)(2,1)}, bf16[512,1024]{1,0:T(8,128)(2,1)}, u32[]{:S(2)}, u32[]{:S(2)}) collective-permute-start(bf16[512,1024]{1,0:T(8,128)(2,1)} %get-tuple-element.132), channel_id=1, source_target_pairs={{0,16},{16,0},{1,17},{17,1},{2,18},{18,2},{3,19},{19,3},{4,20},{20... | collective-permute-start | bytes 3145736 | tf_op jit(solution)/shard_map/ppermute | solution.py:909
  383.0 8.3 %collective-permute-start.43 = (f32[8,2048]{1,0:T(8,128)S(1)}, f32[8,2048]{1,0:T(8,128)S(1)}, u32[]{:S(2)}, u32[]{:S(2)}) collective-permute-start(f32[8,2048]{1,0:T(8,128)S(1)} %copy-done.20), channel_id=1, source_target_pairs={{0,2},{1,3},{2,0},{3,1},{4,6},{5,7},{6,4},{7,5},{8,10},{9,11},{10,... | collective-permute-start | bytes 196616 | tf_op jit(solution)/shard_map/ppermute | solution.py:909
  391.3 8.6 %collective-permute-start.44 = (f32[8,2048]{1,0:T(8,128)S(1)}, f32[8,2048]{1,0:T(8,128)S(1)}, u32[]{:S(2)}, u32[]{:S(2)}) collective-permute-start(f32[8,2048]{1,0:T(8,128)S(1)} %copy-done.20), channel_id=1, source_target_pairs={{0,3},{1,2},{2,1},{3,0},{4,7},{5,6},{6,5},{7,4},{8,11},{9,10},{10,... | collective-permute-start | bytes 196616 | tf_op jit(solution)/shard_map/ppermute | solution.py:909
  (29 other events, 138.8 us)
Sparse Core Ops, SparseCore 0:
  49.5 41.4 all-gather.4
  93.5 41.1 all-gather.8
  137.1 41.1 all-gather.6
  180.0 41.1 all-gather.10
  274.1 98.0 all-reduce.2

commit v3 on v2

--- a/solution.py
+++ b/solution.py
@@ -82,7 +82,7 @@
             out_specs=pl.BlockSpec((rows, cols), lambda j, i, c: (i, j)),
         ),
         compiler_params=kernel_params(2),
-        cost_estimate=SMALL,
+        cost_estimate=spent(10),
         name="grad_hidden_of",
     )(core, upstream, w_down, *deps)
 
@@ -130,7 +130,7 @@
             out_specs=(block, block, block),
         ),
         compiler_params=kernel_params(2),
-        cost_estimate=SMALL,
+        cost_estimate=spent(18),
         name="feed_half",
     )(core, normed, w_gate, w_up, grad_hidden, *deps)
 
@@ -186,86 +186,156 @@
         out_specs=(block,) + (rows,) * chunks,
         scratch_shapes=[pltpu.VMEM((tokens, depth), BF), pltpu.VMEM((tokens, depth), F32)],
         compiler_params=kernel_params(1),
-        cost_estimate=SMALL,
+        cost_estimate=spent(18),
         name="feed_own",
     )(w_gate, w_up, grad_hidden, *normed, *deps)
     return out[0], list(out[1:])
 
 
-def down_kernel(chunks, hidden, weight, *refs):
-    parts = refs[-chunks:]
-    part = contract(hidden[...], weight[...], 1, 0)
-    rows = part.shape[0] // chunks
-    for k, out in enumerate(parts):
-        out[...] = part[k * rows : (k + 1) * rows].astype(BF)
-
-
-def down_projection(hidden, w_down, chunks, deps=()):
+def down_kernel(hidden, weight, *refs):
+    keep, send = refs[-2:]
+    part = contract(hidden[...], weight[...], 1, 0).astype(BF)
+    rows = keep.shape[0]
+    keep[...] = part[:rows]
+    send[...] = part[rows:]
+
+
+def down_projection(hidden, w_down, deps=()):
     tokens, units = hidden.shape
     depth = w_down.shape[1]
     cols = tile(512, depth)
-    return list(
-        pl.pallas_call(
-            functools.partial(down_kernel, chunks),
-            out_shape=(jax.ShapeDtypeStruct((tokens // chunks, depth), BF),) * chunks,
-            grid=(depth // cols,),
-            in_specs=[whole_spec(hidden), pl.BlockSpec((units, cols), lambda j: (0, j))]
-            + unread(deps),
-            out_specs=(pl.BlockSpec((tokens // chunks, cols), lambda j: (0, j)),) * chunks,
-            compiler_params=kernel_params(1),
-            cost_estimate=SMALL,
-                name="down_projection",
-        )(hidden, w_down, *deps)
-    )
-
-
-PIECES = 4
-
-
-def weight_grad_kernel(count, core, *refs):
+    half = jax.ShapeDtypeStruct((tokens // 2, depth), BF)
+    block = pl.BlockSpec((tokens // 2, cols), lambda j: (0, j))
+    return pl.pallas_call(
+        down_kernel,
+        out_shape=(half, half),
+        grid=(depth // cols,),
+        in_specs=[whole_spec(hidden), pl.BlockSpec((units, cols), lambda j: (0, j))]
+        + unread(deps),
+        out_specs=(block, block),
+        compiler_params=kernel_params(1),
+        cost_estimate=spent(7),
+        name="down_projection",
+    )(hidden, w_down, *deps)
+
+
+def add_half_kernel(keep, came, *refs):
+    total = keep[...].astype(F32) + came[...].astype(F32)
+    first, second = refs[-2:]
+    rows = first.shape[0]
+    first[...] = total[:rows].astype(BF)
+    second[...] = total[rows:].astype(BF)
+
+
+def add_half(keep, came, deps=()):
+    rows, depth = keep.shape
+    half = jax.ShapeDtypeStruct((rows // 2, depth), BF)
+    return pl.pallas_call(
+        add_half_kernel,
+        out_shape=(half, half),
+        grid=(1,),
+        in_specs=[whole_spec(keep), whole_spec(came)] + unread(deps),
+        out_specs=(whole_spec(half), whole_spec(half)),
+        compiler_params=kernel_params(1),
+        cost_estimate=spent(2),
+        name="add_half",
+    )(keep, came, *deps)
+
+
+STEPS = 4
+
+
+def weight_grad_kernel(count, pieces, core, *refs):
     lefts, rights = refs[:count], refs[count : 2 * count]
-    wide, lows = refs[-1 - PIECES], refs[-PIECES:]
+    wide, lows = refs[-1 - pieces], refs[-pieces:]
     total = contract(lefts[0][...], rights[0][...], 0, 0)
     for left, right in zip(lefts[1:], rights[1:]):
         total = total + contract(left[...], right[...], 0, 0)
     wide[...] = total
     for k, low in enumerate(lows):
 
-        @pl.when(pl.program_id(1) == k)
+        @pl.when(pl.program_id(1) // (STEPS // pieces) == k)
         def _():
             low[...] = total.astype(BF)
 
 
-def weight_grad(core, lefts, rights, dim, deps=()):
+def weight_grad(core, lefts, rights, dim, pieces, deps=()):
     tokens, m = lefts[0].shape
     n = rights[0].shape[1]
     count = len(lefts)
-    rows, cols = m // PIECES, tile(1024, n)
+    rows, cols = m // STEPS, tile(1024, n)
     across = n // cols
     if dim == 0:
         full = (2 * m, n)
-        place = lambda j, i, c: (c[0] * PIECES + i, j)
+        place = lambda j, i, c: (c[0] * STEPS + i, j)
     else:
         full = (m, 2 * n)
         place = lambda j, i, c: (i, c[0] * across + j)
-    piece = pl.BlockSpec((rows, cols), lambda j, i, c: (0, j))
+    share = STEPS // pieces
+
+    def piece(k):
+        last = share - 1
+        return pl.BlockSpec(
+            (rows, cols), lambda j, i, c: (jnp.clip(i - k * share, 0, last), j)
+        )
+
     out = pl.pallas_call(
-        functools.partial(weight_grad_kernel, count),
+        functools.partial(weight_grad_kernel, count, pieces),
         out_shape=(jax.ShapeDtypeStruct(full, F32),)
-        + (jax.ShapeDtypeStruct((rows, n), BF),) * PIECES,
+        + (jax.ShapeDtypeStruct((rows * share, n), BF),) * pieces,
         grid_spec=pltpu.PrefetchScalarGridSpec(
             num_scalar_prefetch=1,
-            grid=(across, PIECES),
+            grid=(across, STEPS),
             in_specs=[pl.BlockSpec((tokens, rows), lambda j, i, c: (0, i))] * count
             + [pl.BlockSpec((tokens, cols), lambda j, i, c: (0, j))] * count
             + unread(deps),
-            out_specs=(pl.BlockSpec((rows, cols), place),) + (piece,) * PIECES,
+            out_specs=(pl.BlockSpec((rows, cols), place),)
+            + tuple(piece(k) for k in range(pieces)),
         ),
         compiler_params=kernel_params(2),
-        cost_estimate=SMALL,
+        cost_estimate=spent(19),
         name="weight_grad",
     )(core, *lefts, *rights, *deps)
     return out[0], list(out[1:])
+
+
+def pair_grad_kernel(count, core, *refs):
+    lefts = [r[...] for r in refs[:count]]
+    wides, low = refs[-3:-1], refs[-1]
+    for k in range(2):
+        rights = refs[count * (k + 1) : count * (k + 2)]
+        total = contract(lefts[0], rights[0][...], 0, 0)
+        for left, right in zip(lefts[1:], rights[1:]):
+            total = total + contract(left, right[...], 0, 0)
+        wides[k][...] = total
+        low[k] = total.astype(BF)
+
+
+def pair_grad(core, lefts, first, second, deps=()):
+    tokens, m = lefts[0].shape
+    n = first[0].shape[1]
+    count = len(lefts)
+    rows = m // STEPS
+    wide = jax.ShapeDtypeStruct((m, 2 * n), F32)
+    low = jax.ShapeDtypeStruct((2, m, n), BF)
+    place = pl.BlockSpec((rows, n), lambda i, c: (i, c[0]))
+    here = pl.BlockSpec((2, rows, n), lambda i, c: (0, i, 0))
+    out = pl.pallas_call(
+        functools.partial(pair_grad_kernel, count),
+        out_shape=(wide, wide, low),
+        grid_spec=pltpu.PrefetchScalarGridSpec(
+            num_scalar_prefetch=1,
+            grid=(STEPS,),
+            in_specs=[pl.BlockSpec((tokens, rows), lambda i, c: (0, i))] * count
+            + [whole_spec(v) for v in (*first, *second)]
+            + unread(deps),
+            out_specs=(place, place, here),
+        ),
+        compiler_params=kernel_params(1),
+        cost_estimate=spent(34),
+        name="pair_grad",
+    )(core, *lefts, *first, *second, *deps)
+    return out
 
 
 def left_product_kernel(count, left, *refs):
@@ -286,7 +356,7 @@
         + unread(deps),
         out_specs=pl.BlockSpec((rows, cols), lambda i, j: (i, j)),
         compiler_params=kernel_params(2),
-        cost_estimate=SMALL,
+        cost_estimate=spent(4),
         name="left_product",
     )(left, *pieces, *deps)
 
@@ -294,26 +364,26 @@
 def kv_product_kernel(left, right, gain_one, gain_two, *refs):
     out = refs[-1]
     width = right.shape[1]
-    rows = left.shape[1]
-    out[:, :width] = contract(left[...], right[...], 0, 0).astype(BF)
-    gains = jnp.concatenate([gain_one[...], gain_two[...], jnp.zeros((126, rows), F32)], axis=0)
-    out[:, width:] = jnp.transpose(gains).astype(BF)
+    out[:width, :] = contract(right[...], left[...], 0, 0).astype(BF)
+    empty = jnp.zeros((14, left.shape[1]), F32)
+    gains = jnp.concatenate([gain_one[...], gain_two[...], empty], axis=0)
+    out[width:, :] = gains.astype(BF)
 
 
 def kv_product(left, right, gain_one, gain_two, deps=()):
     tokens, m = left.shape
     width = right.shape[1]
-    rows = tile(1024, m)
-    gain = pl.BlockSpec((1, rows), lambda i: (0, i))
+    cols = tile(1024, m)
+    gain = pl.BlockSpec((1, cols), lambda i: (0, i))
     return pl.pallas_call(
         kv_product_kernel,
-        out_shape=jax.ShapeDtypeStruct((m, width + 128), BF),
-        grid=(m // rows,),
-        in_specs=[pl.BlockSpec((tokens, rows), lambda i: (0, i)), whole_spec(right), gain, gain]
+        out_shape=jax.ShapeDtypeStruct((width + 16, m), BF),
+        grid=(m // cols,),
+        in_specs=[pl.BlockSpec((tokens, cols), lambda i: (0, i)), whole_spec(right), gain, gain]
         + unread(deps),
-        out_specs=pl.BlockSpec((rows, width + 128), lambda i: (i, 0)),
-        compiler_params=kernel_params(1),
-        cost_estimate=SMALL,
+        out_specs=pl.BlockSpec((width + 16, cols), lambda i: (0, i)),
+        compiler_params=kernel_params(1),
+        cost_estimate=spent(3),
         name="kv_product",
     )(left, right, gain_one, gain_two, *deps)
 
@@ -343,58 +413,84 @@
             out_specs=tuple(whole_spec(a) for a in outs),
         ),
         compiler_params=kernel_params(1),
-        cost_estimate=SMALL,
+        cost_estimate=spent(40),
         name="mask_padding",
     )(scalars, place, *[value] * chunks, *deps)
 
 
-def gain_rows_kernel(value, out):
-    out[...] = jnp.transpose(value[...].astype(F32))[:8]
-
-
-def gain_rows(value):
+def corner_kernel(value, out):
+    out[...] = value[...]
+
+
+def corner(value):
+    return pl.pallas_call(
+        corner_kernel,
+        out_shape=jax.ShapeDtypeStruct((16, 128), value.dtype),
+        grid=(1,),
+        in_specs=[pl.BlockSpec((16, 128), lambda i: (0, 0))],
+        out_specs=pl.BlockSpec((16, 128), lambda i: (0, 0)),
+        compiler_params=kernel_params(1),
+        cost_estimate=spent(5),
+        name="corner",
+    )(value)
+
+
+def gain_rows_kernel(value, *refs):
+    refs[-1][...] = value[...].astype(F32)
+
+
+def gain_rows(value, deps=()):
     rows, width = value.shape
     return pl.pallas_call(
         gain_rows_kernel,
-        out_shape=jax.ShapeDtypeStruct((8, rows), F32),
+        out_shape=jax.ShapeDtypeStruct((16, width), F32),
         grid=(1,),
-        in_specs=[pl.BlockSpec((rows, 128), lambda i: (0, width // 128 - 1))],
-        out_specs=pl.BlockSpec((8, rows), lambda i: (0, 0)),
-        compiler_params=kernel_params(1),
-        cost_estimate=SMALL,
+        in_specs=[pl.BlockSpec((16, width), lambda i: (rows // 16 - 1, 0))] + unread(deps),
+        out_specs=pl.BlockSpec((16, width), lambda i: (0, 0)),
+        compiler_params=kernel_params(1),
+        cost_estimate=spent(2),
         name="gain_rows",
-    )(value)
-
-
-def fill_other_kernel(core, *refs):
+    )(value, *deps)
+
+
+def fill_other_kernel(pieces, core, *refs):
     step = pl.program_id(0)
-    for k in range(PIECES):
-
-        @pl.when(step == k)
+    for k in range(pieces):
+
+        @pl.when(step // (STEPS // pieces) == k)
         def _():
-            refs[-1][...] = refs[k][...].astype(F32)
-
-
-def fill_other(core, others, held, dim, deps=()):
-    rows, n = others[0].shape
+            refs[-1][...] = refs[k][...].astype(F32).reshape(refs[-1].shape)
+
+
+def fill_other(core, others, index, held, dim, deps=()):
+    pieces = len(others)
+    share = STEPS // pieces
+    rows, n = others[0].shape[1] // share, others[0].shape[2]
     if dim == 0:
-        place = lambda i, c: ((1 - c[0]) * PIECES + i, 0)
+        place = lambda i, c: ((1 - c[0]) * STEPS + i, 0)
     else:
         place = lambda i, c: (i, 1 - c[0])
-    return pl.pallas_call(
-        fill_other_kernel,
+
+    def piece(k):
+        last = share - 1
+        return pl.BlockSpec(
+            (1, rows, n), lambda i, c: (index, jnp.clip(i - k * share, 0, last), 0)
+        )
+
+    return pl.pallas_call(
+        functools.partial(fill_other_kernel, pieces),
         out_shape=jax.ShapeDtypeStruct(held.shape, F32),
         grid_spec=pltpu.PrefetchScalarGridSpec(
             num_scalar_prefetch=1,
-            grid=(PIECES,),
-            in_specs=[whole_spec(o) for o in others]
+            grid=(STEPS,),
+            in_specs=[piece(k) for k in range(pieces)]
             + [pl.BlockSpec(memory_space=pl.ANY)]
             + unread(deps),
             out_specs=pl.BlockSpec((rows, n), place),
         ),
-        input_output_aliases={1 + PIECES: 0},
-        compiler_params=kernel_params(1),
-        cost_estimate=spent(50),
+        input_output_aliases={1 + pieces: 0},
+        compiler_params=kernel_params(1),
+        cost_estimate=spent(6),
         name="fill_other",
     )(core, *others, held, *deps)
 
@@ -460,7 +556,7 @@
             out_specs=tuple(whole_spec(a) for a in outs),
         ),
         compiler_params=kernel_params(1),
-        cost_estimate=SMALL,
+        cost_estimate=spent(4),
         name="project_kv",
     )(me, *[x] * chunks, *args, *deps)
 
@@ -490,7 +586,7 @@
         + unread(deps),
         out_specs=pl.BlockSpec((span, cols), lambda j: (0, j)),
         compiler_params=kernel_params(1),
-        cost_estimate=SMALL,
+        cost_estimate=spent(4),
         name="project_query",
     )(normed, w_query, cosine, sine, *deps)
 
@@ -574,7 +670,7 @@
             out_specs=tuple(whole_spec(a) for a in outs),
         ),
         compiler_params=kernel_params(1),
-        cost_estimate=spent(87),
+        cost_estimate=spent(11),
         name="attend",
     )(shift, *args, *deps)
     return out[0], out[1], list(out[2:])
@@ -615,7 +711,7 @@
             out_specs=tuple(whole_spec(a) for a in outs),
         ),
         compiler_params=kernel_params(1),
-        cost_estimate=SMALL,
+        cost_estimate=spent(3),
         name="middle_norm",
     )(me, x, gain, *chunks, *deps)
 
@@ -636,7 +732,7 @@
         in_specs=[whole_spec(a) for a in chunks] + unread(deps),
         out_specs=tuple(whole_spec(a) for a in outs),
         compiler_params=kernel_params(1),
-        cost_estimate=SMALL,
+        cost_estimate=spent(2),
         name="join_halves",
     )(*chunks, *deps)
 
@@ -675,22 +771,22 @@
         + unread(deps),
         out_specs=tuple(whole_spec(a) for a in outs),
         compiler_params=kernel_params(1),
-        cost_estimate=SMALL,
+        cost_estimate=spent(3),
         name="norm_back",
     )(upstream, *args, *deps)
 
 
-def finish_kernel(count, me, x, inverse, gain, grad_middle, *refs):
+def finish_kernel(count, me, x, inverse, gain, grad_middle, block, *refs):
     grad, _ = norm_gradient(
         sum_chunks(refs[:count]), x[...].astype(F32), inverse[:, :1], gain[...]
     )
-    refs[-1][...] = (grad_middle[...] + grad).astype(BF)
-
-
-def finish(me, x, inverse, gain, grad_middle, chunks, deps=()):
+    refs[-1][...] = jnp.concatenate([grad_middle[...] + grad, block[...]], axis=0).astype(BF)
+
+
+def finish(me, x, inverse, gain, grad_middle, block, chunks, deps=()):
     rows, depth = grad_middle.shape
-    args = (gain, grad_middle, *chunks)
-    outs = jax.ShapeDtypeStruct((rows, depth), BF)
+    args = (gain, grad_middle, block, *chunks)
+    outs = jax.ShapeDtypeStruct((2 * rows, depth), BF)
     return pl.pallas_call(
         functools.partial(finish_kernel, len(chunks)),
         out_shape=outs,
@@ -706,7 +802,7 @@
             out_specs=whole_spec(outs),
         ),
         compiler_params=kernel_params(1),
-        cost_estimate=SMALL,
+        cost_estimate=spent(3),
         name="finish",
     )(me, x, inverse, *args, *deps)
 
@@ -724,7 +820,7 @@
         in_specs=[whole_spec(a) for a in arrays] + unread(deps),
         out_specs=whole_spec(out),
         compiler_params=kernel_params(1),
-        cost_estimate=SMALL,
+        cost_estimate=spent(2),
         name="add_up",
     )(*arrays, *deps)
 
@@ -735,27 +831,65 @@
 
         @pl.when(step == k)
         def _():
-            refs[-1][...] = refs[k][...]
-
-
-def restore(me, pieces, cost, deps=()):
+            rows = refs[k].shape[0] // 2
+            refs[-2][...] = refs[k][:rows]
+            refs[-1][...] = refs[k][rows:]
+
+
+def restore(me, pieces, deps=()):
     count = len(pieces)
-    rows, depth = pieces[0].shape
+    rows, depth = pieces[0].shape[0] // 2, pieces[0].shape[1]
     if rows % 16:
-        return reorder(jnp.concatenate(pieces, axis=0), "tensor")
+        halves = [[p[:rows] for p in pieces], [p[rows:] for p in pieces]]
+        return [reorder(jnp.concatenate(h, axis=0), "tensor") for h in halves]
+    out = jax.ShapeDtypeStruct((count * rows, depth), BF)
+    place = pl.BlockSpec((rows, depth), lambda i, c: (c[0] ^ i, 0))
     return pl.pallas_call(
         functools.partial(restore_kernel, count),
-        out_shape=jax.ShapeDtypeStruct((count * rows, depth), BF),
+        out_shape=(out, out),
         grid_spec=pltpu.PrefetchScalarGridSpec(
             num_scalar_prefetch=1,
             grid=(count,),
             in_specs=[whole_spec(p) for p in pieces] + unread(deps),
-            out_specs=pl.BlockSpec((rows, depth), lambda i, c: (c[0] ^ i, 0)),
-        ),
-        compiler_params=kernel_params(1),
-        cost_estimate=cost,
+            out_specs=(place, place),
+        ),
+        compiler_params=kernel_params(1),
+        cost_estimate=spent(87),
         name="restore",
     )(me, *pieces, *deps)
+
+
+def widen(wo, wq, wkv, width, deps=()):
+    steps = 4
+    depth = wq.shape[0]
+    shapes = [wo.shape, wq.shape, (depth, width), (depth, width)]
+
+    def spec(shape):
+        return pl.BlockSpec((shape[0] // steps, shape[1]), lambda i: (i, 0))
+
+    def kernel(wo, wq, wkv, *refs):
+        wo_out, wq_out, wk_out, wv_out = refs[-4:]
+        wo_out[...] = wo[...].astype(F32)
+        wq_out[...] = wq[...].astype(F32)
+        turned = jnp.transpose(wkv[: 2 * width, :].astype(F32))
+        wk_out[...] = turned[:, :width]
+        wv_out[...] = turned[:, width:]
+
+    return pl.pallas_call(
+        kernel,
+        out_shape=tuple(jax.ShapeDtypeStruct(v, F32) for v in shapes),
+        grid=(steps,),
+        in_specs=[
+            spec(wo.shape),
+            spec(wq.shape),
+            pl.BlockSpec((wkv.shape[0], depth // steps), lambda i: (0, i)),
+        ]
+        + unread(deps),
+        out_specs=tuple(spec(v) for v in shapes),
+        compiler_params=kernel_params(1),
+        cost_estimate=spent(8),
+        name="widen",
+    )(wo, wq, wkv, *deps)
 
 
 def attend_back_kernel(blocks, count, shift, query, attended, stats, place, place_row, begin_row,
@@ -836,7 +970,7 @@
             out_specs=tuple(whole_spec(a) for a in outs),
         ),
         compiler_params=kernel_params(1),
-        cost_estimate=SMALL,
+        cost_estimate=spent(16),
         name="attend_back",
     )(shift, *args, *deps)
     return out[0], list(out[1:])
@@ -884,7 +1018,7 @@
             out_specs=tuple(whole_spec(a) for a in outs),
         ),
         compiler_params=kernel_params(1),
-        cost_estimate=SMALL,
+        cost_estimate=spent(6),
         name="input_back",
     )(me, *args, *[x] * chunks, *deps)
     return out[0], out[1], list(out[2:])
@@ -974,15 +1108,17 @@
     scalars = jnp.stack([me, ends[-1].astype(jnp.int32)])
     places = (place.reshape(span, 1), place.reshape(1, span), begin.reshape(1, span))
 
+    upstream, *upstream_halves = mask_padding(scalars, cotangent, places[0], chunks, ())
+    upstream_all = gather_halves(*upstream_halves)
     normed_one, inverse_one, packed = project_kv(
-        scalars, stream, gain_attn, key_matrix, value_matrix, cosine, sine, chunks, (shift, *places)
+        scalars, stream, gain_attn, key_matrix, value_matrix, cosine, sine, chunks, (shift, *places, upstream)
     )
     packed = spread(packed, "seq")
     query = project_query(normed_one, w_query, cosine, sine)
-    attended, stats, parts = attend(shift, query, packed, places, w_output, chunks)
-
-    upstream, *upstream_halves = mask_padding(scalars, cotangent, places[0], chunks, (parts[0],))
-    upstream_all = gather_halves(*upstream_halves)
+    attended, stats, parts = attend(
+        shift, query, packed, places, w_output, chunks
+    )
+
     sent = exchange(parts, "tensor")
     grad_hidden = grad_hidden_of(core, upstream, w_down, 1, (parts[0],))
     middle, inverse_two, normed = middle_norm(scalars, stream, gain_ffn, sent, (grad_hidden,))
@@ -1001,7 +1137,7 @@
     feed_first = feed_half(
         core, normed_all[0], w_gate, w_up, grad_hidden_first, (grad_middle,)
     )
-    down_parts = down_projection(hidden, w_down, chunks, (feed_first[0],))
+    down_parts = down_projection(hidden, w_down, (feed_first[0],))
     grad_query, kv_terms = attend_back(
         shift,
         query,
@@ -1015,7 +1151,8 @@
         grad_middle_all,
         (down_parts[0],),
     )
-    block_sent = exchange(down_parts, "tensor")
+    mask = chunks // 2
+    down_came = flip(down_parts[1], "tensor", mask)
 
     kv_sent = exchange(kv_terms, "seq")
     wo_part = left_product(attended, grad_middle_all, (grad_query,))
@@ -1039,36 +1176,41 @@
     wkv_part = kv_product(normed_one, grad_kv, gain_one, gain_two, (parts[0],))
     grad_wo, grad_wq, grad_wkv = lax.psum((wo_part, wq_part, wkv_part), ("rows", "seq"))
     feed_second = feed_half(
-        core, normed_all[1], w_gate, w_up, grad_hidden_second, (wkv_part,)
-    )
-    block_chunk = add_up([middle, *block_sent], BF, (feed_second[0],))
-    block_all = spread(block_chunk, "tensor")
+        core, normed_all[1], w_gate, w_up, grad_hidden_second, (corner(wkv_part),)
+    )
+    keep, send = add_half(down_parts[0], down_came, (feed_second[0],))
+    while mask > 2:
+        mask //= 2
+        keep, send = add_half(keep, flip(send, "tensor", mask))
+    mask //= 2
     hidden_all, grad_gate_all, grad_up_all = zip(feed_first, feed_second)
-    grad_down, low = weight_grad(core, hidden_all, upstream_all, 0, (block_chunk,))
-    down_other = [flip(v, "rows", 1) for v in low]
-    grad_input = finish(
-        scalars, stream, inverse_one, gain_attn, grad_middle, sent, (grad_down,)
-    )
-    grad_input_all = spread(grad_input, "tensor")
-    grad_gate_w, low = weight_grad(core, normed_all, grad_gate_all, 1, (grad_input,))
-    gate_other = [flip(v, "rows", 1) for v in low]
-    block_output = restore(scalars, block_all, SMALL, (grad_gate_w,))
-    grad_up_w, low = weight_grad(core, normed_all, grad_up_all, 1, (block_output,))
-    up_other = [flip(v, "rows", 1) for v in low]
-    grad_input = restore(scalars, grad_input_all, spent(25), (grad_up_w,))
-    width_kv = key_matrix.shape[1]
-    gains_sent = spread(gain_rows(grad_wkv), "tensor")
-    grad_down = fill_other(core, down_other, grad_down, 0, (grad_input,))
-    grad_gate_w = fill_other(core, gate_other, grad_gate_w, 1, (grad_down,))
-    gains = add_up(gains_sent, F32, (grad_gate_w,))
-    grad_up_w = fill_other(core, up_other, grad_up_w, 1, (gains,))
+    grad_down, low = weight_grad(core, hidden_all, upstream_all, 0, 2, (keep,))
+    down_other = [flip(v[None], "rows", 1) for v in low]
+    block_chunk = add_up([middle, keep, flip(send, "tensor", mask)], F32, (grad_down,))
+    both = finish(
+        scalars, stream, inverse_one, gain_attn, grad_middle, block_chunk, sent
+    )
+    both_all = spread(both, "tensor")
+    grad_gate_w, grad_up_w, low = pair_grad(
+        core, normed_all, grad_gate_all, grad_up_all, (both,)
+    )
+    pair_other = flip(low, "rows", 1)
+    grad_down = fill_other(core, down_other, 0, grad_down, 0, (grad_up_w,))
+    grad_wo, grad_wq, grad_wk, grad_wv = widen(
+        grad_wo, grad_wq, grad_wkv, key_matrix.shape[1], (grad_down,)
+    )
+    grad_input, block_output = restore(scalars, both_all, (grad_wo,))
+    grad_gate_w = fill_other(core, [pair_other], 0, grad_gate_w, 1, (grad_input,))
+    gains = gain_rows(grad_wkv, (grad_gate_w,))
+    grad_up_w = fill_other(core, [pair_other], 1, grad_up_w, 1, (gains,))
+    gains = add_up(spread(gains, "tensor"), F32, (grad_up_w,))
     return (
         block_output[None],
         grad_input[None],
-        grad_wq.astype(F32),
-        grad_wkv[:, :width_kv].astype(F32),
-        grad_wkv[:, width_kv : 2 * width_kv].astype(F32),
-        grad_wo.astype(F32),
+        grad_wq,
+        grad_wk,
+        grad_wv,
+        grad_wo,
         grad_gate_w,
         grad_up_w,
         grad_down,

time: 424 us -> 411 us (0.969)
  other arithmetic: 13.7 us -> 5.26 us
  starting transfers between devices: 57.1 us -> 63.7 us
  waiting for transfers between devices: 72.3 us -> 65.7 us
    ppermute x45 -> x32, waiting for transfers between devices: 43.8 us -> 64.4 us  [flip(): lax.ppermute(value, axis, [(i, i ^ mask) for i in range(lax.axis_size(axi...]
    psum x1, waiting for transfers between devices: 19.5 us -> 0.01 us  [per_device(): lax.psum((wo_part, wq_part, wkv_part), ('rows', 'seq'))]
    convert_element_type x3 -> x0, other arithmetic: 7.8 us -> none  [the longest x1 2.65 us: per_device(): grad_wkv[:, width_kv:2 * width_kv].astype(F32)]
    all_gather x2, waiting for transfers between devices: 7.76 us -> 0.01 us  [gather_halves(): lax.all_gather(first, ('rows', 'seq'), axis=0, tiled=True)]
    ppermute x45 -> x32, starting transfers between devices: 56.7 us -> 63.5 us  [flip(): lax.ppermute(value, axis, [(i, i ^ mask) for i in range(lax.axis_size(axi...]
    pallas_call x11 -> x12, Pallas kernels: 95.9 us -> 95.2 us  [the longest x1 29.4 us: pair_grad(): pl.pallas_call(functools.partial(pair_grad_kernel, count), out_shape=(wid...]
  transfers between devices with their start and end apart: 50 -> 37, of which waited for: 10 -> 11; matrix products, arithmetic and copies ran while one was open for 2% -> 1% of each run, Pallas kernels for 53% -> 57%
where the time goes in v3:
time: 411 us; the launch traced here: 407 us
  Pallas kernels  245 us (60%)
  waiting for transfers between devices  65.7 us (16%)
  starting transfers between devices  63.7 us (15%)
  between operations  16.8 us (4%)
  local copies, waits for them, and re-layouts  9.95 us (2%)
  other arithmetic  5.26 us (1%)
    ppermute x32, waiting for transfers between devices, flip(): lax.ppermute(value, axis, [(i, i ^ mask) for i in range(lax.axis_size(axi...  64.4 us
    ppermute x32, starting transfers between devices, flip(): lax.ppermute(value, axis, [(i, i ^ mask) for i in range(lax.axis_size(axi...  63.5 us
    pallas_call x2, Pallas kernels, feed_half(): pl.pallas_call(feed_half_kernel, out_shape=(out, out, out), grid_spec=plt...  36 us
    pallas_call x1, Pallas kernels, pair_grad(): pl.pallas_call(functools.partial(pair_grad_kernel, count), out_shape=(wid...  29.4 us
    pallas_call x3, Pallas kernels, grad_hidden_of(): pl.pallas_call(times_transposed_kernel, out_shape=jax.ShapeDtypeStruct((t...  27 us
    pallas_call x1, Pallas kernels, weight_grad(): pl.pallas_call(functools.partial(weight_grad_kernel, count, pieces), out_...  20.5 us
    pallas_call x3, Pallas kernels, fill_other(): pl.pallas_call(functools.partial(fill_other_kernel, pieces), out_shape=ja...  18.3 us
    pallas_call x1, Pallas kernels, feed_own(): pl.pallas_call(functools.partial(feed_own_kernel, len(normed), chunks), o...  18 us
  transfers between devices with their start and end apart: 37, of which 11 were waited for; matrix products, arithmetic and copies ran while one was open for 1% of the time, Pallas kernels for 57%

profile of v3, /device:TPU:0, one launch (start us, length us, event | category | flops | bytes accessed | tf_op | source)
XLA Modules:
  0.0 406.8 jit_solution(12884677291256545950)
XLA Ops:
  12.6 3.8 mask_padding.1
  21.1 4.2 %project_kv.1 = (bf16[320,2048]{1,0:T(8,128)(2,1)}, f32[320,128]{1,0:T(8,128)}, bf16[320,256]{1,0:T(8,128)(2,1)}) custom-call(s32[2]{0:T(128)} %pad_add_fusion.scalars.me, bf16[320,2048]{1,0:T(8,128)(2,1)} %bitcast.29, bf16[320,2048]{1,0:T(8,128)(2,1)} %bitcast.30, bf16[320,2048]{1,0:T(8,128)(2,1)} %bitcast.31, bf16[320,2048]{1,0:T(8,128)(2,1)} %bitcast.32, ...), custom_call_target="tpu_custom_call" | custom-call | flops 4000000000 | bytes 1 | tf_op jit(solution)/shard_map/project_kv/pallas_call | solution.py:547
  25.3 2.9 collective-permute-start
  29.8 3.9 project_query.1.query
  33.7 3.0 collective-permute-done.refs_1_
  36.7 3.3 collective-permute-done.1.refs_2_
  39.9 4.5 %collective-permute-done.2.refs_3_ = bf16[320,256]{1,0:T(8,128)(2,1)S(1)} collective-permute-done((bf16[320,256]{1,0:T(8,128)(2,1)}, bf16[320,256]{1,0:T(8,128)(2,1)S(1)}, u32[]{:S(2)}, u32[]{:S(2)}) %collective-permute-start.2) | collective-permute-done | bytes 163872 | tf_op jit(solution)/shard_map/ppermute | solution.py:1043
  45.1 10.7 %attend.1 = (bf16[320,512]{1,0:T(8,128)(2,1)}, f32[2,1280]{1,0:T(2,128)}, bf16[80,2048]{1,0:T(8,128)(2,1)}, bf16[80,2048]{1,0:T(8,128)(2,1)}, bf16[80,2048]{1,0:T(8,128)(2,1)}, /*index=5*/bf16[80,2048]{1,0:T(8,128)(2,1)}) custom-call(s32[4]{0:T(128)} %pad_add_fusion.1.refs_9_.shift, bf16[320,512]{1,0:T(8,128)(2,1)} %project_query.1.query, ...), custom_call_target="tpu_custom_call" | custom-call | flops 11000000512 | bytes 1 | tf_op jit(solution)/shard_map/attend/pallas_call | solution.py:663
  55.8 3.4 collective-permute-start.3
  60.2 7.2 %grad_hidden_of.3.refs_4_.grad_hidden = bf16[320,2048]{1,0:T(8,128)(2,1)} custom-call(s32[1]{0:T(128)} %bitcast.13.core, bf16[320,2048]{1,0:T(8,128)(2,1)} %get-tuple-element.69.refs_13_.left.upstream, bf16[2048,2048]{1,0:T(8,128)(2,1)} %weight.9, bf16[80,2048]{1,0:T(8,128)(2,1)} %get-tuple-element.73.refs_0_), custom_call_target="tpu_custom_call" | custom-call | flops 10000000000 | bytes 1 | tf_op jit(solution)/shard_map/grad_hidden_of/pallas_call | solution.py:71
  68.5 19.0 %collective-permute-done.4.refs_2_ = bf16[80,2048]{1,0:T(8,128)(2,1)S(1)} collective-permute-done((bf16[80,2048]{1,0:T(8,128)(2,1)}, bf16[80,2048]{1,0:T(8,128)(2,1)S(1)}, u32[]{:S(2)}, u32[]{:S(2)}) %collective-permute-start.4) | collective-permute-done | bytes 327712 | tf_op jit(solution)/shard_map/ppermute | solution.py:1043
  88.4 3.3 middle_norm.1
  91.6 2.9 collective-permute-start.7
  96.0 9.9 %grad_hidden_of.4.refs_4_.grad_hidden = bf16[1280,1024]{1,0:T(8,128)(2,1)} custom-call(s32[1]{0:T(128)} %bitcast.13.core, bf16[1280,2048]{1,0:T(8,128)(2,1)} %all-gather.5.cloned.1.call-done.left.refs_2_, bf16[2048,2048]{1,0:T(8,128)(2,1)} %weight.9, f32[80,2048]{1,0:T(8,128)} %get-tuple-element.77.refs_0_.middle), custom_call_target="tpu_custom_call" | custom-call | flops 10000000000 | bytes 1 | tf_op jit(solution)/shard_map/grad_hidden_of/pallas_call | solution.py:71
  107.2 10.3 %collective-permute-done.7.refs_2_ = bf16[80,2048]{1,0:T(8,128)(2,1)S(1)} collective-permute-done((bf16[80,2048]{1,0:T(8,128)(2,1)}, bf16[80,2048]{1,0:T(8,128)(2,1)S(1)}, u32[]{:S(2)}, u32[]{:S(2)}) %collective-permute-start.7) | collective-permute-done | bytes 327712 | tf_op jit(solution)/shard_map/ppermute | solution.py:1043
  118.9 2.4 join_halves.1
  121.9 18.0 %feed_own.1 = (bf16[320,2048]{1,0:T(8,128)(2,1)}, bf16[80,2048]{1,0:T(8,128)(2,1)}, bf16[80,2048]{1,0:T(8,128)(2,1)}, bf16[80,2048]{1,0:T(8,128)(2,1)}, bf16[80,2048]{1,0:T(8,128)(2,1)}) custom-call(bf16[2048,2048]{1,0:T(8,128)(2,1)} %gate_w.5, bf16[2048,2048]{1,0:T(8,128)(2,1)} %up_w.5, bf16[320,2048]{1,0:T(8,128)(2,1)} %grad_hidden_of.3.refs_4_.grad_hidden, ...), custom_call_target="tpu_custom_call" | custom-call | flops 17999998976 | bytes 1 | tf_op jit(solution)/shard_map/feed_own/pallas_call | solution.py:180
  139.9 5.7 %collective-permute-start.10 = (bf16[80,2048]{1,0:T(8,128)(2,1)}, bf16[80,2048]{1,0:T(8,128)(2,1)S(1)}, u32[]{:S(2)}, u32[]{:S(2)}) collective-permute-start(bf16[80,2048]{1,0:T(8,128)(2,1)} %get-tuple-element.85), channel_id=1, source_target_pairs={{0,2},{1,3},{2,0},{3,1},{4,6},{5,7},{6,4},{7,5},{8,10},{9,11},{10,... | collective-permute-start | bytes 983048 | tf_op jit(solution)/shard_map/ppermute | solution.py:1043
  145.6 2.0 collective-permute-start.9
  147.6 9.9 %grad_hidden_of.5.refs_4_.grad_hidden = bf16[1280,1024]{1,0:T(8,128)(2,1)} custom-call(s32[1]{0:T(128)} %bitcast.13.core, bf16[1280,2048]{1,0:T(8,128)(2,1)} %all-gather.7.cloned.1.call-done.left.refs_3_, bf16[2048,2048]{1,0:T(8,128)(2,1)} %weight.9, bf16[80,2048]{1,0:T(8,128)(2,1)} %get-tuple-element.83.refs_0_), custom_call_target="tpu_custom_call" | custom-call | flops 10000000000 | bytes 1 | tf_op jit(solution)/shard_map/grad_hidden_of/pallas_call | solution.py:71
  157.5 10.6 %collective-permute-done.10.refs_2_ = bf16[80,2048]{1,0:T(8,128)(2,1)S(1)} collective-permute-done((bf16[80,2048]{1,0:T(8,128)(2,1)}, bf16[80,2048]{1,0:T(8,128)(2,1)S(1)}, u32[]{:S(2)}, u32[]{:S(2)}) %collective-permute-start.10) | collective-permute-done | bytes 327712 | tf_op jit(solution)/shard_map/ppermute | solution.py:1043
  169.0 3.0 norm_back.1
  172.0 5.3 %collective-permute-start.13 = (bf16[80,2048]{1,0:T(8,128)(2,1)}, bf16[80,2048]{1,0:T(8,128)(2,1)S(1)}, u32[]{:S(2)}, u32[]{:S(2)}) collective-permute-start(bf16[80,2048]{1,0:T(8,128)(2,1)} %get-tuple-element.95.refs_4_.refs_0_), channel_id=1, source_target_pairs={{0,1},{1,0},{2,3},{3,2},{4,5},{5,4},{6,7},{7,6},{8,9},{9,8},{10,11... | collective-permute-start | bytes 983048 | tf_op jit(solution)/shard_map/ppermute | solution.py:1043
  179.8 17.7 %feed_half.2 = (bf16[1280,1024]{1,0:T(8,128)(2,1)}, bf16[1280,1024]{1,0:T(8,128)(2,1)}, bf16[1280,1024]{1,0:T(8,128)(2,1)}) custom-call(s32[1]{0:T(128)} %bitcast.13.core, bf16[1280,2048]{1,0:T(8,128)(2,1)} %all-gather.9.cloned.1.call-done.normed.refs_0_, bf16[2048,2048]{1,0:T(8,128)(2,1)} %gate_w.5, bf16[2048,2048]{1,0:T(8,128)(2,1)} %up_w.5, ...), custom_call_target="tpu_custom_call" | custom-call | flops 17999998976 | bytes 1 | tf_op jit(solution)/shard_map/feed_half/pallas_call | solution.py:117
  197.5 7.5 %down_projection.1 = (bf16[160,2048]{1,0:T(8,128)(2,1)}, bf16[160,2048]{1,0:T(8,128)(2,1)}) custom-call(bf16[320,2048]{1,0:T(8,128)(2,1)} %get-tuple-element.89.hidden, bf16[2048,2048]{1,0:T(8,128)(2,1)} %weight.9, bf16[1280,1024]{1,0:T(8,128)(2,1)} %get-tuple-element.90.refs_0_), custom_call_target="tpu_custom_call" | custom-call | flops 7000000000 | bytes 1 | tf_op jit(solution)/shard_map/down_projection/pallas_call | solution.py:209
  205.9 15.4 %attend_back.1 = (bf16[320,512]{1,0:T(8,128)(2,1)}, bf16[320,256]{1,0:T(8,128)(2,1)}, bf16[320,256]{1,0:T(8,128)(2,1)}, bf16[320,256]{1,0:T(8,128)(2,1)}, bf16[320,256]{1,0:T(8,128)(2,1)}) custom-call(s32[4]{0:T(128)} %pad_add_fusion.1.refs_9_.shift, bf16[320,512]{1,0:T(8,128)(2,1)} %project_query.1.query, bf16[320,512]{1,0:T(8,128)(2,1)} %get-tuple-element.93.attended.left, ...), custom_call_target="tpu_custom_call" | custom-call | flops 16000000000 | bytes 1 | tf_op jit(solution)/shard_map/attend_back/pallas_call | solution.py:963
  222.4 2.3 collective-permute-start.18
  224.7 4.9 %left_product.2.refs_1_ = bf16[512,2048]{1,0:T(8,128)(2,1)} custom-call(bf16[320,512]{1,0:T(8,128)(2,1)} %get-tuple-element.93.attended.left, bf16[80,2048]{1,0:T(8,128)(2,1)} %get-tuple-element.95.refs_4_.refs_0_, bf16[80,2048]{1,0:T(8,128)(2,1)} %copy-done.9, bf16[80,2048]{1,0:T(8,128)(2,1)} %copy-done.10, bf16[80,2048]{1,0:T(8,128)(2,1)} %copy-done.11, ...), custom_call_target="tpu_custom_call" | custom-call | flops 4000000000 | bytes 1 | tf_op jit(solution)/shard_map/left_product/pallas_call | solution.py:350
  229.6 3.9 left_product.3.refs_8_
  233.5 4.0 collective-permute-start.12
  238.2 6.0 %input_back.1 = (bf16[320,256]{1,0:T(8,128)(2,1)}, f32[1,2048]{1,0:T(1,128)}, bf16[80,2048]{1,0:T(8,128)(2,1)}, bf16[80,2048]{1,0:T(8,128)(2,1)}, bf16[80,2048]{1,0:T(8,128)(2,1)}, /*index=5*/bf16[80,2048]{1,0:T(8,128)(2,1)}) custom-call(s32[2]{0:T(128)} %pad_add_fusion.scalars.me, bf16[320,512]{1,0:T(8,128)(2,1)} %get-tuple-element.96.refs_4_.refs_0_.grad_query, ...), custom_call_target="tpu_custom_call" | custom-call | flops 6000000000 | bytes 1 | tf_op jit(solution)/shard_map/input_back/pallas_call | solution.py:1009
  244.2 3.1 kv_product.1.value
  249.3 3.8 collective-permute-start.22
  253.1 18.3 %feed_half.3 = (bf16[1280,1024]{1,0:T(8,128)(2,1)}, bf16[1280,1024]{1,0:T(8,128)(2,1)}, bf16[1280,1024]{1,0:T(8,128)(2,1)}) custom-call(s32[1]{0:T(128)} %bitcast.13.core, bf16[1280,2048]{1,0:T(8,128)(2,1)} %all-gather.11.cloned.1.call-done.refs_9_.normed.refs_1_, bf16[2048,2048]{1,0:T(8,128)(2,1)} %gate_w.5, bf16[2048,2048]{1,0:T(8,128)(2,1)} %up_w.5, ...), custom_call_target="tpu_custom_call" | custom-call | flops 17999998976 | bytes 1 | tf_op jit(solution)/shard_map/feed_half/pallas_call | solution.py:117
  271.5 6.8 %collective-permute-done.12.came = bf16[160,2048]{1,0:T(8,128)(2,1)} collective-permute-done((bf16[160,2048]{1,0:T(8,128)(2,1)S(1)}, bf16[160,2048]{1,0:T(8,128)(2,1)}, u32[]{:S(2)}, u32[]{:S(2)}) %collective-permute-start.12) | collective-permute-done | bytes 655392 | tf_op jit(solution)/shard_map/ppermute | solution.py:1043
  278.2 2.3 add_half.1
  280.8 20.5 %weight_grad.1 = (f32[2048,2048]{1,0:T(8,128)}, bf16[512,2048]{1,0:T(8,128)(2,1)}, bf16[512,2048]{1,0:T(8,128)(2,1)}) custom-call(s32[1]{0:T(128)} %bitcast.13.core, bf16[1280,1024]{1,0:T(8,128)(2,1)} %get-tuple-element.90.refs_0_, bf16[1280,1024]{1,0:T(8,128)(2,1)} %get-tuple-element.105.refs_0_.refs_1_, ...), custom_call_target="tpu_custom_call" | custom-call | flops 19000000512 | bytes 1 | tf_op jit(solution)/shard_map/weight_grad/pallas_call | solution.py:282
  302.1 2.2 add_up.2.block
  304.4 3.8 finish.1.refs_6_.refs_0_
  310.0 2.1 collective-permute-start.24
  313.2 29.4 %pair_grad.1 = (f32[2048,2048]{1,0:T(8,128)}, f32[2048,2048]{1,0:T(8,128)}, bf16[2,2048,1024]{2,1,0:T(8,128)(2,1)}) custom-call(s32[1]{0:T(128)} %bitcast.13.core, bf16[1280,2048]{1,0:T(8,128)(2,1)} %all-gather.9.cloned.1.call-done.normed.refs_0_, bf16[1280,2048]{1,0:T(8,128)(2,1)} %all-gather.11.cloned.1.call-done.refs_9_.normed.refs_1_, ...), custom_call_target="tpu_custom_call" | custom-call | flops 33999998976 | bytes 1 | tf_op jit(solution)/shard_map/pair_grad/pallas_call | solution.py:323
  342.7 6.4 %fill_other.3.refs_0_ = f32[2048,2048]{1,0:T(8,128)} custom-call(s32[1]{0:T(128)} %bitcast.13.core, bf16[1,512,2048]{2,1,0:T(8,128)(2,1)} %collective-permute-done.26.refs_0_, bf16[1,512,2048]{2,1,0:T(8,128)(2,1)} %collective-permute-done.27.refs_1_, f32[2048,2048]{1,0:T(8,128)} %get-tuple-element.108.refs_3_.refs_2_, ...), custom_call_target="tpu_custom_call", output_to_operand_aliasing={{}: (3, {})} | custom-call | flops 6000000000 | bytes 1 | tf_op jit(solution)/shard_map/fill_other/pallas_call | solution.py:480
  349.1 6.9 %widen.1 = (f32[512,2048]{1,0:T(8,128)}, f32[2048,512]{1,0:T(8,128)}, f32[2048,128]{1,0:T(8,128)}, f32[2048,128]{1,0:T(8,128)}) custom-call(bf16[512,2048]{1,0:T(8,128)(2,1)} %get-tuple-element.127.wo, bf16[2048,512]{1,0:T(8,128)(2,1)} %get-tuple-element.128.wq, bf16[272,2048]{1,0:T(8,128)(2,1)} %get-tuple-element.129.wkv.value, f32[2048,2048]{1,0:T(8,128)} %fill_other.3.refs_0_), custom_call_target="tpu_custom_call" | custom-call | flops 8000000000 | bytes 1 | tf_op jit(solution)/shard_map/widen/pallas_call | solution.py:878
  356.9 4.4 %restore.1 = (bf16[320,2048]{1,0:T(8,128)(2,1)}, bf16[320,2048]{1,0:T(8,128)(2,1)}) custom-call(s32[2]{0:T(128)} %pad_add_fusion.scalars.me, bf16[160,2048]{1,0:T(8,128)(2,1)} %finish.1.refs_6_.refs_0_, bf16[160,2048]{1,0:T(8,128)(2,1)} %copy-done.7, bf16[160,2048]{1,0:T(8,128)(2,1)} %collective-permute-done.24.refs_2_, ...), custom_call_target="tpu_custom_call" | custom-call | flops 86999998464 | bytes 1 | tf_op jit(solution)/shard_map/restore/pallas_call | solution.py:847
  361.3 6.0 %fill_other.4.refs_0_ = f32[2048,2048]{1,0:T(8,128)} custom-call(s32[1]{0:T(128)} %bitcast.13.core, bf16[2,2048,1024]{2,1,0:T(8,128)(2,1)} %collective-permute-done.28.refs_0_, f32[2048,2048]{1,0:T(8,128)} %get-tuple-element.126.refs_1_, bf16[320,2048]{1,0:T(8,128)(2,1)} %get-tuple-element.121.refs_2_), custom_call_target="tpu_custom_call", output_to_operand_aliasing={{}: (2, {})} | custom-call | flops 6000000000 | bytes 1 | tf_op jit(solution)/shard_map/fill_other/pallas_call | solution.py:480
  368.7 13.9 %collective-permute-start.29 = (f32[16,2048]{1,0:T(8,128)}, f32[16,2048]{1,0:T(8,128)S(1)}, u32[]{:S(2)}, u32[]{:S(2)}) collective-permute-start(f32[16,2048]{1,0:T(8,128)} %gain_rows.1.refs_2_.refs_0_), channel_id=1, source_target_pairs={{0,1},{1,0},{2,3},{3,2},{4,5},{5,4},{6,7},{7,6},{8,9},{9,8},{10,11... | collective-permute-start | bytes 393224 | tf_op jit(solution)/shard_map/ppermute | solution.py:1043
  385.9 6.0 %fill_other.5.refs_4_ = f32[2048,2048]{1,0:T(8,128)} custom-call(s32[1]{0:T(128)} %bitcast.13.core, bf16[2,2048,1024]{2,1,0:T(8,128)(2,1)} %collective-permute-done.28.refs_0_, f32[2048,2048]{1,0:T(8,128)} %get-tuple-element.118.refs_3_.refs_1_, f32[16,2048]{1,0:T(8,128)} %gain_rows.1.refs_2_.refs_0_), custom_call_target="tpu_custom_call", output_to_operand_aliasing={{}: (2, {})} | custom-call | flops 6000000000 | bytes 1 | tf_op jit(solution)/shard_map/fill_other/pallas_call | solution.py:480
  391.8 3.7 collective-permute-done.30.refs_2_
  (123 shorter events, 39.8 us)
Async XLA Ops:
  7.2 88.9 %all-gather.5.cloned.1.call-start = ((), (), s32[]{:S(2)}) async-start(), calls=%async_computation | async-start | bytes 5898240 | tf_op jit(solution)/shard_map/all_gather | solution.py:1065
  12.6 7.2 %copy-start.4 = (f32[128]{0:T(128)S(1)}, f32[128]{0:T(128)}, u32[]{:S(2)}) copy-start(f32[128]{0:T(128)} %constant.53) | copy-start | bytes 1540
  12.6 7.2 %copy-start.5 = (f32[128]{0:T(128)S(1)}, f32[128]{0:T(128)}, u32[]{:S(2)}) copy-start(f32[128]{0:T(128)} %constant.54) | copy-start | bytes 1540
  16.4 131.2 %all-gather.7.cloned.1.call-start = ((), (), s32[]{:S(2)}) async-start(), calls=%async_computation.1 | async-start | bytes 5898240 | tf_op jit(solution)/shard_map/all_gather | solution.py:1066
  17.1 162.7 %all-gather.9.cloned.1.call-start = ((), (), s32[]{:S(2)}) async-start(), calls=%async_computation.2 | async-start | bytes 5898240 | tf_op jit(solution)/shard_map/all_gather | solution.py:1065
  25.3 11.3 %collective-permute-start = (bf16[320,256]{1,0:T(8,128)(2,1)}, bf16[320,256]{1,0:T(8,128)(2,1)S(1)}, u32[]{:S(2)}, u32[]{:S(2)}) collective-permute-start(bf16[320,256]{1,0:T(8,128)(2,1)} %get-tuple-element.72.refs_0_), channel_id=1, source_target_pairs={{0,4},{4,0},{8,12},{12,8},{1,5},{5,1},{9,13},{13,9},{2,6},{6,2},{1... | collective-permute-start | bytes 491528 | tf_op jit(solution)/shard_map/ppermute | solution.py:1043
  28.3 11.6 %collective-permute-start.1 = (bf16[320,256]{1,0:T(8,128)(2,1)}, bf16[320,256]{1,0:T(8,128)(2,1)S(1)}, u32[]{:S(2)}, u32[]{:S(2)}) collective-permute-start(bf16[320,256]{1,0:T(8,128)(2,1)} %get-tuple-element.72.refs_0_), channel_id=1, source_target_pairs={{0,8},{4,12},{8,0},{12,4},{1,9},{5,13},{9,1},{13,5},{2,10},{6,14},... | collective-permute-start | bytes 491528 | tf_op jit(solution)/shard_map/ppermute | solution.py:1043
  29.8 14.6 %collective-permute-start.2 = (bf16[320,256]{1,0:T(8,128)(2,1)}, bf16[320,256]{1,0:T(8,128)(2,1)S(1)}, u32[]{:S(2)}, u32[]{:S(2)}) collective-permute-start(bf16[320,256]{1,0:T(8,128)(2,1)} %get-tuple-element.72.refs_0_), channel_id=1, source_target_pairs={{0,12},{4,8},{8,4},{12,0},{1,13},{5,9},{9,5},{13,1},{2,14},{6,10},... | collective-permute-start | bytes 491528 | tf_op jit(solution)/shard_map/ppermute | solution.py:1043
  36.7 7.8 %copy-start.21 = (bf16[320,256]{1,0:T(8,128)(2,1)}, bf16[320,256]{1,0:T(8,128)(2,1)S(1)}, u32[]{:S(2)}) copy-start(bf16[320,256]{1,0:T(8,128)(2,1)S(1)} %collective-permute-done.refs_1_) | copy-start | bytes 491524
  39.9 4.5 %copy-start.22 = (bf16[320,256]{1,0:T(8,128)(2,1)}, bf16[320,256]{1,0:T(8,128)(2,1)S(1)}, u32[]{:S(2)}) copy-start(bf16[320,256]{1,0:T(8,128)(2,1)S(1)} %collective-permute-done.1.refs_2_) | copy-start | bytes 491524
  55.8 12.7 %collective-permute-start.3 = (bf16[80,2048]{1,0:T(8,128)(2,1)}, bf16[80,2048]{1,0:T(8,128)(2,1)S(1)}, u32[]{:S(2)}, u32[]{:S(2)}) collective-permute-start(bf16[80,2048]{1,0:T(8,128)(2,1)} %get-tuple-element.74), channel_id=1, source_target_pairs={{0,3},{1,2},{2,1},{3,0},{4,7},{5,6},{6,5},{7,4},{8,11},{9,10},{10,... | collective-permute-start | bytes 983048 | tf_op jit(solution)/shard_map/ppermute | solution.py:1043
  59.2 28.3 %collective-permute-start.4 = (bf16[80,2048]{1,0:T(8,128)(2,1)}, bf16[80,2048]{1,0:T(8,128)(2,1)S(1)}, u32[]{:S(2)}, u32[]{:S(2)}) collective-permute-start(bf16[80,2048]{1,0:T(8,128)(2,1)} %get-tuple-element.75), channel_id=1, source_target_pairs={{0,2},{1,3},{2,0},{3,1},{4,6},{5,7},{6,4},{7,5},{8,10},{9,11},{10,... | collective-permute-start | bytes 983048 | tf_op jit(solution)/shard_map/ppermute | solution.py:1043
  59.2 28.3 %collective-permute-start.5 = (bf16[80,2048]{1,0:T(8,128)(2,1)}, bf16[80,2048]{1,0:T(8,128)(2,1)S(1)}, u32[]{:S(2)}, u32[]{:S(2)}) collective-permute-start(bf16[80,2048]{1,0:T(8,128)(2,1)} %get-tuple-element.76), channel_id=1, source_target_pairs={{0,1},{1,0},{2,3},{3,2},{4,5},{5,4},{6,7},{7,6},{8,9},{9,8},{10,11... | collective-permute-start | bytes 983048 | tf_op jit(solution)/shard_map/ppermute | solution.py:1043
  68.5 19.0 %copy-start.15 = (bf16[80,2048]{1,0:T(8,128)(2,1)}, bf16[80,2048]{1,0:T(8,128)(2,1)S(1)}, u32[]{:S(2)}) copy-start(bf16[80,2048]{1,0:T(8,128)(2,1)S(1)} %collective-permute-done.3.refs_1_) | copy-start | bytes 983044
  91.6 15.5 %collective-permute-start.6 = (bf16[80,2048]{1,0:T(8,128)(2,1)}, bf16[80,2048]{1,0:T(8,128)(2,1)S(1)}, u32[]{:S(2)}, u32[]{:S(2)}) collective-permute-start(bf16[80,2048]{1,0:T(8,128)(2,1)} %get-tuple-element.79.refs_0_), channel_id=1, source_target_pairs={{0,1},{1,0},{2,3},{3,2},{4,5},{5,4},{6,7},{7,6},{8,9},{9,8},{10,11... | collective-permute-start | bytes 983048 | tf_op jit(solution)/shard_map/ppermute | solution.py:1043
  91.6 25.8 %collective-permute-start.7 = (bf16[80,2048]{1,0:T(8,128)(2,1)}, bf16[80,2048]{1,0:T(8,128)(2,1)S(1)}, u32[]{:S(2)}, u32[]{:S(2)}) collective-permute-start(bf16[80,2048]{1,0:T(8,128)(2,1)} %get-tuple-element.79.refs_0_), channel_id=1, source_target_pairs={{0,2},{1,3},{2,0},{3,1},{4,6},{5,7},{6,4},{7,5},{8,10},{9,11},{10,... | collective-permute-start | bytes 983048 | tf_op jit(solution)/shard_map/ppermute | solution.py:1043
  94.6 22.9 %collective-permute-start.8 = (bf16[80,2048]{1,0:T(8,128)(2,1)}, bf16[80,2048]{1,0:T(8,128)(2,1)S(1)}, u32[]{:S(2)}, u32[]{:S(2)}) collective-permute-start(bf16[80,2048]{1,0:T(8,128)(2,1)} %get-tuple-element.79.refs_0_), channel_id=1, source_target_pairs={{0,3},{1,2},{2,1},{3,0},{4,7},{5,6},{6,5},{7,4},{8,11},{9,10},{10,... | collective-permute-start | bytes 983048 | tf_op jit(solution)/shard_map/ppermute | solution.py:1043
  107.2 10.3 %copy-start.16 = (bf16[80,2048]{1,0:T(8,128)(2,1)}, bf16[80,2048]{1,0:T(8,128)(2,1)S(1)}, u32[]{:S(2)}) copy-start(bf16[80,2048]{1,0:T(8,128)(2,1)S(1)} %collective-permute-done.6.refs_1_) | copy-start | bytes 983044
  121.3 116.2 %all-gather.11.cloned.1.call-start = ((), (), s32[]{:S(2)}) async-start(), calls=%async_computation.3 | async-start | bytes 5898240 | tf_op jit(solution)/shard_map/all_gather | solution.py:1066
  139.9 28.2 %collective-permute-start.10 = (bf16[80,2048]{1,0:T(8,128)(2,1)}, bf16[80,2048]{1,0:T(8,128)(2,1)S(1)}, u32[]{:S(2)}, u32[]{:S(2)}) collective-permute-start(bf16[80,2048]{1,0:T(8,128)(2,1)} %get-tuple-element.85), channel_id=1, source_target_pairs={{0,2},{1,3},{2,0},{3,1},{4,6},{5,7},{6,4},{7,5},{8,10},{9,11},{10,... | collective-permute-start | bytes 983048 | tf_op jit(solution)/shard_map/ppermute | solution.py:1043
  145.6 22.5 %collective-permute-start.11 = (bf16[80,2048]{1,0:T(8,128)(2,1)}, bf16[80,2048]{1,0:T(8,128)(2,1)S(1)}, u32[]{:S(2)}, u32[]{:S(2)}) collective-permute-start(bf16[80,2048]{1,0:T(8,128)(2,1)} %get-tuple-element.86), channel_id=1, source_target_pairs={{0,1},{1,0},{2,3},{3,2},{4,5},{5,4},{6,7},{7,6},{8,9},{9,8},{10,11... | collective-permute-start | bytes 983048 | tf_op jit(solution)/shard_map/ppermute | solution.py:1043
  145.6 22.5 %collective-permute-start.9 = (bf16[80,2048]{1,0:T(8,128)(2,1)}, bf16[80,2048]{1,0:T(8,128)(2,1)S(1)}, u32[]{:S(2)}, u32[]{:S(2)}) collective-permute-start(bf16[80,2048]{1,0:T(8,128)(2,1)} %get-tuple-element.84), channel_id=1, source_target_pairs={{0,3},{1,2},{2,1},{3,0},{4,7},{5,6},{6,5},{7,4},{8,11},{9,10},{10,... | collective-permute-start | bytes 983048 | tf_op jit(solution)/shard_map/ppermute | solution.py:1043
  168.1 0.9 copy-start.14
  172.0 32.9 %collective-permute-start.13 = (bf16[80,2048]{1,0:T(8,128)(2,1)}, bf16[80,2048]{1,0:T(8,128)(2,1)S(1)}, u32[]{:S(2)}, u32[]{:S(2)}) collective-permute-start(bf16[80,2048]{1,0:T(8,128)(2,1)} %get-tuple-element.95.refs_4_.refs_0_), channel_id=1, source_target_pairs={{0,1},{1,0},{2,3},{3,2},{4,5},{5,4},{6,7},{7,6},{8,9},{9,8},{10,11... | collective-permute-start | bytes 983048 | tf_op jit(solution)/shard_map/ppermute | solution.py:1043
  177.3 27.6 %collective-permute-start.14 = (bf16[80,2048]{1,0:T(8,128)(2,1)}, bf16[80,2048]{1,0:T(8,128)(2,1)S(1)}, u32[]{:S(2)}, u32[]{:S(2)}) collective-permute-start(bf16[80,2048]{1,0:T(8,128)(2,1)} %get-tuple-element.95.refs_4_.refs_0_), channel_id=1, source_target_pairs={{0,2},{1,3},{2,0},{3,1},{4,6},{5,7},{6,4},{7,5},{8,10},{9,11},{10,... | collective-permute-start | bytes 983048 | tf_op jit(solution)/shard_map/ppermute | solution.py:1043
  178.3 26.6 %collective-permute-start.15 = (bf16[80,2048]{1,0:T(8,128)(2,1)}, bf16[80,2048]{1,0:T(8,128)(2,1)S(1)}, u32[]{:S(2)}, u32[]{:S(2)}) collective-permute-start(bf16[80,2048]{1,0:T(8,128)(2,1)} %get-tuple-element.95.refs_4_.refs_0_), channel_id=1, source_target_pairs={{0,3},{1,2},{2,1},{3,0},{4,7},{5,6},{6,5},{7,4},{8,11},{9,10},{10,... | collective-permute-start | bytes 983048 | tf_op jit(solution)/shard_map/ppermute | solution.py:1043
  205.0 0.9 copy-start.11
  221.2 16.3 %collective-permute-start.16 = (bf16[320,256]{1,0:T(8,128)(2,1)}, bf16[320,256]{1,0:T(8,128)(2,1)S(1)}, u32[]{:S(2)}, u32[]{:S(2)}) collective-permute-start(bf16[320,256]{1,0:T(8,128)(2,1)} %get-tuple-element.98), channel_id=1, source_target_pairs={{0,12},{4,8},{8,4},{12,0},{1,13},{5,9},{9,5},{13,1},{2,14},{6,10},... | collective-permute-start | bytes 491528 | tf_op jit(solution)/shard_map/ppermute | solution.py:1043
  221.3 16.2 %collective-permute-start.17 = (bf16[320,256]{1,0:T(8,128)(2,1)}, bf16[320,256]{1,0:T(8,128)(2,1)S(1)}, u32[]{:S(2)}, u32[]{:S(2)}) collective-permute-start(bf16[320,256]{1,0:T(8,128)(2,1)} %get-tuple-element.99), channel_id=1, source_target_pairs={{0,8},{4,12},{8,0},{12,4},{1,9},{5,13},{9,1},{13,5},{2,10},{6,14},... | collective-permute-start | bytes 491528 | tf_op jit(solution)/shard_map/ppermute | solution.py:1043
  222.4 15.1 %collective-permute-start.18 = (bf16[320,256]{1,0:T(8,128)(2,1)}, bf16[320,256]{1,0:T(8,128)(2,1)}, u32[]{:S(2)}, u32[]{:S(2)}) collective-permute-start(bf16[320,256]{1,0:T(8,128)(2,1)} %get-tuple-element.100), channel_id=1, source_target_pairs={{0,4},{4,0},{8,12},{12,8},{1,5},{5,1},{9,13},{13,9},{2,6},{6,2},{1... | collective-permute-start | bytes 491528 | tf_op jit(solution)/shard_map/ppermute | solution.py:1043
  229.6 3.9 copy-start.6
  233.5 44.7 %collective-permute-start.12 = (bf16[160,2048]{1,0:T(8,128)(2,1)S(1)}, bf16[160,2048]{1,0:T(8,128)(2,1)}, u32[]{:S(2)}, u32[]{:S(2)}) collective-permute-start(bf16[160,2048]{1,0:T(8,128)(2,1)S(1)} %copy-done.6), channel_id=1, source_target_pairs={{0,2},{1,3},{2,0},{3,1},{4,6},{5,7},{6,4},{7,5},{8,10},{9,11},{10,... | collective-permute-start | bytes 1966088 | tf_op jit(solution)/shard_map/ppermute | solution.py:1043
  247.4 1.9 copy-start.8
  248.7 100.4 %all-reduce.3.cloned.1.call-start = ((), (), s32[]{:S(2)}) async-start(), calls=%async_computation.4 | async-start | bytes 10616832 | tf_op jit(solution)/shard_map/psum | solution.py:1177
  248.7 55.7 %collective-permute-start.20 = (bf16[80,2048]{1,0:T(8,128)(2,1)}, bf16[80,2048]{1,0:T(8,128)(2,1)}, u32[]{:S(2)}, u32[]{:S(2)}) collective-permute-start(bf16[80,2048]{1,0:T(8,128)(2,1)} %get-tuple-element.109), channel_id=1, source_target_pairs={{0,3},{1,2},{2,1},{3,0},{4,7},{5,6},{6,5},{7,4},{8,11},{9,10},{10,... | collective-permute-start | bytes 983048 | tf_op jit(solution)/shard_map/ppermute | solution.py:1043
  249.3 55.1 %collective-permute-start.21 = (bf16[80,2048]{1,0:T(8,128)(2,1)}, bf16[80,2048]{1,0:T(8,128)(2,1)}, u32[]{:S(2)}, u32[]{:S(2)}) collective-permute-start(bf16[80,2048]{1,0:T(8,128)(2,1)} %get-tuple-element.110), channel_id=1, source_target_pairs={{0,2},{1,3},{2,0},{3,1},{4,6},{5,7},{6,4},{7,5},{8,10},{9,11},{10,... | collective-permute-start | bytes 983048 | tf_op jit(solution)/shard_map/ppermute | solution.py:1043
  249.3 55.1 %collective-permute-start.22 = (bf16[80,2048]{1,0:T(8,128)(2,1)S(1)}, bf16[80,2048]{1,0:T(8,128)(2,1)}, u32[]{:S(2)}, u32[]{:S(2)}) collective-permute-start(bf16[80,2048]{1,0:T(8,128)(2,1)S(1)} %copy-done.8), channel_id=1, source_target_pairs={{0,1},{1,0},{2,3},{3,2},{4,5},{5,4},{6,7},{7,6},{8,9},{9,8},{10,11... | collective-permute-start | bytes 983048 | tf_op jit(solution)/shard_map/ppermute | solution.py:1043
  280.5 20.9 %collective-permute-start.19 = (bf16[80,2048]{1,0:T(8,128)(2,1)}, bf16[80,2048]{1,0:T(8,128)(2,1)S(1)}, u32[]{:S(2)}, u32[]{:S(2)}) collective-permute-start(bf16[80,2048]{1,0:T(8,128)(2,1)} %get-tuple-element.107), channel_id=1, source_target_pairs={{0,1},{1,0},{2,3},{3,2},{4,5},{5,4},{6,7},{7,6},{8,9},{9,8},{10,11... | collective-permute-start | bytes 983048 | tf_op jit(solution)/shard_map/ppermute | solution.py:1043
  301.4 41.2 %collective-permute-start.26 = (bf16[1,512,2048]{2,1,0:T(8,128)(2,1)}, bf16[1,512,2048]{2,1,0:T(8,128)(2,1)}, u32[]{:S(2)}, u32[]{:S(2)}) collective-permute-start(bf16[1,512,2048]{2,1,0:T(8,128)(2,1)} %bitcast.24), channel_id=1, source_target_pairs={{0,16},{16,0},{1,17},{17,1},{2,18},{18,2},{3,19},{19,3},{4,20},{20... | collective-permute-start | bytes 6291464 | tf_op jit(solution)/shard_map/ppermute | solution.py:1043
  301.4 41.3 %collective-permute-start.27 = (bf16[1,512,2048]{2,1,0:T(8,128)(2,1)}, bf16[1,512,2048]{2,1,0:T(8,128)(2,1)}, u32[]{:S(2)}, u32[]{:S(2)}) collective-permute-start(bf16[1,512,2048]{2,1,0:T(8,128)(2,1)} %bitcast.23), channel_id=1, source_target_pairs={{0,16},{16,0},{1,17},{17,1},{2,18},{18,2},{3,19},{19,3},{4,20},{20... | collective-permute-start | bytes 6291464 | tf_op jit(solution)/shard_map/ppermute | solution.py:1043
  308.2 47.8 %collective-permute-start.23 = (bf16[160,2048]{1,0:T(8,128)(2,1)}, bf16[160,2048]{1,0:T(8,128)(2,1)S(1)}, u32[]{:S(2)}, u32[]{:S(2)}) collective-permute-start(bf16[160,2048]{1,0:T(8,128)(2,1)} %finish.1.refs_6_.refs_0_), channel_id=1, source_target_pairs={{0,1},{1,0},{2,3},{3,2},{4,5},{5,4},{6,7},{7,6},{8,9},{9,8},{10,11... | collective-permute-start | bytes 1966088 | tf_op jit(solution)/shard_map/ppermute | solution.py:1043
  310.0 46.9 %collective-permute-start.24 = (bf16[160,2048]{1,0:T(8,128)(2,1)}, bf16[160,2048]{1,0:T(8,128)(2,1)}, u32[]{:S(2)}, u32[]{:S(2)}) collective-permute-start(bf16[160,2048]{1,0:T(8,128)(2,1)} %finish.1.refs_6_.refs_0_), channel_id=1, source_target_pairs={{0,2},{1,3},{2,0},{3,1},{4,6},{5,7},{6,4},{7,5},{8,10},{9,11},{10,... | collective-permute-start | bytes 1966088 | tf_op jit(solution)/shard_map/ppermute | solution.py:1043
  312.0 44.9 %collective-permute-start.25 = (bf16[160,2048]{1,0:T(8,128)(2,1)}, bf16[160,2048]{1,0:T(8,128)(2,1)}, u32[]{:S(2)}, u32[]{:S(2)}) collective-permute-start(bf16[160,2048]{1,0:T(8,128)(2,1)} %finish.1.refs_6_.refs_0_), channel_id=1, source_target_pairs={{0,3},{1,2},{2,1},{3,0},{4,7},{5,6},{6,5},{7,4},{8,11},{9,10},{10,... | collective-permute-start | bytes 1966088 | tf_op jit(solution)/shard_map/ppermute | solution.py:1043
  342.6 18.6 %collective-permute-start.28 = (bf16[2,2048,1024]{2,1,0:T(8,128)(2,1)}, bf16[2,2048,1024]{2,1,0:T(8,128)(2,1)}, u32[]{:S(2)}, u32[]{:S(2)}) collective-permute-start(bf16[2,2048,1024]{2,1,0:T(8,128)(2,1)} %get-tuple-element.125), channel_id=1, source_target_pairs={{0,16},{16,0},{1,17},{17,1},{2,18},{18,2},{3,19},{19,3},{4,20},{20... | collective-permute-start | bytes 25165832 | tf_op jit(solution)/shard_map/ppermute | solution.py:1043
  368.7 23.1 %collective-permute-start.29 = (f32[16,2048]{1,0:T(8,128)}, f32[16,2048]{1,0:T(8,128)S(1)}, u32[]{:S(2)}, u32[]{:S(2)}) collective-permute-start(f32[16,2048]{1,0:T(8,128)} %gain_rows.1.refs_2_.refs_0_), channel_id=1, source_target_pairs={{0,1},{1,0},{2,3},{3,2},{4,5},{5,4},{6,7},{7,6},{8,9},{9,8},{10,11... | collective-permute-start | bytes 393224 | tf_op jit(solution)/shard_map/ppermute | solution.py:1043
  382.6 12.9 %collective-permute-start.30 = (f32[16,2048]{1,0:T(8,128)}, f32[16,2048]{1,0:T(8,128)S(1)}, u32[]{:S(2)}, u32[]{:S(2)}) collective-permute-start(f32[16,2048]{1,0:T(8,128)} %gain_rows.1.refs_2_.refs_0_), channel_id=1, source_target_pairs={{0,2},{1,3},{2,0},{3,1},{4,6},{5,7},{6,4},{7,5},{8,10},{9,11},{10,... | collective-permute-start | bytes 393224 | tf_op jit(solution)/shard_map/ppermute | solution.py:1043
  384.4 11.1 %collective-permute-start.31 = (f32[16,2048]{1,0:T(8,128)}, f32[16,2048]{1,0:T(8,128)S(1)}, u32[]{:S(2)}, u32[]{:S(2)}) collective-permute-start(f32[16,2048]{1,0:T(8,128)} %gain_rows.1.refs_2_.refs_0_), channel_id=1, source_target_pairs={{0,3},{1,2},{2,1},{3,0},{4,7},{5,6},{6,5},{7,4},{8,11},{9,10},{10,... | collective-permute-start | bytes 393224 | tf_op jit(solution)/shard_map/ppermute | solution.py:1043
  391.8 3.7 copy-start.1
  (15 other events, 11.1 us)
Sparse Core Ops, SparseCore 0:
  16.5 50.9 all-gather.4
  69.9 41.1 all-gather.6
  121.4 42.5 all-gather.8
  166.4 41.1 all-gather.10
  253.4 90.7 all-reduce.2
